TPU v7x, 128 devices: a whole 4x4x4 slice. The times are simulated.
128 devices in a mesh: gz: 16 (over x_lo, y, core), gy: 8 (over x_hi, z).
Axes of the slice: x: 4 (x_hi: 2, x_lo: 2; x = x_hi * 2 + x_lo), y: 4, z: 4, core: 2. Of those that a mesh axis runs over, the one named last changes fastest.
Arguments:
- air_now: float32 [128, 1024, 1024], P('gz', 'gy'), may hold values from -6 to 6
- air_prev: float32 [128, 1024, 1024], P('gz', 'gy'), may hold values from -6 to 6
- plate_now: float32 [2048, 4096], P(('gz', 'gy')), may hold values from -6 to 6
- plate_prev: float32 [2048, 4096], P(('gz', 'gy')), may hold values from -6 to 6
- plate_level: int32 [1], replicated, may hold values from 0 to 126
- plate_shift: int32 [1], replicated, may hold values from 0 to 512
Outputs:
- air_field: float32 [128, 1024, 1024], P('gz', 'gy')
- plate_field: float32 [2048, 4096], P(('gz', 'gy'))
Inputs may be any that keep to these rules, and one draw needn't show every extreme that they name: plate_level[0] and plate_level[0] + 1 are both air levels. The plate's footprint, rows plate_shift[0] to plate_shift[0] + 511, lies inside the air box.
All inputs are finite; a program needn't handle non-finite values.
Results may differ from a plain program's by a relative error of at most 0.0001.
Values sent between devices are 32-bit elements; how exact they have to be, the bound alone decides.
No kernel may reach another device: no remote copies, remote signals or barrier semaphores. Data moves between devices by JAX's collectives and lax.ppermute only.
A program may use at most 128 MiB of HBM per device.

v0:
```python
import jax
import jax.numpy as jnp
from jax import lax
from jax.sharding import PartitionSpec as P

STEPS = 2


def padded(cells, sides, width):
    for axis, dim in sides:
        count = lax.axis_size(axis)
        ends = count - 1
        head = lax.slice_in_dim(cells, 0, width, axis=dim)
        tail = lax.slice_in_dim(cells, cells.shape[dim] - width, cells.shape[dim], axis=dim)
        cells = jnp.concatenate(
            [
                lax.ppermute(tail, axis, [(i, (i + 1) % count) for i in range(ends)]),
                cells,
                lax.ppermute(head, axis, [((i + 1) % count, i) for i in range(ends)]),
            ],
            axis=dim,
        )
    return cells


def flat_laplace(extended):
    sides = jnp.pad(extended, ((0, 0), (1, 1)))
    beside_all = extended[2:] + extended[:-2] + sides[1:-1, 2:] + sides[1:-1, :-2]
    return beside_all - 4.0 * extended[1:-1]


def place_rows(block, first_row, strip_start, breadth):
    spread = jnp.pad(block, ((breadth, breadth), (0, 0)))
    begin = jnp.clip(strip_start - first_row + breadth, 0, block.shape[0] + breadth)
    return lax.dynamic_slice_in_dim(spread, begin, breadth, 0)


def shards(air_now, air_prev, plate_now, plate_prev, plate_level, plate_shift):
    depth, breadth, width = air_now.shape
    rows = plate_now.shape[0]
    foot = rows // 4
    n_gy = lax.axis_size("gy")
    n_all = lax.axis_size("gz") * n_gy
    slab = lax.axis_index("gz")
    strip = lax.axis_index("gy")
    device = slab * n_gy + strip
    level = plate_level[0]
    shift = plate_shift[0]
    base = slab * depth
    levels = base + jnp.arange(depth, dtype=jnp.int32)
    select = (levels == level).astype(jnp.float32) - (levels == level + 1).astype(jnp.float32)
    lower_in = (level >= base) & (level < base + depth)
    upper_in = (level + 1 >= base) & (level + 1 < base + depth)
    global_rows = device * rows - 1 + jnp.arange(rows + 2, dtype=jnp.int32)
    inside = ((global_rows >= 0) & (global_rows < n_all * rows))[:, None]
    for step in range(STEPS):
        upper = lax.dynamic_index_in_dim(
            air_now, jnp.clip(level + 1 - base, 0, depth - 1), 0, keepdims=False
        )
        lower = lax.dynamic_index_in_dim(
            air_now, jnp.clip(level - base, 0, depth - 1), 0, keepdims=False
        )
        contrib = jnp.where(upper_in, upper, 0.0) - jnp.where(lower_in, lower, 0.0)
        column = lax.psum(contrib, "gz")
        plane = lax.all_gather(column, "gy", axis=0, tiled=True)
        pressure = lax.dynamic_slice_in_dim(plane, shift + device * foot, foot, 0)
        force = jnp.repeat(jnp.repeat(pressure, 4, 0), 4, 1)
        motion = (plate_now - plate_prev).reshape(foot, 4, width, 4).mean(axis=(1, 3))
        everyone = lax.all_gather(motion, ("gz", "gy"), axis=0, tiled=True)
        source = place_rows(everyone, shift, strip * breadth, breadth)
        extended = padded(air_now, (("gz", 0), ("gy", 1)), 1)
        sides = jnp.pad(air_now, ((0, 0), (0, 0), (1, 1)))
        beside_all = extended[2:, 1:-1] + extended[:-2, 1:-1]
        beside_all = beside_all + extended[1:-1, 2:] + extended[1:-1, :-2]
        beside_all = beside_all + sides[:, :, 2:] + sides[:, :, :-2]
        air_next = 2.0 * air_now - air_prev + 0.3 * (beside_all - 6.0 * air_now)
        air_next = air_next + 0.5 * source[None] * select[:, None, None]
        rim = padded(plate_now, ((("gz", "gy"), 0),), 2)
        inner = jnp.where(inside, flat_laplace(rim), 0.0)
        bend = flat_laplace(inner)
        plate_next = (2.0 * plate_now - 0.99 * plate_prev - 0.04 * bend + 0.5 * force) / 1.01
        air_prev, air_now = (air_now, air_next)
        plate_prev, plate_now = (plate_now, plate_next)
    return (air_now, plate_now)


def solution(mesh):
    in_specs = (
        P("gz", "gy", None),
        P("gz", "gy", None),
        P(("gz", "gy"), None),
        P(("gz", "gy"), None),
        P(),
        P(),
    )
    out_specs = (P("gz", "gy", None), P(("gz", "gy"), None))
    return jax.shard_map(shards, mesh=mesh, in_specs=in_specs, out_specs=out_specs, check_vma=False)
```

profile of v0, /device:TPU:6, one launch (start us, length us, event | category | flops | bytes accessed | tf_op | source)
XLA Modules:
  0.0 969.1 jit_solution(17518173730790294697)
XLA Ops:
  7.2 0.0 all-gather.11.cloned.1.call-start
  7.2 1.1 sub.78
  8.3 10.7 %reshape.56 = f32[4,4,1024,4]{3,2,1,0:T(8,128)} reshape(f32[16,4096]{1,0:T(8,128)S(1)} %sub.78) | data formatting | bytes 524288 | tf_op jit(solution)/shard_map/reshape | solution.py:68
  19.0 4.0 reduce_sum.18
  23.0 0.6 multiply_bitcast_fusion.1
  23.6 0.0 all-gather.11.cloned.1.call-update
  23.7 0.0 all-reduce.11.cloned.1.call-start
  24.4 2.6 subtract_bitcast_fusion.1
  27.0 1.9 collective-permute-start.1
  28.9 5.8 collective-permute-start
  35.3 4.3 collective-permute-done.1
  39.7 2.5 constant_dynamic-update-slice_fusion.1
  42.3 2.3 copy-done.2
  44.6 0.1 fusion.44
  44.7 6.8 collective-permute-start.2
  51.5 1.9 collective-permute-start.3
  53.4 270.7 %all-gather.11.cloned.1.call-done = f32[128,4,1024]{2,1,0:T(4,128)} async-done(((f32[1,4,1024]{2,1,0:T(4,128)}), f32[128,4,1024]{2,1,0:T(4,128)}) %all-gather.11.cloned.1.call-update) | async-done | bytes 2097168 | tf_op jit(solution)/shard_map/all_gather | solution.py:69
  324.1 2.0 reshape.59
  326.1 0.1 fusion.18
  326.3 14.0 %fusion.5 = f32[8,128,1024]{2,1,0:T(8,128)S(1)} fusion(f32[8,128,1024]{2,1,0:T(8,128)} %param.6, f32[10,128,1024]{2,1,0:T(8,128)} %copy-done.2, f32[10,1,1024]{2,1,0:T(1,128)S(1)} %collective-permute-done.3, f32[10,1,1024]{2,1,0:T(1,128)S(1)} %collective-permute-done.2, f32[1,128,1024]{2,1,0:T(8,128)S(1)} %collective-permute-done.1, ...), kind=kLoop, calls=%fused_computation.9 | loop fusion | flops 17825792 | bytes 19480608 | tf_op jit(solution)/shard_map/add | solution.py:77
  340.3 2.0 copy-done
  342.3 1.2 subtract_bitcast_fusion
  343.5 0.0 all-reduce.11.cloned.1.call-update
  343.5 0.0 all-gather.7.cloned.1.call-start
  343.5 121.1 %all-reduce.11.cloned.1.call-done = (f32[128,1024]{1,0:T(8,128)}, f32[128,1024]{1,0:T(8,128)}) async-done(((f32[128,1024]{1,0:T(8,128)}, f32[128,1024]{1,0:T(8,128)}), (f32[128,1024]{1,0:T(8,128)}, f32[128,1024]{1,0:T(8,128)})) %all-reduce.11.cloned.1.call-update) | async-done | bytes 1048592 | tf_op jit(solution)/shard_map/psum | solution.py:64
  464.7 0.0 all-gather.9.cloned.1.call-start
  464.7 0.5 all-gather.9.cloned.1.call-update
  465.3 0.0 all-gather.13.cloned.1.call-start
  465.4 5.7 collective-permute-start.8
  471.1 1.9 collective-permute-start.9
  473.1 7.4 collective-permute-done.9
  480.5 0.1 pad_maximum_fusion.12
  480.6 0.3 fusion.23
  480.9 58.1 %all-gather.7.cloned.1.call-done = f32[1024,1024]{1,0:T(8,128)} async-done(((f32[128,1024]{1,0:T(8,128)}), f32[1024,1024]{1,0:T(8,128)}) %all-gather.7.cloned.1.call-update) | async-done | bytes 4194320 | tf_op jit(solution)/shard_map/all_gather | solution.py:65
  538.9 71.9 %all-gather.9.cloned.1.call-done = f32[1024,1024]{1,0:T(8,128)} async-done(((f32[128,1024]{1,0:T(8,128)}), f32[1024,1024]{1,0:T(8,128)}) %all-gather.9.cloned.1.call-update) | async-done | bytes 4194320 | tf_op jit(solution)/shard_map/all_gather | solution.py:65
  610.8 0.9 dynamic-slice_multiply_fusion
  611.7 0.2 copy.85
  611.9 0.4 broadcast_in_dim.44
  612.3 0.6 copy.86
  612.9 0.9 broadcast_multiply_fusion
  613.8 0.6 fusion.45
  614.5 4.2 collective-permute-start.10
  618.6 2.1 collective-permute-start.11
  620.8 0.2 copy.87
  621.0 0.4 broadcast_in_dim.46
  621.4 0.6 copy.88
  621.9 6.4 collective-permute-done.11
  628.4 0.8 pad_maximum_fusion.13
  629.2 1.1 fusion.21
  630.3 0.9 fusion.40
  631.2 10.7 %reshape.57 = f32[4,4,1024,4]{3,2,1,0:T(8,128)} reshape(f32[16,4096]{1,0:T(8,128)S(1)} %get-tuple-element.25) | data formatting | bytes 524288 | tf_op jit(solution)/shard_map/reshape | solution.py:68
  641.9 4.1 reduce_sum.19
  646.0 0.6 multiply_bitcast_fusion
  646.7 2.5 collective-permute-start.4
  649.2 1.9 collective-permute-start.5
  651.2 4.8 collective-permute-done.4
  656.0 6.0 collective-permute-done.5
  662.0 1.1 pad_maximum_fusion.16
  663.1 2.5 collective-permute-start.6
  665.6 3.3 collective-permute-start.7
  669.0 275.8 %all-gather.13.cloned.1.call-done = f32[128,4,1024]{2,1,0:T(4,128)} async-done(((f32[1,4,1024]{2,1,0:T(4,128)}), f32[128,4,1024]{2,1,0:T(4,128)}) %all-gather.13.cloned.1.call-update) | async-done | bytes 2097168 | tf_op jit(solution)/shard_map/all_gather | solution.py:69
  944.8 2.0 reshape.61
  946.8 0.1 fusion.19
  946.9 15.6 %fusion.11 = f32[8,128,1024]{2,1,0:T(8,128)} fusion(f32[8,128,1024]{2,1,0:T(8,128)} %copy-done, f32[10,1,1024]{2,1,0:T(1,128)S(1)} %collective-permute-done.7, f32[1,128,1024]{2,1,0:T(8,128)S(1)} %collective-permute-done.4, f32[1,128,1024]{2,1,0:T(8,128)S(1)} %collective-permute-done.5, f32[10,1,1024]{2,1,0:T(1,128)S(1)} %collective-permute-done.6, ...), kind=kLoop, calls=%fused_computation.15 | loop fusion | flops 22020096 | bytes 14237728 | tf_op jit(solution)/shard_map/add | solution.py:77
  (36 shorter events, 0.3 us)
Async XLA Ops:
  7.2 317.0 %all-gather.11.cloned.1.call-start = ((), (), s32[]{:S(2)}) async-start(), calls=%async_computation.2 | async-start | bytes 2113536 | tf_op jit(solution)/shard_map/all_gather | solution.py:69
  23.7 441.0 %all-reduce.11.cloned.1.call-start = ((), (), s32[]{:S(2)}) async-start(), calls=%async_computation.4 | async-start | bytes 2097152 | tf_op jit(solution)/shard_map/psum | solution.py:64
  27.0 12.7 %collective-permute-start.1 = (f32[1,128,1024]{2,1,0:T(8,128)S(1)}, f32[1,128,1024]{2,1,0:T(8,128)S(1)}, u32[]{:S(2)}, u32[]{:S(2)}) collective-permute-start(f32[1,128,1024]{2,1,0:T(8,128)S(1)} %get-tuple-element.22), channel_id=1, source_target_pairs={{0,8},{8,16},{16,24},{24,32},{32,40},{40,48},{48,56},{56,64},{64,7... | collective-permute-start | bytes 1572872 | tf_op jit(solution)/shard_map/ppermute | solution.py:17
  28.9 13.3 %collective-permute-start = (f32[1,128,1024]{2,1,0:T(8,128)S(1)}, f32[1,128,1024]{2,1,0:T(8,128)S(1)}, u32[]{:S(2)}, u32[]{:S(2)}) collective-permute-start(f32[1,128,1024]{2,1,0:T(8,128)S(1)} %get-tuple-element.23), channel_id=1, source_target_pairs={{8,0},{16,8},{24,16},{32,24},{40,32},{48,40},{56,48},{64,56},{72,6... | collective-permute-start | bytes 1572872 | tf_op jit(solution)/shard_map/ppermute | solution.py:19
  35.3 290.9 %copy-start.7 = (f32[8]{0:T(128)}, f32[8]{0:T(128)S(1)}, u32[]{:S(2)}) copy-start(f32[8]{0:T(128)S(1)} %fusion.41) | copy-start | bytes 100
  42.3 2.3 copy-start.2
  44.7 281.6 %collective-permute-start.2 = (f32[10,1,1024]{2,1,0:T(1,128)S(1)}, f32[10,1,1024]{2,1,0:T(1,128)S(1)}, u32[]{:S(2)}, u32[]{:S(2)}) collective-permute-start(f32[10,1,1024]{2,1,0:T(1,128)S(1)} %get-tuple-element.16), channel_id=1, source_target_pairs={{1,0},{2,1},{3,2},{4,3},{5,4},{6,5},{7,6},{9,8},{10,9},{11,10},{12... | collective-permute-start | bytes 122888 | tf_op jit(solution)/shard_map/ppermute | solution.py:19
  51.5 274.8 %collective-permute-start.3 = (f32[10,1,1024]{2,1,0:T(1,128)S(1)}, f32[10,1,1024]{2,1,0:T(1,128)S(1)}, u32[]{:S(2)}, u32[]{:S(2)}) collective-permute-start(f32[10,1,1024]{2,1,0:T(1,128)S(1)} %get-tuple-element.17), channel_id=1, source_target_pairs={{0,1},{1,2},{2,3},{3,4},{4,5},{5,6},{6,7},{8,9},{9,10},{10,11},{11... | collective-permute-start | bytes 122888 | tf_op jit(solution)/shard_map/ppermute | solution.py:17
  340.3 2.0 copy-start
  342.3 123.0 %copy-start.1 = (f32[16,4096]{1,0:T(8,128)S(1)}, f32[16,4096]{1,0:T(8,128)}, u32[]{:S(2)}) copy-start(f32[16,4096]{1,0:T(8,128)} %param.8) | copy-start | bytes 786436
  343.5 195.4 %all-gather.7.cloned.1.call-start = ((), (), s32[]{:S(2)}) async-start(), calls=%async_computation | async-start | bytes 4718592 | tf_op jit(solution)/shard_map/all_gather | solution.py:65
  464.7 146.1 %all-gather.9.cloned.1.call-start = ((), (), s32[]{:S(2)}) async-start(), calls=%async_computation.1 | async-start | bytes 4718592 | tf_op jit(solution)/shard_map/all_gather | solution.py:65
  465.3 147.6 %copy-start.3 = (f32[16,4096]{1,0:T(8,128)S(1)}, f32[16,4096]{1,0:T(8,128)}, u32[]{:S(2)}) copy-start(f32[16,4096]{1,0:T(8,128)} %param.9) | copy-start | bytes 786436
  465.3 479.5 %all-gather.13.cloned.1.call-start = ((), (), s32[]{:S(2)}) async-start(), calls=%async_computation.3 | async-start | bytes 2113536 | tf_op jit(solution)/shard_map/all_gather | solution.py:69
  465.4 7.7 collective-permute-start.8
  471.1 9.4 collective-permute-start.9
  473.1 65.9 %copy-start.9 = (pred[18]{0:T(512)(128)(4,1)}, pred[18]{0:T(512)(128)(4,1)S(1)}, u32[]{:S(2)}) copy-start(pred[18]{0:T(512)(128)(4,1)S(1)} %compare_and_fusion) | copy-start | bytes 58
  613.8 16.5 %copy-start.4 = (f32[16,4096]{1,0:T(8,128)S(1)}, f32[16,4096]{1,0:T(8,128)}, u32[]{:S(2)}) copy-start(f32[16,4096]{1,0:T(8,128)} %get-tuple-element.13) | copy-start | bytes 786436
  614.5 7.5 collective-permute-start.10
  618.6 9.7 %collective-permute-start.11 = (f32[2,4096]{1,0:T(2,128)}, f32[2,4096]{1,0:T(2,128)}, u32[]{:S(2)}, u32[]{:S(2)}) collective-permute-start(f32[2,4096]{1,0:T(2,128)} %get-tuple-element.26), channel_id=1, source_target_pairs={{0,1},{1,2},{2,3},{3,4},{4,5},{5,6},{6,7},{7,8},{8,9},{9,10},{10,1... | collective-permute-start | bytes 98312 | tf_op jit(solution)/shard_map/ppermute | solution.py:17
  641.9 4.8 copy-start.6
  641.9 7.3 copy-start.5
  646.7 9.3 collective-permute-start.4
  649.2 12.8 %collective-permute-start.5 = (f32[1,128,1024]{2,1,0:T(8,128)S(1)}, f32[1,128,1024]{2,1,0:T(8,128)S(1)}, u32[]{:S(2)}, u32[]{:S(2)}) collective-permute-start(f32[1,128,1024]{2,1,0:T(8,128)S(1)} %copy-done.5), channel_id=1, source_target_pairs={{0,8},{8,16},{16,24},{24,32},{32,40},{40,48},{48,56},{56,64},{64,7... | collective-permute-start | bytes 1572872 | tf_op jit(solution)/shard_map/ppermute | solution.py:17
  663.1 283.8 %copy-start.8 = (f32[8]{0:T(128)S(1)}, f32[8]{0:T(128)}, u32[]{:S(2)}) copy-start(f32[8]{0:T(128)} %copy-done.7) | copy-start | bytes 100
  663.1 283.8 %collective-permute-start.6 = (f32[10,1,1024]{2,1,0:T(1,128)S(1)}, f32[10,1,1024]{2,1,0:T(1,128)S(1)}, u32[]{:S(2)}, u32[]{:S(2)}) collective-permute-start(f32[10,1,1024]{2,1,0:T(1,128)S(1)} %get-tuple-element.14), channel_id=1, source_target_pairs={{1,0},{2,1},{3,2},{4,3},{5,4},{6,5},{7,6},{9,8},{10,9},{11,10},{12... | collective-permute-start | bytes 122888 | tf_op jit(solution)/shard_map/ppermute | solution.py:19
  665.6 281.3 %collective-permute-start.7 = (f32[10,1,1024]{2,1,0:T(1,128)S(1)}, f32[10,1,1024]{2,1,0:T(1,128)S(1)}, u32[]{:S(2)}, u32[]{:S(2)}) collective-permute-start(f32[10,1,1024]{2,1,0:T(1,128)S(1)} %get-tuple-element.15), channel_id=1, source_target_pairs={{0,1},{1,2},{2,3},{3,4},{4,5},{5,6},{6,7},{8,9},{9,10},{10,11},{11... | collective-permute-start | bytes 122888 | tf_op jit(solution)/shard_map/ppermute | solution.py:17
Sparse Core Ops, SparseCore 0:
  23.8 300.3 all-gather.10
  343.6 120.9 all-reduce.10
  467.3 71.5 all-gather.6
  541.4 69.3 all-gather.8
  646.8 297.9 all-gather.12
where the time goes:
time: 973 us; the launch traced here: 969 us
  waiting for transfers between devices  827 us (85%)
  other arithmetic  50.1 us (5%)
  starting transfers between devices  40.8 us (4%)
  local copies, waits for them, and re-layouts  35.4 us (4%)
  between operations  15.5 us (2%)
    all_gather x2, waiting for transfers between devices, shards(): everyone = lax.all_gather(motion, ('gz', 'gy'), axis=0, tiled=True)  547 us
    all_gather x2, waiting for transfers between devices, shards(): plane = lax.all_gather(column, 'gy', axis=0, tiled=True)  130 us
    psum x1, waiting for transfers between devices, shards(): column = lax.psum(contrib, 'gz')  121 us
    add x2, other arithmetic, shards(): air_next = air_next + 0.5 * source[None] * select[:, None, None]  29.7 us
    ppermute x6, starting transfers between devices, padded(): lax.ppermute(head, axis, [((i + 1) % count, i) for i in range(ends)])  27.5 us
    ppermute x6, waiting for transfers between devices, padded(): lax.ppermute(tail, axis, [(i, (i + 1) % count) for i in range(ends)])  24.2 us
    reshape x2, local copies, waits for them, and re-layouts, shards(): (plate_now - plate_prev).reshape(foot, 4, width, 4).mean(axis=(1, 3))  21.4 us
  transfers between devices with their start and end apart: 17, of which 10 were waited for; matrix products, arithmetic and copies ran while one was open for 1% of the time, Pallas kernels for 0%

commit v1 on v0

v1 whole, which is shorter than its diff:
```python
import functools

import jax
import jax.numpy as jnp
from jax import lax
from jax.experimental import pallas as pl
from jax.experimental.pallas import tpu as pltpu
from jax.sharding import PartitionSpec as P

F32 = jnp.float32
C_PRESS = 0.5 / 1.01
HIGH = lax.Precision.HIGHEST


def params(mib):
    return pltpu.CompilerParams(vmem_limit_bytes=mib << 20)


def cost(nbytes):
    return pl.CostEstimate(flops=nbytes, bytes_accessed=nbytes, transcendentals=0)


def iota(shape, axis):
    return lax.broadcasted_iota(jnp.int32, shape, axis)


def left_right(x):
    width = x.shape[1]
    col = iota(x.shape, 1)
    west = jnp.where(col == 0, 0.0, pltpu.roll(x, 1, 1))
    east = jnp.where(col == width - 1, 0.0, pltpu.roll(x, width - 1, 1))
    return west + east


def up_down(x, above, below):
    height = x.shape[0]
    row = iota(x.shape, 0)
    up = jnp.where(row == 0, above, pltpu.roll(x, 1, 0))
    down = jnp.where(row == height - 1, below, pltpu.roll(x, height - 1, 0))
    return up + down


def air_kernel(now, prev, zlo, zhi, ylo, yhi, out, *edges):
    z = pl.program_id(0)
    depth = now.shape[0]
    here = now[z]
    under = jnp.where(z == 0, zlo[...], now[jnp.maximum(z - 1, 0)])
    over = jnp.where(z == depth - 1, zhi[...], now[jnp.minimum(z + 1, depth - 1)])
    total = under + over + left_right(here)
    total = total + up_down(here, ylo[pl.ds(z, 1), :], yhi[pl.ds(z, 1), :])
    nxt = 0.2 * here - prev[0] + 0.3 * total
    out[0] = nxt
    if edges:
        height = here.shape[0]
        edges[0][pl.ds(z, 1), :] = nxt[0:1]
        edges[1][pl.ds(z, 1), :] = nxt[height - 1 : height]


def air_step(now, prev, zlo, zhi, ylo, yhi, want_edges):
    depth, height, width = now.shape
    plane = pl.BlockSpec((1, height, width), lambda z: (z, 0, 0))
    face = pl.BlockSpec((height, width), lambda z: (0, 0))
    rows = pl.BlockSpec((depth, width), lambda z: (0, 0))
    out_shape = [jax.ShapeDtypeStruct(now.shape, F32)]
    out_specs = [plane]
    if want_edges:
        out_shape += [jax.ShapeDtypeStruct((depth, width), F32)] * 2
        out_specs += [rows, rows]
    return pl.pallas_call(
        air_kernel,
        grid=(depth,),
        in_specs=[
            pl.BlockSpec((depth, height, width), lambda z: (0, 0, 0)),
            plane,
            face,
            face,
            rows,
            rows,
        ],
        out_specs=out_specs,
        out_shape=out_shape,
        compiler_params=params(30),
        cost_estimate=cost(14 << 20),
    )(now, prev, zlo, zhi, ylo, yhi)


def press_kernel(scal, up2, up1, at0, dn1, pup1, pat0, ylo, yhi, out, c0, c1):
    level, shift, base = scal[0], scal[1], scal[2]
    depth = ylo.shape[0]
    height, width = c0.shape

    def mine(z):
        return jnp.where((z >= base) & (z < base + depth), 1.0, 0.0).astype(F32)

    here = (level + 2 >= base) & (level - 1 < base + depth)

    @pl.when(jnp.logical_not(here))
    def _():
        out[...] = jnp.zeros(out.shape, F32)

    @pl.when(here)
    def _():
        m1, m0 = mine(level + 1), mine(level)
        m2, mm = mine(level + 2), mine(level - 1)
        z = iota((depth, width), 0) + base
        pick = jnp.where(z == level + 1, 1.0, 0.0) - jnp.where(z == level, 1.0, 0.0)
        above = jnp.sum(pick * ylo[...], axis=0, keepdims=True)
        below = jnp.sum(pick * yhi[...], axis=0, keepdims=True)
        top, bottom = m1 * up1[0], m0 * at0[0]
        press = top - bottom
        flat = left_right(press) + up_down(press, above, below) - 4.0 * press
        vertical = m2 * up2[0] - 3.0 * press - mm * dn1[0]
        older = m1 * pup1[0] - m0 * pat0[0]
        c0[...] = press
        c1[...] = 2.0 * press - older + 0.3 * (flat + vertical)
        b = shift & 31
        turn = (32 - b) & 31
        for k in range(height // 32):
            r0 = pltpu.roll(c0[32 * k : 32 * k + 32], turn, 0)
            r1 = pltpu.roll(c1[32 * k : 32 * k + 32], turn, 0)
            for y in range(8):
                out[y, 8 * k : 8 * k + 4, :] = r0[4 * y : 4 * y + 4]
                out[y, 8 * k + 4 : 8 * k + 8, :] = r1[4 * y : 4 * y + 4]


def press_pack(scal, air_now, air_prev, ylo, yhi):
    depth, height, width = air_now.shape

    def plane(offset):
        def where(i, scal):
            return (jnp.clip(scal[0] + offset - scal[2], 0, depth - 1), 0, 0)

        return pl.BlockSpec((1, height, width), where)

    rows = pl.BlockSpec((depth, width), lambda i, scal: (0, 0))
    return pl.pallas_call(
        press_kernel,
        grid_spec=pltpu.PrefetchScalarGridSpec(
            num_scalar_prefetch=1,
            grid=(1,),
            in_specs=[plane(2), plane(1), plane(0), plane(-1), plane(1), plane(0), rows, rows],
            out_specs=pl.BlockSpec((8, 32, width), lambda i, scal: (0, 0, 0)),
            scratch_shapes=[pltpu.VMEM((height, width), F32)] * 2,
        ),
        out_shape=jax.ShapeDtypeStruct((8, 32, width), F32),
        compiler_params=params(30),
        cost_estimate=cost(4 << 20),
    )(scal, air_now, air_now, air_now, air_now, air_prev, air_prev, ylo, yhi)


def flat_laplace(x):
    height = x.shape[0]
    return left_right(x) + pltpu.roll(x, 1, 0) + pltpu.roll(x, height - 1, 0) - 4.0 * x


def inside_rows(shape, first, last_row):
    row = iota(shape, 0) + first
    return (row >= 0) & (row < last_row)


def plate_kernel(n_rows, scal, now, prev, lo, hi, next_ext, motion):
    rows, cols = now.shape
    first = scal[3] * rows - 4
    here = now[...]
    ext = jnp.concatenate([lo[0:4], here, hi[0:4]], axis=0)
    old = jnp.concatenate([lo[4:8], prev[...], hi[4:8]], axis=0)
    ok = inside_rows(ext.shape, first, n_rows)
    inner = jnp.where(ok, flat_laplace(ext), 0.0)
    bend = flat_laplace(inner)
    nxt = (2.0 * ext - 0.99 * old - 0.04 * bend) * (1.0 / 1.01)
    nxt = jnp.where(ok, nxt, 0.0)
    next_ext[...] = nxt
    both = jnp.concatenate([here - prev[...], nxt[4 : 4 + rows] - here], axis=0)
    fold = jnp.where((iota((512, 128), 0) >> 2) == iota((512, 128), 1), 1.0, 0.0)
    parts = [
        jnp.dot(both[:, 512 * q : 512 * q + 512], fold, precision=HIGH, preferred_element_type=F32)
        for q in range(cols // 512)
    ]
    narrow = jnp.concatenate(parts, axis=1)
    pick = jnp.where(iota((8, 32), 0) == (iota((8, 32), 1) >> 2), 1.0 / 16.0, 0.0)
    motion[...] = jnp.dot(pick, narrow, precision=HIGH, preferred_element_type=F32)


def plate_first(scal, now, prev, lo, hi, n_rows):
    rows, cols = now.shape
    return pl.pallas_call(
        functools.partial(plate_kernel, n_rows),
        in_specs=[pl.BlockSpec(memory_space=pltpu.SMEM)]
        + [pl.BlockSpec(memory_space=pltpu.VMEM)] * 4,
        out_specs=[pl.BlockSpec(memory_space=pltpu.VMEM)] * 2,
        out_shape=[
            jax.ShapeDtypeStruct((rows + 8, cols), F32),
            jax.ShapeDtypeStruct((8, cols // 4), F32),
        ],
        compiler_params=params(16),
        cost_estimate=cost(4 << 20),
    )(scal, now, prev, lo, hi)


def carries(shape, strip, b):
    return (4 * strip + (iota(shape, 0) & 3) + b) >= 32


def to_plate_kernel(scal, came, motion, out):
    shift, strip = scal[1], scal[4]
    a, b = shift >> 5, shift & 31
    move = motion[...]
    carry = carries(move.shape, strip, b)
    for dest in range(16):
        at = pl.multiple_of(8 * (dest + a), 8)
        after = pl.multiple_of(8 * jnp.minimum(dest + a + 1, 31), 8)
        out[dest, 0:8, :] = jnp.where(carry, came[pl.ds(after, 8), :], came[pl.ds(at, 8), :])
        out[dest, 8:16, :] = move


def to_plate(scal, came, motion):
    width = motion.shape[1]
    return pl.pallas_call(
        to_plate_kernel,
        in_specs=[pl.BlockSpec(memory_space=pltpu.SMEM)]
        + [pl.BlockSpec(memory_space=pltpu.VMEM)] * 2,
        out_specs=pl.BlockSpec(memory_space=pltpu.VMEM),
        out_shape=jax.ShapeDtypeStruct((16, 16, width), F32),
        compiler_params=params(16),
        cost_estimate=cost(2 << 20),
    )(scal, came, motion)


def to_air_kernel(scal, came, pressure, out):
    shift, strip = scal[1], scal[4]
    a, b = shift >> 5, shift & 31
    width = pressure.shape[1]
    total = came[0, 0:8, :]
    for src in range(1, 16):
        total = total + came[src, 0:8, :]
    pressure[...] = total
    shape = (8, width)
    carry = carries(shape, strip, b)
    row = iota(shape, 0)
    place = (4 * strip + (row & 3) + b) & 31
    first_field = row < 4

    def tile(block):
        def one(src):
            ok = jnp.where((src >= 0) & (src < 16), 1.0, 0.0).astype(F32)
            return came[jnp.clip(src, 0, 15), 8:16, :] * ok

        return jnp.where(carry, one(block - a - 1), one(block - a))

    for s in range(8):
        tiles = [tile(4 * s + k) for k in range(4)]
        for k in range(4):
            out[s, 8 * k : 8 * k + 8, :] = tiles[k]
        if s > 0:
            before = jnp.where(first_field & (place == 31), tile(4 * s - 1), 0.0)
        else:
            before = jnp.zeros(shape, F32)
        if s < 7:
            behind = jnp.where(first_field & (place == 0), tile(4 * s + 4), 0.0)
        else:
            behind = jnp.zeros(shape, F32)
        out[s, 32:40, :] = before + pltpu.roll(behind, 4, 0)


def to_air(scal, came):
    width = came.shape[2]
    return pl.pallas_call(
        to_air_kernel,
        in_specs=[
            pl.BlockSpec(memory_space=pltpu.SMEM),
            pl.BlockSpec(memory_space=pltpu.VMEM),
        ],
        out_specs=[pl.BlockSpec(memory_space=pltpu.VMEM)] * 2,
        out_shape=[
            jax.ShapeDtypeStruct((8, width), F32),
            jax.ShapeDtypeStruct((8, 40, width), F32),
        ],
        compiler_params=params(16),
        cost_estimate=cost(2 << 20),
    )(scal, came)


def local_press_kernel(scal, up1, at0, zlo, zhi, out):
    level, shift, base, strip = scal[0], scal[1], scal[2], scal[4]
    height, width = out.shape
    depth = 8
    top = jnp.where(level + 1 == base + depth, zhi[...], up1[0])
    bottom = jnp.where(level == base - 1, zlo[...], at0[0])
    y = iota((height, width), 0) + strip * height - shift
    out[...] = jnp.where((y >= 0) & (y < 512), (0.5 * C_PRESS) * (top - bottom), 0.0)


def local_press(scal, air_now, zlo, zhi):
    depth, height, width = air_now.shape

    def plane(offset):
        def where(i, scal):
            return (jnp.clip(scal[0] + offset - scal[2], 0, depth - 1), 0, 0)

        return pl.BlockSpec((1, height, width), where)

    face = pl.BlockSpec((height, width), lambda i, scal: (0, 0))
    return pl.pallas_call(
        local_press_kernel,
        grid_spec=pltpu.PrefetchScalarGridSpec(
            num_scalar_prefetch=1,
            grid=(1,),
            in_specs=[plane(1), plane(0), face, face],
            out_specs=face,
        ),
        out_shape=jax.ShapeDtypeStruct((height, width), F32),
        compiler_params=params(16),
        cost_estimate=cost(2 << 20),
    )(scal, air_now, air_now, zlo, zhi)


def force_kernel(scal, field, came, press, out, q, r):
    level, shift, base = scal[0], scal[1], scal[2]
    t = pl.program_id(0)
    height, width = q.shape
    depth = 8
    b = shift & 31

    @pl.when(t == 0)
    def _():
        for k in range(height // 32):
            for f, ref in ((0, r), (1, q)):
                rows = [came[y, 8 * k + 4 * f : 8 * k + 4 * f + 4, :] for y in range(8)]
                ref[32 * k : 32 * k + 32, :] = pltpu.roll(jnp.concatenate(rows, axis=0), b, 0)
        rim = came[0, 32:40, :]
        for y in range(1, 8):
            rim = rim + came[y, 32:40, :]
        above = jnp.sum(rim[0:4], axis=0, keepdims=True)
        below = jnp.sum(rim[4:8], axis=0, keepdims=True)
        motion = r[...]
        around = left_right(motion) + up_down(motion, above, below)
        q[...] = (0.55 - 0.6) * motion + 0.15 * around + 0.5 * q[...] + press[...]

    z = jnp.clip(level - 1 + t - base, 0, depth - 1) + base

    def is_level(other):
        return jnp.where(z == other, 1.0, 0.0).astype(F32)

    wq = is_level(level) - is_level(level + 1)
    wr = 0.15 * (is_level(level - 1) - is_level(level + 2))
    out[0] = field[0] + wq * q[...] + wr * r[...]


def add_force(scal, field, came, press):
    depth, height, width = field.shape

    def where(t, scal):
        return (jnp.clip(scal[0] - 1 + t - scal[2], 0, depth - 1), 0, 0)

    plane = pl.BlockSpec((1, height, width), where)
    return pl.pallas_call(
        force_kernel,
        grid_spec=pltpu.PrefetchScalarGridSpec(
            num_scalar_prefetch=1,
            grid=(4,),
            in_specs=[
                plane,
                pl.BlockSpec((8, 40, width), lambda t, scal: (0, 0, 0)),
                pl.BlockSpec((height, width), lambda t, scal: (0, 0)),
            ],
            out_specs=plane,
            scratch_shapes=[pltpu.VMEM((height, width), F32)] * 2,
        ),
        out_shape=jax.ShapeDtypeStruct(field.shape, F32),
        input_output_aliases={1: 0},
        compiler_params=params(24),
        cost_estimate=cost(4 << 20),
    )(scal, field, came, press)


def plate_last_kernel(n_rows, scal, now, next_ext, pressure, motion, lo, hi, out):
    rows, cols = now.shape
    first = scal[3] * rows - 4
    own = pressure[...]
    width = own.shape[1]
    lines = jnp.concatenate(
        [own[0:4], own[4:8] - motion[0:4], lo[...], hi[...], jnp.zeros((6, width), F32)], axis=0
    )
    spread = jnp.where((iota((128, 512), 1) >> 2) == iota((128, 512), 0), 1.0, 0.0)
    parts = [
        jnp.dot(lines[:, 128 * q : 128 * q + 128], spread, precision=HIGH, preferred_element_type=F32)
        for q in range(width // 128)
    ]
    wide = jnp.concatenate(parts, axis=1)
    e = iota((24, 16), 0)
    line = iota((24, 16), 1)
    source = jnp.where(e < 4, 8, jnp.where(e >= 20, 9, (e - 4) >> 2))
    pick = jnp.where(line == source, C_PRESS, 0.0)
    push = jnp.dot(pick, wide, precision=HIGH, preferred_element_type=F32)
    pick = jnp.where(iota((16, 16), 1) == 4 + (iota((16, 16), 0) >> 2), C_PRESS, 0.0)
    push_last = jnp.dot(pick, wide, precision=HIGH, preferred_element_type=F32)
    ok = inside_rows(next_ext.shape, first, n_rows)
    mid = jnp.where(ok, next_ext[...] + push, 0.0)
    inner = jnp.where(ok, flat_laplace(mid), 0.0)
    bend = flat_laplace(inner)[4 : 4 + rows]
    final = (2.0 * mid[4 : 4 + rows] - 0.99 * now[...] - 0.04 * bend) * (1.0 / 1.01)
    out[...] = final + push_last


def plate_last(scal, now, next_ext, pressure, motion, lo, hi, n_rows):
    return pl.pallas_call(
        functools.partial(plate_last_kernel, n_rows),
        in_specs=[pl.BlockSpec(memory_space=pltpu.SMEM)]
        + [pl.BlockSpec(memory_space=pltpu.VMEM)] * 6,
        out_specs=pl.BlockSpec(memory_space=pltpu.VMEM),
        out_shape=jax.ShapeDtypeStruct(now.shape, F32),
        compiler_params=params(16),
        cost_estimate=cost(4 << 20),
    )(scal, now, next_ext, pressure, motion, lo, hi)


def neighbours(n):
    return [(i, i + 1) for i in range(n - 1)], [(i + 1, i) for i in range(n - 1)]


def shards(air_now, air_prev, plate_now, plate_prev, plate_level, plate_shift):
    depth, height, width = air_now.shape
    n_gz, n_gy = lax.axis_size("gz"), lax.axis_size("gy")
    slab, strip = lax.axis_index("gz"), lax.axis_index("gy")
    device = slab * n_gy + strip
    n_rows = plate_now.shape[0] * n_gz * n_gy
    zero = jnp.int32(0)
    scal = jnp.stack(
        [plate_level[0], plate_shift[0], slab * depth, device, strip, zero, zero, zero]
    ).astype(jnp.int32)
    up_y, down_y = neighbours(n_gy)
    up_z, down_z = neighbours(n_gz)
    up_d, down_d = neighbours(n_gz * n_gy)

    ylo = lax.ppermute(air_now[:, height - 1, :], "gy", up_y)
    yhi = lax.ppermute(air_now[:, 0, :], "gy", down_y)
    sent = press_pack(scal, air_now, air_prev, ylo, yhi)
    came = lax.all_to_all(sent, "gy", 0, 0).reshape(256, width)

    lo = jnp.concatenate([plate_now[-4:], plate_prev[-4:]], axis=0)
    hi = jnp.concatenate([plate_now[:4], plate_prev[:4]], axis=0)
    lo = lax.ppermute(lo, ("gz", "gy"), up_d)
    hi = lax.ppermute(hi, ("gz", "gy"), down_d)
    plate_ext, motion = plate_first(scal, plate_now, plate_prev, lo, hi, n_rows)

    zlo = lax.ppermute(air_now[depth - 1], "gz", up_z)
    zhi = lax.ppermute(air_now[0], "gz", down_z)
    air_1, first_rows, last_rows = air_step(air_now, air_prev, zlo, zhi, ylo, yhi, True)
    press_now = local_press(scal, air_now, zlo, zhi)
    ylo = lax.ppermute(last_rows, "gy", up_y)
    yhi = lax.ppermute(first_rows, "gy", down_y)
    zlo = lax.ppermute(air_1[depth - 1], "gz", up_z)
    zhi = lax.ppermute(air_1[0], "gz", down_z)
    (air_2,) = air_step(air_1, air_now, zlo, zhi, ylo, yhi, False)

    came = lax.all_to_all(to_plate(scal, came, motion), "gz", 0, 0)
    pressure, sent = to_air(scal, came)
    came = lax.all_to_all(sent, "gy", 0, 0)

    lo = lax.ppermute(pressure[3:4], ("gz", "gy"), up_d)
    hi = lax.ppermute(pressure[0:1], ("gz", "gy"), down_d)
    plate_2 = plate_last(scal, plate_now, plate_ext, pressure, motion, lo, hi, n_rows)
    air_2 = add_force(scal, air_2, came, press_now)
    return (air_2, plate_2)


def solution(mesh):
    in_specs = (
        P("gz", "gy", None),
        P("gz", "gy", None),
        P(("gz", "gy"), None),
        P(("gz", "gy"), None),
        P(),
        P(),
    )
    out_specs = (P("gz", "gy", None), P(("gz", "gy"), None))
    return jax.shard_map(shards, mesh=mesh, in_specs=in_specs, out_specs=out_specs, check_vma=False)
```

time: 973 us -> 126 us (0.13)
  waiting for transfers between devices: 827 us -> 12 us
  other arithmetic: 50.1 us -> 0.06 us
  starting transfers between devices: 40.8 us -> 72.3 us
  Pallas kernels: 0 us -> 24 us
  local copies, waits for them, and re-layouts: 35.4 us -> 14.6 us
  between operations: 15.5 us -> 2.23 us
    all_gather x4 -> x0, waiting for transfers between devices: 676 us -> none  [the longest x2 547 us: shards(): everyone = lax.all_gather(motion, ('gz', 'gy'), axis=0, tiled=True)]
    psum x1 -> x0, waiting for transfers between devices: 121 us -> none  [shards(): column = lax.psum(contrib, 'gz')]
    add x2 -> x0, other arithmetic: 29.7 us -> none  [shards(): air_next = air_next + 0.5 * source[None] * select[:, None, None]]
    pallas_call x0 -> x9, Pallas kernels: none -> 24 us  [the longest x2 10.5 us: air_step(): pl.pallas_call(air_kernel, grid=(depth,), in_specs=[pl.BlockSpec((depth,...]
    ppermute x12, waiting for transfers between devices: 29.1 us -> 6.28 us  [the longest x1 6.25 us: shards(): lo = lax.ppermute(lo, ('gz', 'gy'), up_d)]
    reshape x2 -> x0, local copies, waits for them, and re-layouts: 21.4 us -> none  [shards(): (plate_now - plate_prev).reshape(foot, 4, width, 4).mean(axis=(1, 3))]
    all_to_all x0 -> x3, starting transfers between devices: none -> 18.9 us  [the longest x1 6.78 us: shards(): came = lax.all_to_all(sent, 'gy', 0, 0).reshape(256, width)]
    ppermute x12, starting transfers between devices: 40.6 us -> 53.4 us  [the longest x1 7.8 us: shards(): hi = lax.ppermute(pressure[0:1], ('gz', 'gy'), down_d)]
  transfers between devices with their start and end apart: 17 -> 15, of which waited for: 10 -> 2; matrix products, arithmetic and copies ran while one was open for 1% -> 3% of each run, Pallas kernels for 0% -> 14%
where the time goes in v1:
time: 126 us; the launch traced here: 125 us
  starting transfers between devices  72.3 us (57%)
  Pallas kernels  24 us (19%)
  local copies, waits for them, and re-layouts  14.6 us (12%)
  waiting for transfers between devices  12 us (10%)
  between operations  2.23 us (2%)
    pallas_call x2, Pallas kernels, air_step(): pl.pallas_call(air_kernel, grid=(depth,), in_specs=[pl.BlockSpec((depth,...  10.5 us
    unnamed x26, local copies, waits for them, and re-layouts  9.86 us
    ppermute x1, starting transfers between devices, shards(): hi = lax.ppermute(pressure[0:1], ('gz', 'gy'), down_d)  7.8 us
    all_to_all x1, starting transfers between devices, shards(): came = lax.all_to_all(sent, 'gy', 0, 0).reshape(256, width)  6.78 us
    ppermute x1, waiting for transfers between devices, shards(): lo = lax.ppermute(lo, ('gz', 'gy'), up_d)  6.25 us
    all_to_all x1, starting transfers between devices, shards(): came = lax.all_to_all(sent, 'gy', 0, 0)  6.15 us
    ppermute x1, starting transfers between devices, shards(): hi = lax.ppermute(hi, ('gz', 'gy'), down_d)  6.08 us
    ppermute x1, starting transfers between devices, shards(): yhi = lax.ppermute(first_rows, 'gy', down_y)  6.08 us
  transfers between devices with their start and end apart: 15, of which 2 were waited for; matrix products, arithmetic and copies ran while one was open for 3% of the time, Pallas kernels for 14%

profile of v1, /device:TPU:6, one launch (start us, length us, event | category | flops | bytes accessed | tf_op | source)
XLA Modules:
  0.0 125.2 jit_solution(862611214153858491)
XLA Ops:
  0.6 1.1 fusion
  1.7 3.8 %collective-permute-start.2 = (f32[8,1024]{1,0:T(8,128)S(1)}, f32[8,1024]{1,0:T(8,128)S(1)}, u32[]{:S(2)}, u32[]{:S(2)}) collective-permute-start(f32[8,1024]{1,0:T(8,128)S(1)} %bitcast.19), channel_id=1, source_target_pairs={{0,1},{1,2},{2,3},{3,4},{4,5},{5,6},{6,7},{8,9},{9,10},{10,11},{11... | collective-permute-start | bytes 98312 | tf_op jit(solution)/shard_map/ppermute | solution.py:435
  5.6 5.6 %collective-permute-start.3 = (f32[8,1024]{1,0:T(8,128)S(1)}, f32[8,1024]{1,0:T(8,128)S(1)}, u32[]{:S(2)}, u32[]{:S(2)}) collective-permute-start(f32[8,1024]{1,0:T(8,128)S(1)} %bitcast.20), channel_id=1, source_target_pairs={{1,0},{2,1},{3,2},{4,3},{5,4},{6,5},{7,6},{9,8},{10,9},{11,10},{12... | collective-permute-start | bytes 98312 | tf_op jit(solution)/shard_map/ppermute | solution.py:436
  11.2 1.1 fusion.1
  13.7 0.1 stack.15.scal
  13.8 0.0 collective-permute-done.2.ylo
  13.8 0.0 collective-permute-done.3.yhi
  13.8 0.0 copy-start
  13.8 2.2 %copy-done = f32[8,128,1024]{2,1,0:T(8,128)S(1)} copy-done((f32[8,128,1024]{2,1,0:T(8,128)S(1)}, f32[8,128,1024]{2,1,0:T(8,128)}, u32[]{:S(2)}) %copy-start) | copy-done | bytes 4194328
  16.0 0.0 copy-start.3
  16.0 2.2 %copy-done.3 = f32[8,128,1024]{2,1,0:T(8,128)S(1)} copy-done((f32[8,128,1024]{2,1,0:T(8,128)S(1)}, f32[8,128,1024]{2,1,0:T(8,128)}, u32[]{:S(2)}) %copy-start.3) | copy-done | bytes 4194328
  18.2 0.0 copy-start.5
  18.2 1.6 %shard_map.79 = f32[8,32,1024]{2,1,0:T(8,128)} custom-call(s32[8]{0:T(128)S(1)} %stack.15.scal, f32[8,128,1024]{2,1,0:T(8,128)S(1)} %copy-done, f32[8,128,1024]{2,1,0:T(8,128)S(1)} %copy-done, f32[8,128,1024]{2,1,0:T(8,128)S(1)} %copy-done, f32[8,128,1024]{2,1,0:T(8,128)S(1)} %copy-done, f32[8,128,1024]{2,1,0:T(8,128)S(1)} %copy-done.3, ...), custom_call_target="tpu_custom_call" | custom-call | flops 4194304 | bytes 4194304 | tf_op jit(solution)/shard_map/pallas_call | solution.py:136
  19.8 6.8 %all-to-all-start = ((f32[8,32,1024]{2,1,0:T(8,128)}), f32[8,32,1024]{2,1,0:T(8,128)S(1)}, u32[]{:S(2)}, u32[]{:S(2)}) async-start(f32[8,32,1024]{2,1,0:T(8,128)} %shard_map.79), calls=%async_computation | async-start | bytes 2097152 | tf_op jit(solution)/shard_map/all_to_all | solution.py:438
  26.6 3.4 %collective-permute-start.8 = (f32[8,4096]{1,0:T(8,128)S(1)}, f32[8,4096]{1,0:T(8,128)S(1)}, u32[]{:S(2)}, u32[]{:S(2)}) collective-permute-start(f32[8,4096]{1,0:T(8,128)S(1)} %pad_maximum_fusion), channel_id=1, source_target_pairs={{0,1},{1,2},{2,3},{3,4},{4,5},{5,6},{6,7},{7,8},{8,9},{9,10},{10,1... | collective-permute-start | bytes 393224 | tf_op jit(solution)/shard_map/ppermute | solution.py:442
  30.0 6.1 %collective-permute-start.9 = (f32[8,4096]{1,0:T(8,128)S(1)}, f32[8,4096]{1,0:T(8,128)S(1)}, u32[]{:S(2)}, u32[]{:S(2)}) collective-permute-start(f32[8,4096]{1,0:T(8,128)S(1)} %pad_maximum_fusion.1), channel_id=1, source_target_pairs={{1,0},{2,1},{3,2},{4,3},{5,4},{6,5},{7,6},{8,7},{9,8},{10,9},{11,1... | collective-permute-start | bytes 393224 | tf_op jit(solution)/shard_map/ppermute | solution.py:443
  36.1 6.3 %collective-permute-done.8.lo = f32[8,4096]{1,0:T(8,128)S(1)} collective-permute-done((f32[8,4096]{1,0:T(8,128)S(1)}, f32[8,4096]{1,0:T(8,128)S(1)}, u32[]{:S(2)}, u32[]{:S(2)}) %collective-permute-start.8) | collective-permute-done | bytes 131104 | tf_op jit(solution)/shard_map/ppermute | solution.py:442
  42.3 0.0 collective-permute-done.9.hi
  42.3 0.0 copy-done.5
  42.3 0.0 copy-done.7
  42.3 2.5 %shard_map.80 = (f32[24,4096]{1,0:T(8,128)S(1)}, f32[8,1024]{1,0:T(8,128)S(1)}) custom-call(s32[8]{0:T(128)S(1)} %stack.15.scal, f32[16,4096]{1,0:T(8,128)S(1)} %copy-done.5, f32[16,4096]{1,0:T(8,128)S(1)} %copy-done.7, f32[8,4096]{1,0:T(8,128)S(1)} %collective-permute-done.8.lo, f32[8,4096]{1,0:T(8,128)S(1)} %collective-permute-done.9.hi), custom_call_target="tpu_custom_call" | custom-call | flops 4194304 | bytes 4194304 | tf_op jit(solution)/shard_map/pallas_call | solution.py:186
  44.8 0.0 all-to-all-done
  44.8 1.6 %shard_map.81 = f32[16,16,1024]{2,1,0:T(8,128)} custom-call(s32[8]{0:T(128)S(1)} %stack.15.scal, f32[256,1024]{1,0:T(8,128)S(1)} %bitcast.18, f32[8,1024]{1,0:T(8,128)S(1)} %get-tuple-element.12.motion), custom_call_target="tpu_custom_call" | custom-call | flops 2097152 | bytes 2097152 | tf_op jit(solution)/shard_map/pallas_call | solution.py:218
  46.4 5.9 %all-to-all-start.1 = ((f32[16,16,1024]{2,1,0:T(8,128)}), f32[16,16,1024]{2,1,0:T(8,128)S(1)}, u32[]{:S(2)}, u32[]{:S(2)}) async-start(f32[16,16,1024]{2,1,0:T(8,128)} %shard_map.81), calls=%async_computation.1 | async-start | bytes 2097152 | tf_op jit(solution)/shard_map/all_to_all | solution.py:456
  52.4 2.3 %slice_bitcast_fusion.2 = (f32[128,1024]{1,0:T(8,128)}, f32[128,1024]{1,0:T(8,128)}) fusion(f32[8,128,1024]{2,1,0:T(8,128)} %at0.3), kind=kLoop, calls=%fused_computation.2 | loop fusion | bytes 2097152 | tf_op jit(solution)/shard_map/squeeze | solution.py:447
  54.7 2.0 %collective-permute-start = (f32[128,1024]{1,0:T(8,128)}, f32[128,1024]{1,0:T(8,128)S(1)}, u32[]{:S(2)}, u32[]{:S(2)}) collective-permute-start(f32[128,1024]{1,0:T(8,128)} %get-tuple-element.21), channel_id=1, source_target_pairs={{0,8},{8,16},{16,24},{24,32},{32,40},{40,48},{48,56},{56,64},{64,7... | collective-permute-start | bytes 1572872 | tf_op jit(solution)/shard_map/ppermute | solution.py:446
  56.7 5.6 %collective-permute-start.1 = (f32[128,1024]{1,0:T(8,128)}, f32[128,1024]{1,0:T(8,128)S(1)}, u32[]{:S(2)}, u32[]{:S(2)}) collective-permute-start(f32[128,1024]{1,0:T(8,128)} %get-tuple-element.20), channel_id=1, source_target_pairs={{8,0},{16,8},{24,16},{32,24},{40,32},{48,40},{56,48},{64,56},{72,6... | collective-permute-start | bytes 1572872 | tf_op jit(solution)/shard_map/ppermute | solution.py:447
  62.4 5.7 %all-to-all-done.1.came = f32[16,16,1024]{2,1,0:T(8,128)S(1)} async-done(((f32[16,16,1024]{2,1,0:T(8,128)}), f32[16,16,1024]{2,1,0:T(8,128)S(1)}, u32[]{:S(2)}, u32[]{:S(2)}) %all-to-all-start.1) | async-done | bytes 1048608 | tf_op jit(solution)/shard_map/all_to_all | solution.py:456
  68.1 0.7 shard_map.82
  68.8 0.0 copy-start.6
  68.8 1.1 copy-done.6
  69.9 0.0 copy-done.8
  69.9 6.1 %all-to-all-start.2 = ((f32[8,40,1024]{2,1,0:T(8,128)}), f32[8,40,1024]{2,1,0:T(8,128)S(1)}, u32[]{:S(2)}, u32[]{:S(2)}) async-start(f32[8,40,1024]{2,1,0:T(8,128)} %copy-done.6), calls=%async_computation.2 | async-start | bytes 2621440 | tf_op jit(solution)/shard_map/all_to_all | solution.py:458
  76.0 0.0 collective-permute-done.zlo
  76.0 0.0 collective-permute-done.1.zhi
  76.0 0.0 copy-start.1
  76.0 2.2 %copy-done.1 = f32[8,128,1024]{2,1,0:T(8,128)S(1)} copy-done((f32[8,128,1024]{2,1,0:T(8,128)S(1)}, f32[8,128,1024]{2,1,0:T(8,128)}, u32[]{:S(2)}) %copy-start.1) | copy-done | bytes 4194328
  78.2 2.2 %copy-done.4 = f32[8,128,1024]{2,1,0:T(8,128)S(1)} copy-done((f32[8,128,1024]{2,1,0:T(8,128)S(1)}, f32[8,128,1024]{2,1,0:T(8,128)}, u32[]{:S(2)}) %copy-start.4) | copy-done | bytes 4194328
  80.4 4.5 %shard_map.77 = (f32[8,128,1024]{2,1,0:T(8,128)S(1)}, f32[8,1024]{1,0:T(8,128)S(1)}, f32[8,1024]{1,0:T(8,128)S(1)}) custom-call(f32[8,128,1024]{2,1,0:T(8,128)S(1)} %copy-done.1, f32[8,128,1024]{2,1,0:T(8,128)S(1)} %copy-done.4, f32[128,1024]{1,0:T(8,128)S(1)} %collective-permute-done.zlo, f32[128,1024]{1,0:T(8,128)S(1)} %collective-permute-done.1.zhi, ...), custom_call_target="tpu_custom_call" | custom-call | flops 14680064 | bytes 14680064 | tf_op jit(solution)/shard_map/pallas_call | solution.py:69
  84.9 0.1 slice_bitcast_fusion
  85.0 1.9 %collective-permute-start.4 = (f32[128,1024]{1,0:T(8,128)S(1)}, f32[128,1024]{1,0:T(8,128)S(1)}, u32[]{:S(2)}, u32[]{:S(2)}) collective-permute-start(f32[128,1024]{1,0:T(8,128)S(1)} %get-tuple-element.17), channel_id=1, source_target_pairs={{0,8},{8,16},{16,24},{24,32},{32,40},{40,48},{48,56},{56,64},{64,7... | collective-permute-start | bytes 1572872 | tf_op jit(solution)/shard_map/ppermute | solution.py:452
  86.9 5.8 %collective-permute-start.5 = (f32[128,1024]{1,0:T(8,128)S(1)}, f32[128,1024]{1,0:T(8,128)S(1)}, u32[]{:S(2)}, u32[]{:S(2)}) collective-permute-start(f32[128,1024]{1,0:T(8,128)S(1)} %get-tuple-element.16), channel_id=1, source_target_pairs={{8,0},{16,8},{24,16},{32,24},{40,32},{48,40},{56,48},{64,56},{72,6... | collective-permute-start | bytes 1572872 | tf_op jit(solution)/shard_map/ppermute | solution.py:453
  92.7 3.4 %collective-permute-start.6 = (f32[8,1024]{1,0:T(8,128)S(1)}, f32[8,1024]{1,0:T(8,128)S(1)}, u32[]{:S(2)}, u32[]{:S(2)}) collective-permute-start(f32[8,1024]{1,0:T(8,128)S(1)} %get-tuple-element.10), channel_id=1, source_target_pairs={{0,1},{1,2},{2,3},{3,4},{4,5},{5,6},{6,7},{8,9},{9,10},{10,11},{11... | collective-permute-start | bytes 98312 | tf_op jit(solution)/shard_map/ppermute | solution.py:450
  96.1 6.1 %collective-permute-start.7 = (f32[8,1024]{1,0:T(8,128)S(1)}, f32[8,1024]{1,0:T(8,128)S(1)}, u32[]{:S(2)}, u32[]{:S(2)}) collective-permute-start(f32[8,1024]{1,0:T(8,128)S(1)} %get-tuple-element.11), channel_id=1, source_target_pairs={{1,0},{2,1},{3,2},{4,3},{5,4},{6,5},{7,6},{9,8},{10,9},{11,10},{12... | collective-permute-start | bytes 98312 | tf_op jit(solution)/shard_map/ppermute | solution.py:451
  102.1 0.0 copy-done.10
  102.2 1.9 %collective-permute-start.10 = (f32[1,1024]{1,0:T(1,128)S(1)}, f32[1,1024]{1,0:T(1,128)S(1)}, u32[]{:S(2)}, u32[]{:S(2)}) collective-permute-start(f32[1,1024]{1,0:T(1,128)S(1)} %get-tuple-element.27), channel_id=1, source_target_pairs={{0,1},{1,2},{2,3},{3,4},{4,5},{5,6},{6,7},{7,8},{8,9},{9,10},{10,1... | collective-permute-start | bytes 12296 | tf_op jit(solution)/shard_map/ppermute | solution.py:460
  104.1 0.0 collective-permute-done.6.ylo
  104.1 0.0 copy-start.2
  104.1 7.8 %collective-permute-start.11 = (f32[1,1024]{1,0:T(1,128)S(1)}, f32[1,1024]{1,0:T(1,128)S(1)}, u32[]{:S(2)}, u32[]{:S(2)}) collective-permute-start(f32[1,1024]{1,0:T(1,128)S(1)} %get-tuple-element.26), channel_id=1, source_target_pairs={{1,0},{2,1},{3,2},{4,3},{5,4},{6,5},{7,6},{8,7},{9,8},{10,9},{11,1... | collective-permute-start | bytes 12296 | tf_op jit(solution)/shard_map/ppermute | solution.py:461
  111.9 0.7 shard_map.83.press
  112.6 0.0 copy-start.9
  112.6 0.0 copy-start.11
  112.6 0.0 collective-permute-done.7.yhi
  112.6 0.0 collective-permute-done.4.zlo
  112.6 0.0 collective-permute-done.5.zhi
  112.6 0.0 copy-done.2
  112.6 6.0 %shard_map.78.field = f32[8,128,1024]{2,1,0:T(8,128)} custom-call(f32[8,128,1024]{2,1,0:T(8,128)S(1)} %get-tuple-element.9.now, f32[8,128,1024]{2,1,0:T(8,128)S(1)} %copy-done.2, f32[128,1024]{1,0:T(8,128)S(1)} %collective-permute-done.4.zlo, f32[128,1024]{1,0:T(8,128)S(1)} %collective-permute-done.5.zhi, f32[8,1024]{1,0:T(8,128)S(1)} %collective-permute-done.6.ylo, ...), custom_call_target="tpu_custom_call" | custom-call | flops 14680064 | bytes 14680064 | tf_op jit(solution)/shard_map/pallas_call | solution.py:69
  118.7 0.0 collective-permute-done.10.lo
  118.7 0.0 collective-permute-done.11.hi
  118.7 0.0 copy-done.9
  118.7 0.0 copy-done.11
  118.7 3.1 %shard_map.85 = f32[16,4096]{1,0:T(8,128)} custom-call(s32[8]{0:T(128)S(1)} %stack.15.scal, f32[16,4096]{1,0:T(8,128)S(1)} %copy-done.5, f32[24,4096]{1,0:T(8,128)S(1)} %get-tuple-element.14.next_ext, f32[8,1024]{1,0:T(8,128)S(1)} %copy-done.11, f32[8,1024]{1,0:T(8,128)S(1)} %copy-done.9, f32[1,1024]{1,0:T(1,128)S(1)} %collective-permute-done.10.lo, ...), custom_call_target="tpu_custom_call" | custom-call | flops 4194304 | bytes 4194304 | tf_op jit(solution)/shard_map/pallas_call | solution.py:406
  121.8 0.0 all-to-all-done.2.came
  121.8 3.4 %shard_map.84 = f32[8,128,1024]{2,1,0:T(8,128)} custom-call(s32[8]{0:T(128)S(1)} %stack.15.scal, f32[8,128,1024]{2,1,0:T(8,128)} %shard_map.78.field, f32[8,40,1024]{2,1,0:T(8,128)S(1)} %all-to-all-done.2.came, f32[128,1024]{1,0:T(8,128)S(1)} %shard_map.83.press), custom_call_target="tpu_custom_call", output_to_operand_aliasing={{}: (1, {})} | custom-call | flops 4194304 | bytes 4194304 | tf_op jit(solution)/shard_map/pallas_call | solution.py:356
  (10 shorter events, 0.1 us)
Async XLA Ops:
  1.7 12.0 %collective-permute-start.2 = (f32[8,1024]{1,0:T(8,128)S(1)}, f32[8,1024]{1,0:T(8,128)S(1)}, u32[]{:S(2)}, u32[]{:S(2)}) collective-permute-start(f32[8,1024]{1,0:T(8,128)S(1)} %bitcast.19), channel_id=1, source_target_pairs={{0,1},{1,2},{2,3},{3,4},{4,5},{5,6},{6,7},{8,9},{9,10},{10,11},{11... | collective-permute-start | bytes 98312 | tf_op jit(solution)/shard_map/ppermute | solution.py:435
  5.6 8.2 %collective-permute-start.3 = (f32[8,1024]{1,0:T(8,128)S(1)}, f32[8,1024]{1,0:T(8,128)S(1)}, u32[]{:S(2)}, u32[]{:S(2)}) collective-permute-start(f32[8,1024]{1,0:T(8,128)S(1)} %bitcast.20), channel_id=1, source_target_pairs={{1,0},{2,1},{3,2},{4,3},{5,4},{6,5},{7,6},{9,8},{10,9},{11,10},{12... | collective-permute-start | bytes 98312 | tf_op jit(solution)/shard_map/ppermute | solution.py:436
  13.8 2.2 %copy-start = (f32[8,128,1024]{2,1,0:T(8,128)S(1)}, f32[8,128,1024]{2,1,0:T(8,128)}, u32[]{:S(2)}) copy-start(f32[8,128,1024]{2,1,0:T(8,128)} %at0.3) | copy-start | bytes 12582916
  16.0 2.2 %copy-start.3 = (f32[8,128,1024]{2,1,0:T(8,128)S(1)}, f32[8,128,1024]{2,1,0:T(8,128)}, u32[]{:S(2)}) copy-start(f32[8,128,1024]{2,1,0:T(8,128)} %pat0.1) | copy-start | bytes 12582916
  18.2 24.2 %copy-start.5 = (f32[16,4096]{1,0:T(8,128)S(1)}, f32[16,4096]{1,0:T(8,128)}, u32[]{:S(2)}) copy-start(f32[16,4096]{1,0:T(8,128)} %now.5) | copy-start | bytes 786436
  18.2 24.2 %copy-start.7 = (f32[16,4096]{1,0:T(8,128)S(1)}, f32[16,4096]{1,0:T(8,128)}, u32[]{:S(2)}) copy-start(f32[16,4096]{1,0:T(8,128)} %prev.5) | copy-start | bytes 786436
  19.8 25.1 %all-to-all-start = ((f32[8,32,1024]{2,1,0:T(8,128)}), f32[8,32,1024]{2,1,0:T(8,128)S(1)}, u32[]{:S(2)}, u32[]{:S(2)}) async-start(f32[8,32,1024]{2,1,0:T(8,128)} %shard_map.79), calls=%async_computation | async-start | bytes 2097152 | tf_op jit(solution)/shard_map/all_to_all | solution.py:438
  26.6 15.8 %collective-permute-start.8 = (f32[8,4096]{1,0:T(8,128)S(1)}, f32[8,4096]{1,0:T(8,128)S(1)}, u32[]{:S(2)}, u32[]{:S(2)}) collective-permute-start(f32[8,4096]{1,0:T(8,128)S(1)} %pad_maximum_fusion), channel_id=1, source_target_pairs={{0,1},{1,2},{2,3},{3,4},{4,5},{5,6},{6,7},{7,8},{8,9},{9,10},{10,1... | collective-permute-start | bytes 393224 | tf_op jit(solution)/shard_map/ppermute | solution.py:442
  30.0 12.3 %collective-permute-start.9 = (f32[8,4096]{1,0:T(8,128)S(1)}, f32[8,4096]{1,0:T(8,128)S(1)}, u32[]{:S(2)}, u32[]{:S(2)}) collective-permute-start(f32[8,4096]{1,0:T(8,128)S(1)} %pad_maximum_fusion.1), channel_id=1, source_target_pairs={{1,0},{2,1},{3,2},{4,3},{5,4},{6,5},{7,6},{8,7},{9,8},{10,9},{11,1... | collective-permute-start | bytes 393224 | tf_op jit(solution)/shard_map/ppermute | solution.py:443
  44.8 25.0 %copy-start.8 = (f32[8,1024]{1,0:T(8,128)}, f32[8,1024]{1,0:T(8,128)S(1)}, u32[]{:S(2)}) copy-start(f32[8,1024]{1,0:T(8,128)S(1)} %get-tuple-element.12.motion) | copy-start | bytes 98308
  46.4 21.7 %all-to-all-start.1 = ((f32[16,16,1024]{2,1,0:T(8,128)}), f32[16,16,1024]{2,1,0:T(8,128)S(1)}, u32[]{:S(2)}, u32[]{:S(2)}) async-start(f32[16,16,1024]{2,1,0:T(8,128)} %shard_map.81), calls=%async_computation.1 | async-start | bytes 2097152 | tf_op jit(solution)/shard_map/all_to_all | solution.py:456
  54.7 21.3 %collective-permute-start = (f32[128,1024]{1,0:T(8,128)}, f32[128,1024]{1,0:T(8,128)S(1)}, u32[]{:S(2)}, u32[]{:S(2)}) collective-permute-start(f32[128,1024]{1,0:T(8,128)} %get-tuple-element.21), channel_id=1, source_target_pairs={{0,8},{8,16},{16,24},{24,32},{32,40},{40,48},{48,56},{56,64},{64,7... | collective-permute-start | bytes 1572872 | tf_op jit(solution)/shard_map/ppermute | solution.py:446
  56.7 19.3 %collective-permute-start.1 = (f32[128,1024]{1,0:T(8,128)}, f32[128,1024]{1,0:T(8,128)S(1)}, u32[]{:S(2)}, u32[]{:S(2)}) collective-permute-start(f32[128,1024]{1,0:T(8,128)} %get-tuple-element.20), channel_id=1, source_target_pairs={{8,0},{16,8},{24,16},{32,24},{40,32},{48,40},{56,48},{64,56},{72,6... | collective-permute-start | bytes 1572872 | tf_op jit(solution)/shard_map/ppermute | solution.py:447
  68.8 1.1 copy-start.6
  69.9 32.3 %copy-start.10 = (f32[8,1024]{1,0:T(8,128)}, f32[8,1024]{1,0:T(8,128)S(1)}, u32[]{:S(2)}) copy-start(f32[8,1024]{1,0:T(8,128)S(1)} %get-tuple-element.15.pressure) | copy-start | bytes 98308
  69.9 51.9 %all-to-all-start.2 = ((f32[8,40,1024]{2,1,0:T(8,128)}), f32[8,40,1024]{2,1,0:T(8,128)S(1)}, u32[]{:S(2)}, u32[]{:S(2)}) async-start(f32[8,40,1024]{2,1,0:T(8,128)} %copy-done.6), calls=%async_computation.2 | async-start | bytes 2621440 | tf_op jit(solution)/shard_map/all_to_all | solution.py:458
  76.0 2.2 %copy-start.1 = (f32[8,128,1024]{2,1,0:T(8,128)S(1)}, f32[8,128,1024]{2,1,0:T(8,128)}, u32[]{:S(2)}) copy-start(f32[8,128,1024]{2,1,0:T(8,128)} %at0.3) | copy-start | bytes 12582916
  78.2 2.2 %copy-start.4 = (f32[8,128,1024]{2,1,0:T(8,128)S(1)}, f32[8,128,1024]{2,1,0:T(8,128)}, u32[]{:S(2)}) copy-start(f32[8,128,1024]{2,1,0:T(8,128)} %pat0.1) | copy-start | bytes 12582916
  85.0 27.6 %collective-permute-start.4 = (f32[128,1024]{1,0:T(8,128)S(1)}, f32[128,1024]{1,0:T(8,128)S(1)}, u32[]{:S(2)}, u32[]{:S(2)}) collective-permute-start(f32[128,1024]{1,0:T(8,128)S(1)} %get-tuple-element.17), channel_id=1, source_target_pairs={{0,8},{8,16},{16,24},{24,32},{32,40},{40,48},{48,56},{56,64},{64,7... | collective-permute-start | bytes 1572872 | tf_op jit(solution)/shard_map/ppermute | solution.py:452
  86.9 25.7 %collective-permute-start.5 = (f32[128,1024]{1,0:T(8,128)S(1)}, f32[128,1024]{1,0:T(8,128)S(1)}, u32[]{:S(2)}, u32[]{:S(2)}) collective-permute-start(f32[128,1024]{1,0:T(8,128)S(1)} %get-tuple-element.16), channel_id=1, source_target_pairs={{8,0},{16,8},{24,16},{32,24},{40,32},{48,40},{56,48},{64,56},{72,6... | collective-permute-start | bytes 1572872 | tf_op jit(solution)/shard_map/ppermute | solution.py:453
  92.7 11.4 %collective-permute-start.6 = (f32[8,1024]{1,0:T(8,128)S(1)}, f32[8,1024]{1,0:T(8,128)S(1)}, u32[]{:S(2)}, u32[]{:S(2)}) collective-permute-start(f32[8,1024]{1,0:T(8,128)S(1)} %get-tuple-element.10), channel_id=1, source_target_pairs={{0,1},{1,2},{2,3},{3,4},{4,5},{5,6},{6,7},{8,9},{9,10},{10,11},{11... | collective-permute-start | bytes 98312 | tf_op jit(solution)/shard_map/ppermute | solution.py:450
  96.1 16.6 %collective-permute-start.7 = (f32[8,1024]{1,0:T(8,128)S(1)}, f32[8,1024]{1,0:T(8,128)S(1)}, u32[]{:S(2)}, u32[]{:S(2)}) collective-permute-start(f32[8,1024]{1,0:T(8,128)S(1)} %get-tuple-element.11), channel_id=1, source_target_pairs={{1,0},{2,1},{3,2},{4,3},{5,4},{6,5},{7,6},{9,8},{10,9},{11,10},{12... | collective-permute-start | bytes 98312 | tf_op jit(solution)/shard_map/ppermute | solution.py:451
  102.2 16.5 %collective-permute-start.10 = (f32[1,1024]{1,0:T(1,128)S(1)}, f32[1,1024]{1,0:T(1,128)S(1)}, u32[]{:S(2)}, u32[]{:S(2)}) collective-permute-start(f32[1,1024]{1,0:T(1,128)S(1)} %get-tuple-element.27), channel_id=1, source_target_pairs={{0,1},{1,2},{2,3},{3,4},{4,5},{5,6},{6,7},{7,8},{8,9},{9,10},{10,1... | collective-permute-start | bytes 12296 | tf_op jit(solution)/shard_map/ppermute | solution.py:460
  104.1 8.5 %copy-start.2 = (f32[8,128,1024]{2,1,0:T(8,128)S(1)}, f32[8,128,1024]{2,1,0:T(8,128)}, u32[]{:S(2)}) copy-start(f32[8,128,1024]{2,1,0:T(8,128)} %at0.3) | copy-start | bytes 12582916
  104.1 14.6 %collective-permute-start.11 = (f32[1,1024]{1,0:T(1,128)S(1)}, f32[1,1024]{1,0:T(1,128)S(1)}, u32[]{:S(2)}, u32[]{:S(2)}) collective-permute-start(f32[1,1024]{1,0:T(1,128)S(1)} %get-tuple-element.26), channel_id=1, source_target_pairs={{1,0},{2,1},{3,2},{4,3},{5,4},{6,5},{7,6},{8,7},{9,8},{10,9},{11,1... | collective-permute-start | bytes 12296 | tf_op jit(solution)/shard_map/ppermute | solution.py:461
  112.6 6.1 %copy-start.9 = (f32[8,1024]{1,0:T(8,128)S(1)}, f32[8,1024]{1,0:T(8,128)}, u32[]{:S(2)}) copy-start(f32[8,1024]{1,0:T(8,128)} %copy-done.8) | copy-start | bytes 98308
  112.6 6.1 %copy-start.11 = (f32[8,1024]{1,0:T(8,128)S(1)}, f32[8,1024]{1,0:T(8,128)}, u32[]{:S(2)}) copy-start(f32[8,1024]{1,0:T(8,128)} %copy-done.10) | copy-start | bytes 98308

commit v2 on v1

v2 whole, which is shorter than its diff:
```python
import functools

import jax
import jax.numpy as jnp
from jax import lax
from jax.experimental import pallas as pl
from jax.experimental.pallas import tpu as pltpu
from jax.sharding import PartitionSpec as P

F32 = jnp.float32
C_PRESS = 0.5 / 1.01
HIGH = lax.Precision.HIGHEST


def params(mib):
    return pltpu.CompilerParams(vmem_limit_bytes=mib << 20)


class Place:
    def __init__(self, level, shift):
        self.level, self.shift = level, shift

    def __getitem__(self, i):
        if i == 0:
            return self.level[0]
        if i == 1:
            return self.shift[0]
        slab, strip = lax.axis_index("gz"), lax.axis_index("gy")
        return {2: slab * 8, 3: slab * lax.axis_size("gy") + strip, 4: strip, 5: slab}[i]


def placed(kernel):
    def run(level, shift, *refs):
        kernel(Place(level, shift), *refs)

    return run


def cost(nbytes):
    return pl.CostEstimate(flops=nbytes, bytes_accessed=nbytes, transcendentals=0)


def iota(shape, axis):
    return lax.broadcasted_iota(jnp.int32, shape, axis)


def left_right(x):
    width = x.shape[1]
    col = iota(x.shape, 1)
    west = jnp.where(col == 0, 0.0, pltpu.roll(x, 1, 1))
    east = jnp.where(col == width - 1, 0.0, pltpu.roll(x, width - 1, 1))
    return west + east


def up_down(x, above, below):
    height = x.shape[0]
    row = iota(x.shape, 0)
    up = jnp.where(row == 0, above, pltpu.roll(x, 1, 0))
    down = jnp.where(row == height - 1, below, pltpu.roll(x, height - 1, 0))
    return up + down


def sweep(load, count, above, below, emit):
    here = load(0)
    shape = here.shape
    width = shape[1]
    row, col = iota(shape, 0), iota(shape, 1)
    top, bottom, left, right = row == 0, row == 7, col == 0, col == width - 1
    from_above = above
    up, down = pltpu.roll(here, 1, 0), pltpu.roll(here, 7, 0)
    for i in range(count):
        if i + 1 < count:
            later = load(i + 1)
            later_up, later_down = pltpu.roll(later, 1, 0), pltpu.roll(later, 7, 0)
            from_below = later_down
        else:
            from_below = below
        west = jnp.where(left, 0.0, pltpu.roll(here, 1, 1))
        east = jnp.where(right, 0.0, pltpu.roll(here, width - 1, 1))
        vertical = jnp.where(top, from_above, up) + jnp.where(bottom, from_below, down)
        emit(i, here, west + east + vertical)
        if i + 1 < count:
            from_above = up
            here, up, down = later, later_up, later_down


def pack_kernel(now0, now1, old0, old1, plate_now, plate_prev, first, last):
    rows = plate_now.shape[0]
    cols = plate_now.shape[1]
    width = now0.shape[2]
    for out, now, old, edge, inner, r in (
        (first, now0, old0, 0, 1, 0),
        (last, now1, old1, 7, 6, rows - 4),
    ):
        here = now[:, edge, :]
        depth = here.shape[0]
        out[0:4, 0:cols] = plate_now[r : r + 4, :]
        out[4:8, 0:cols] = plate_prev[r : r + 4, :]
        out[:, cols : cols + width] = here
        around = left_right(here) + up_down(here, 0.0, 0.0) + now[:, inner, :]
        out[:, cols + width : cols + 2 * width] = 0.2 * here - old[:, edge, :] + 0.3 * around


def face_kernel(scal, here, inner, old, lo, hi, motion, on_chip, off_chip):
    height, width = here.shape[1], here.shape[2]
    strip = scal[4]
    lower_core = (scal[5] & 1) == 0

    def one(level, out):
        above = jnp.where(strip > 0, lo[pl.ds(level, 1), :], 0.0)
        below = jnp.where(strip < 7, hi[pl.ds(level, 1), :], 0.0)

        def emit(i, x, around):
            at = slice(8 * i, 8 * i + 8)
            out[at, :] = x
            part = 0.2 * x - old[0, at, :] + 0.3 * (around + inner[0, at, :])
            out[height + 8 * i : height + 8 * i + 8, :] = part

        sweep(lambda i: here[0, 8 * i : 8 * i + 8, :], height // 8, above, below, emit)
        row = iota((8, width), 0)
        ends = jnp.where(row == 0, above, jnp.where(row == 1, below, 0.0))
        out[2 * height : 2 * height + 8, :] = ends
        out[2 * height + 8 : 2 * height + 16, :] = motion[...]

    @pl.when(pl.program_id(0) == 0)
    def _():
        one(jnp.where(lower_core, 7, 0), on_chip)

    @pl.when(pl.program_id(0) == 1)
    def _():
        one(jnp.where(lower_core, 0, 7), off_chip)


def faces(scal, air_now, air_prev, lo, hi, motion, cols):
    depth, height, width = air_now.shape

    def plane(inner):
        def where(i, *scal):
            top = ((Place(*scal)[5] + i) & 1) == 0
            return (jnp.where(top, depth - 1 - inner, inner), 0, 0)

        return pl.BlockSpec((1, height, width), where)

    edge = pl.BlockSpec((8, width), lambda i, *scal: (0, cols // width))
    out = pl.BlockSpec((2 * height + 16, width), lambda i, *scal: (0, 0))
    return pl.pallas_call(
        placed(face_kernel),
        grid_spec=pltpu.PrefetchScalarGridSpec(
            num_scalar_prefetch=2,
            grid=(2,),
            in_specs=[
                plane(0),
                plane(1),
                plane(0),
                edge,
                edge,
                pl.BlockSpec((8, width), lambda i, *scal: (0, 0)),
            ],
            out_specs=[out, out],
        ),
        out_shape=[jax.ShapeDtypeStruct((2 * height + 16, width), F32)] * 2,
        compiler_params=params(59),
        cost_estimate=cost(5 << 20),
    )(*scal, air_now, air_now, air_prev, lo, hi, motion)


def air_kernel(scal, now, prev, on_chip, off_chip, ylo, yhi, out, press, keep, mid):
    level, shift, first, strip, slab = scal[0], scal[1], scal[2], scal[4], scal[5]
    t = pl.program_id(0)
    _, height, width = now.shape
    depth = 8
    strips = [slice(8 * i, 8 * i + 8) for i in range(height // 8)]
    y_lo = jnp.where(strip > 0, 1.0, 0.0).astype(F32)
    y_hi = jnp.where(strip < 7, 1.0, 0.0).astype(F32)
    lower_core = (slab & 1) == 0

    def zlo(first, count):
        at = slice(first, first + count)
        return jnp.where(lower_core, off_chip[at, :], on_chip[at, :])

    def zhi(first, count):
        at = slice(first, first + count)
        return jnp.where(lower_core, on_chip[at, :], off_chip[at, :])

    @pl.when(t == 0)
    def _():
        inside = jnp.where(slab > 0, 1.0, 0.0).astype(F32)
        for i, at in enumerate(strips):
            keep[0, at, :] = zlo(8 * i, 8)
            keep[depth + 1, at, :] = zhi(8 * i, 8)
            mid[0, at, :] = inside * (zlo(height + 8 * i, 8) + 0.3 * now[0, at, :])

    @pl.when(t == depth - 1)
    def _():
        inside = jnp.where(slab < 15, 1.0, 0.0).astype(F32)
        for i, at in enumerate(strips):
            mid[depth + 1, at, :] = inside * (zhi(height + 8 * i, 8) + 0.3 * now[0, at, :])

    @pl.when(t < depth)
    def _():
        for at in strips:
            keep[t + 1, at, :] = now[0, at, :]

    @pl.when((t >= 1) & (t <= depth))
    def _():
        z = t - 1
        above = y_lo * ylo[pl.ds(z, 1), 0:width]
        below = y_hi * yhi[pl.ds(z, 1), 0:width]

        def emit(i, x, around):
            at = strips[i]
            total = around + keep[z, at, :] + keep[z + 2, at, :]
            mid[z + 1, at, :] = 0.2 * x - prev[0, at, :] + 0.3 * total

        sweep(lambda i: keep[z + 1, strips[i], :], len(strips), above, below, emit)

    @pl.when(t >= 2)
    def _():
        z = t - 2
        at_bottom = jnp.where(z == 0, 0.3, 0.0).astype(F32)
        at_top = jnp.where(z == depth - 1, 0.3, 0.0).astype(F32)

        def rim(rows, line, r):
            row = rows[pl.ds(z, 1), width : 2 * width] + 0.3 * line
            return row + at_bottom * zlo(r, 1) + at_top * zhi(r, 1)

        above = y_lo * rim(ylo, keep[z + 1, 0:1, :], 2 * height)
        below = y_hi * rim(yhi, keep[z + 1, height - 1 : height, :], 2 * height + 1)

        def emit(i, x, around):
            at = strips[i]
            total = around + mid[z, at, :] + mid[z + 2, at, :]
            out[0, at, :] = 0.2 * x - keep[z + 1, at, :] + 0.3 * total

        sweep(lambda i: mid[z + 1, strips[i], :], len(strips), above, below, emit)

    @pl.when(t == depth)
    def _():
        upper = jnp.clip(level + 1 - first, -1, depth) + 1
        lower = jnp.clip(level - first, -1, depth) + 1
        for i, at in enumerate(strips):
            y = iota((8, width), 0) + (strip * height + 8 * i - shift)
            gap = keep[upper, at, :] - keep[lower, at, :]
            press[at, :] = jnp.where((y >= 0) & (y < 512), (0.5 * C_PRESS) * gap, 0.0)


def air_steps(scal, now, prev, on_chip, off_chip, ylo, yhi, cols):
    depth, height, width = now.shape

    def plane(lag):
        return pl.BlockSpec(
            (1, height, width), lambda t, *scal: (jnp.clip(t - lag, 0, depth - 1), 0, 0)
        )

    z_face = pl.BlockSpec((2 * height + 16, width), lambda t, *scal: (0, 0))
    rows = pl.BlockSpec((8, 2 * width), lambda t, *scal: (0, cols // (2 * width)))
    return pl.pallas_call(
        placed(air_kernel),
        grid_spec=pltpu.PrefetchScalarGridSpec(
            num_scalar_prefetch=2,
            grid=(depth + 2,),
            in_specs=[plane(0), plane(1), z_face, z_face, rows, rows],
            out_specs=[
                plane(2),
                pl.BlockSpec((height, width), lambda t, *scal: (0, 0)),
            ],
            scratch_shapes=[pltpu.VMEM((depth + 2, height, width), F32)] * 2,
        ),
        out_shape=[
            jax.ShapeDtypeStruct(now.shape, F32),
            jax.ShapeDtypeStruct((height, width), F32),
        ],
        compiler_params=params(59),
        cost_estimate=cost(24 << 20),
    )(*scal, now, prev, on_chip, off_chip, ylo, yhi)


def fold_row(row):
    return jnp.concatenate([row[:, 128 * q : 128 * q + 128] for q in range(8)], axis=0)


def press_kernel(scal, up2, up1, at0, dn1, pup1, pat0, out):
    level, shift, base = scal[0], scal[1], scal[2]
    depth = 8
    width = up1.shape[2]

    def mine(z):
        return jnp.where((z >= base) & (z < base + depth), 1.0, 0.0).astype(F32)

    here = (level + 2 >= base) & (level - 1 < base + depth)

    @pl.when(jnp.logical_not(here))
    def _():
        out[...] = jnp.zeros(out.shape, F32)

    @pl.when(here)
    def _():
        m1, m0 = mine(level + 1), mine(level)
        m2, mm = mine(level + 2), mine(level - 1)
        b = shift & 31
        turn = (32 - b) & 31
        for k in range(up1.shape[1] // 32):
            at = slice(32 * k, 32 * k + 32)
            press = m1 * up1[0, at, :] - m0 * at0[0, at, :]
            vertical = m2 * up2[0, at, :] - 3.0 * press - mm * dn1[0, at, :]
            older = m1 * pup1[0, at, :] - m0 * pat0[0, at, :]
            r0 = pltpu.roll(press, turn, 0)
            r1 = pltpu.roll(0.3 * vertical - older, turn, 0)
            folded = [fold_row(r0[i : i + 1]) for i in range(32) if i & 3 in (0, 3)]
            for y in range(8):
                tile = slice(8 * k, 8 * k + 8)
                out[y, 8 * k : 8 * k + 4, 0:width] = r0[4 * y : 4 * y + 4]
                out[y, 8 * k + 4 : 8 * k + 8, 0:width] = r1[4 * y : 4 * y + 4]
                out[y, tile, width : width + 128] = folded[(2 * y - 1) % 16]
                out[y, tile, width + 128 : width + 256] = folded[(2 * y + 2) % 16]


def front_kernel(scal, *refs):
    pack_kernel(*refs[0:6], *refs[12:14])
    press_kernel(scal, *refs[6:12], refs[14])


def front(scal, air_now, air_prev, plate_now, plate_prev):
    depth, height, width = air_now.shape
    rows, cols = plate_now.shape
    low = pl.BlockSpec((depth, 8, width), lambda i, *scal: (0, 0, 0))
    high = pl.BlockSpec((depth, 8, width), lambda i, *scal: (0, height // 8 - 1, 0))
    plate = pl.BlockSpec((rows, cols), lambda i, *scal: (0, 0))
    pack = pl.BlockSpec((8, cols + 2 * width), lambda i, *scal: (0, 0))

    def plane(offset):
        def where(k, *scal):
            scal = Place(*scal)
            return (jnp.clip(scal[0] + offset - scal[2], 0, depth - 1), 0, 0)

        return pl.BlockSpec((1, height, width), where)

    return pl.pallas_call(
        placed(front_kernel),
        grid_spec=pltpu.PrefetchScalarGridSpec(
            num_scalar_prefetch=2,
            grid=(1,),
            in_specs=[low, high, low, high, plate, plate]
            + [plane(2), plane(1), plane(0), plane(-1), plane(1), plane(0)],
            out_specs=[pack, pack, pl.BlockSpec((8, 32, width + 256), lambda k, *scal: (0, 0, 0))],
        ),
        out_shape=[jax.ShapeDtypeStruct((8, cols + 2 * width), F32)] * 2
        + [jax.ShapeDtypeStruct((8, 32, width + 256), F32)],
        compiler_params=params(59),
        cost_estimate=cost(6 << 20),
    )(
        *scal,
        *(air_now, air_now, air_prev, air_prev, plate_now, plate_prev),
        *(air_now, air_now, air_now, air_now, air_prev, air_prev),
    )


def flat_laplace(x):
    height = x.shape[0]
    return left_right(x) + pltpu.roll(x, 1, 0) + pltpu.roll(x, height - 1, 0) - 4.0 * x


def inside_rows(shape, first, last_row):
    row = iota(shape, 0) + first
    return (row >= 0) & (row < last_row)


def plate_kernel(n_rows, scal, now, prev, lo, hi, next_ext, motion):
    rows, cols = now.shape
    first = scal[3] * rows - 4
    here = now[...]
    ext = jnp.concatenate([lo[0:4, 0:cols], here, hi[0:4, 0:cols]], axis=0)
    old = jnp.concatenate([lo[4:8, 0:cols], prev[...], hi[4:8, 0:cols]], axis=0)
    ok = inside_rows(ext.shape, first, n_rows)
    inner = jnp.where(ok, flat_laplace(ext), 0.0)
    bend = flat_laplace(inner)
    nxt = (2.0 * ext - 0.99 * old - 0.04 * bend) * (1.0 / 1.01)
    nxt = jnp.where(ok, nxt, 0.0)
    next_ext[...] = nxt
    both = jnp.concatenate([here - prev[...], nxt[4 : 4 + rows] - here], axis=0)
    fold = jnp.where((iota((512, 128), 0) >> 2) == iota((512, 128), 1), 1.0, 0.0)
    parts = [
        jnp.dot(both[:, 512 * q : 512 * q + 512], fold, precision=HIGH, preferred_element_type=F32)
        for q in range(cols // 512)
    ]
    narrow = jnp.concatenate(parts, axis=1)
    pick = jnp.where(iota((8, 32), 0) == (iota((8, 32), 1) >> 2), 1.0 / 16.0, 0.0)
    motion[...] = jnp.dot(pick, narrow, precision=HIGH, preferred_element_type=F32)


def plate_first(scal, now, prev, lo, hi, n_rows):
    rows, cols = now.shape
    return pl.pallas_call(
        placed(functools.partial(plate_kernel, n_rows)),
        in_specs=[pl.BlockSpec(memory_space=pltpu.SMEM)] * 2
        + [pl.BlockSpec(memory_space=pltpu.VMEM)] * 4,
        out_specs=[pl.BlockSpec(memory_space=pltpu.VMEM)] * 2,
        out_shape=[
            jax.ShapeDtypeStruct((rows + 8, cols), F32),
            jax.ShapeDtypeStruct((8, cols // 4), F32),
        ],
        compiler_params=params(16),
        cost_estimate=cost(4 << 20),
    )(*scal, now, prev, lo, hi)


def carries(shape, strip, b):
    return (4 * strip + (iota(shape, 0) & 3) + b) >= 32


def to_plate_kernel(scal, came, motion, out):
    shift, strip = scal[1], scal[4]
    a, b = shift >> 5, shift & 31
    move = motion[...]
    width = move.shape[1]
    carry = carries(move.shape, strip, b)
    before = (4 * strip - 1 + b) >> 5
    behind = (4 * strip + 4 + b) >> 5

    def folded(block, lane):
        ok = jnp.where((block >= 0) & (block < 32), 1.0, 0.0).astype(F32)
        at = pl.multiple_of(8 * jnp.clip(block, 0, 31), 8)
        return came[pl.ds(at, 8), lane : lane + 128] * ok

    slab = scal[5]
    pair = jnp.clip((scal[0] - 1) >> 3, 0, 14)
    aside = (slab < pair) | (slab > pair + 1)
    for dest in range(16):
        at = pl.multiple_of(8 * (dest + a), 8)
        after = pl.multiple_of(8 * jnp.minimum(dest + a + 1, 31), 8)
        tile = jnp.where(carry, came[pl.ds(after, 8), 0:width], came[pl.ds(at, 8), 0:width])
        wants = aside & ((pair == dest) | (pair + 1 == dest))
        out[dest, :, 0:width] = jnp.where(wants, move, tile)
        out[dest, :, width : width + 128] = folded(dest + a + before, width)
        out[dest, :, width + 128 : width + 256] = folded(dest + a + behind, width + 128)


def to_plate(scal, came, motion):
    width = motion.shape[1]
    return pl.pallas_call(
        placed(to_plate_kernel),
        in_specs=[pl.BlockSpec(memory_space=pltpu.SMEM)] * 2
        + [pl.BlockSpec(memory_space=pltpu.VMEM)] * 2,
        out_specs=pl.BlockSpec(memory_space=pltpu.VMEM),
        out_shape=jax.ShapeDtypeStruct((16, 8, width + 256), F32),
        compiler_params=params(16),
        cost_estimate=cost(2 << 20),
    )(*scal, came, motion)


def to_air_kernel(scal, came, motion, on_chip, off_chip, pressure, out, moves):
    shift, strip, slab = scal[1], scal[4], scal[5]
    a, b = shift >> 5, shift & 31
    width = out.shape[2]
    pair = jnp.clip((scal[0] - 1) >> 3, 0, 14)
    pressure[...] = came[pair] + came[pair + 1]
    for src in range(16):
        moves[src] = came[src, :, 0:width]
    moves[slab] = motion[...]

    moves[slab ^ 1] = on_chip[...]

    @pl.when((slab > 0) & (slab < 15))
    def _():
        moves[jnp.where((slab & 1) == 0, slab - 1, slab + 1)] = off_chip[...]

    shape = (8, width)
    carry = carries(shape, strip, b)
    row = iota(shape, 0)
    place = (4 * strip + (row & 3) + b) & 31
    first_field = row < 4

    def tile(block):
        def one(src):
            ok = jnp.where((src >= 0) & (src < 16), 1.0, 0.0).astype(F32)
            return moves[jnp.clip(src, 0, 15)] * ok

        return jnp.where(carry, one(block - a - 1), one(block - a))

    for s in range(8):
        tiles = [tile(4 * s + k) for k in range(4)]
        for k in range(4):
            out[s, 8 * k : 8 * k + 8, :] = tiles[k]
        if s > 0:
            before = jnp.where(first_field & (place == 31), tile(4 * s - 1), 0.0)
        else:
            before = jnp.zeros(shape, F32)
        if s < 7:
            behind = jnp.where(first_field & (place == 0), tile(4 * s + 4), 0.0)
        else:
            behind = jnp.zeros(shape, F32)
        out[s, 32:40, :] = before + pltpu.roll(behind, 4, 0)


def to_air(scal, came, motion, on_chip, off_chip):
    width = motion.shape[1]
    return pl.pallas_call(
        placed(to_air_kernel),
        in_specs=[pl.BlockSpec(memory_space=pltpu.SMEM)] * 2
        + [pl.BlockSpec(memory_space=pltpu.VMEM)] * 4,
        out_specs=[pl.BlockSpec(memory_space=pltpu.VMEM)] * 2,
        out_shape=[
            jax.ShapeDtypeStruct((8, width + 256), F32),
            jax.ShapeDtypeStruct((8, 40, width), F32),
        ],
        scratch_shapes=[pltpu.VMEM((16, 8, width), F32)],
        compiler_params=params(16),
        cost_estimate=cost(2 << 20),
    )(*scal, came, motion, on_chip, off_chip)


def force_kernel(scal, field, came, press, out, q, r):
    level, shift, base = scal[0], scal[1], scal[2]
    t = pl.program_id(0)
    height, width = q.shape
    depth = 8
    b = shift & 31

    @pl.when(t == 0)
    def _():
        for k in range(height // 32):
            for f, ref in ((0, r), (1, q)):
                rows = [came[y, 8 * k + 4 * f : 8 * k + 4 * f + 4, :] for y in range(8)]
                ref[32 * k : 32 * k + 32, :] = pltpu.roll(jnp.concatenate(rows, axis=0), b, 0)
        rim = came[0, 32:40, :]
        for y in range(1, 8):
            rim = rim + came[y, 32:40, :]
        above = jnp.sum(rim[0:4], axis=0, keepdims=True)
        below = jnp.sum(rim[4:8], axis=0, keepdims=True)
        motion = r[...]
        around = left_right(motion) + up_down(motion, above, below)
        q[...] = (0.55 - 0.6) * motion + 0.15 * around + 0.5 * q[...] + press[...]

    z = jnp.clip(level - 1 + t - base, 0, depth - 1) + base

    def is_level(other):
        return jnp.where(z == other, 1.0, 0.0).astype(F32)

    wq = is_level(level) - is_level(level + 1)
    wr = 0.15 * (is_level(level - 1) - is_level(level + 2))
    out[0] = field[0] + wq * q[...] + wr * r[...]


def add_force(scal, field, came, press):
    depth, height, width = field.shape

    def where(t, *scal):
        scal = Place(*scal)
        return (jnp.clip(scal[0] - 1 + t - scal[2], 0, depth - 1), 0, 0)

    plane = pl.BlockSpec((1, height, width), where)
    return pl.pallas_call(
        placed(force_kernel),
        grid_spec=pltpu.PrefetchScalarGridSpec(
            num_scalar_prefetch=2,
            grid=(4,),
            in_specs=[
                plane,
                pl.BlockSpec((8, 40, width), lambda t, *scal: (0, 0, 0)),
                pl.BlockSpec((height, width), lambda t, *scal: (0, 0)),
            ],
            out_specs=plane,
            scratch_shapes=[pltpu.VMEM((height, width), F32)] * 2,
        ),
        out_shape=jax.ShapeDtypeStruct(field.shape, F32),
        input_output_aliases={2: 0},
        compiler_params=params(24),
        cost_estimate=cost(4 << 20),
    )(*scal, field, came, press)


def unfold(tile):
    return jnp.concatenate([tile[q : q + 1] for q in range(8)], axis=1)


def plate_last_kernel(n_rows, scal, now, next_ext, pressure, motion, out):
    rows, cols = now.shape
    first = scal[3] * rows - 4
    width = motion.shape[1]
    press = pressure[0:4, 0:width]
    lo = unfold(pressure[:, width : width + 128])
    hi = unfold(pressure[:, width + 128 : width + 256])
    around = left_right(press) + up_down(press, lo, hi) - 4.0 * press
    later = 2.0 * press + 0.3 * around + pressure[4:8, 0:width] - motion[0:4]
    lines = jnp.concatenate([press, later, lo, hi, jnp.zeros((6, width), F32)], axis=0)
    spread = jnp.where((iota((128, 512), 1) >> 2) == iota((128, 512), 0), 1.0, 0.0)
    parts = [
        jnp.dot(lines[:, 128 * q : 128 * q + 128], spread, precision=HIGH, preferred_element_type=F32)
        for q in range(width // 128)
    ]
    wide = jnp.concatenate(parts, axis=1)
    e = iota((24, 16), 0)
    line = iota((24, 16), 1)
    source = jnp.where(e < 4, 8, jnp.where(e >= 20, 9, (e - 4) >> 2))
    pick = jnp.where(line == source, C_PRESS, 0.0)
    push = jnp.dot(pick, wide, precision=HIGH, preferred_element_type=F32)
    pick = jnp.where(iota((16, 16), 1) == 4 + (iota((16, 16), 0) >> 2), C_PRESS, 0.0)
    push_last = jnp.dot(pick, wide, precision=HIGH, preferred_element_type=F32)
    ok = inside_rows(next_ext.shape, first, n_rows)
    mid = jnp.where(ok, next_ext[...] + push, 0.0)
    inner = jnp.where(ok, flat_laplace(mid), 0.0)
    bend = flat_laplace(inner)[4 : 4 + rows]
    final = (2.0 * mid[4 : 4 + rows] - 0.99 * now[...] - 0.04 * bend) * (1.0 / 1.01)
    out[...] = final + push_last


def plate_last(scal, now, next_ext, pressure, motion, n_rows):
    return pl.pallas_call(
        placed(functools.partial(plate_last_kernel, n_rows)),
        in_specs=[pl.BlockSpec(memory_space=pltpu.SMEM)] * 2
        + [pl.BlockSpec(memory_space=pltpu.VMEM)] * 4,
        out_specs=pl.BlockSpec(memory_space=pltpu.VMEM),
        out_shape=jax.ShapeDtypeStruct(now.shape, F32),
        compiler_params=params(16),
        cost_estimate=cost(4 << 20),
    )(*scal, now, next_ext, pressure, motion)


def neighbours(n):
    return [(i, i + 1) for i in range(n - 1)], [(i + 1, i) for i in range(n - 1)]


def shards(air_now, air_prev, plate_now, plate_prev, plate_level, plate_shift):
    depth, height, width = air_now.shape
    n_gz, n_gy = lax.axis_size("gz"), lax.axis_size("gy")
    n_rows = plate_now.shape[0] * n_gz * n_gy
    cols = plate_now.shape[1]
    scal = (plate_level, plate_shift)
    up_d, down_d = neighbours(n_gz * n_gy)

    first, last, sent = front(scal, air_now, air_prev, plate_now, plate_prev)
    lo = lax.ppermute(last, ("gz", "gy"), up_d)
    hi = lax.ppermute(first, ("gz", "gy"), down_d)
    sent, lo, hi = lax.optimization_barrier((sent, lo, hi))
    came = lax.all_to_all(sent, "gy", 0, 0).reshape(256, width + 256)

    plate_ext, motion = plate_first(scal, plate_now, plate_prev, lo, hi, n_rows)
    on_chip, off_chip = faces(scal, air_now, air_prev, lo, hi, motion, cols)
    on_chip = lax.ppermute(on_chip, "gz", [(i, i ^ 1) for i in range(n_gz)])
    across = [(i, i + 1) for i in range(1, n_gz - 1, 2)]
    off_chip = lax.ppermute(off_chip, "gz", across + [(j, i) for i, j in across])

    came = lax.all_to_all(to_plate(scal, came, motion), "gz", 0, 0)
    air_2, press_now = air_steps(scal, air_now, air_prev, on_chip, off_chip, lo, hi, cols)
    end = 2 * height + 8
    pressure, sent = to_air(scal, came, motion, on_chip[end : end + 8], off_chip[end : end + 8])
    came = lax.all_to_all(sent, "gy", 0, 0)

    plate_2 = plate_last(scal, plate_now, plate_ext, pressure, motion, n_rows)
    air_2 = add_force(scal, air_2, came, press_now)
    return (air_2, plate_2)


def solution(mesh):
    in_specs = (
        P("gz", "gy", None),
        P("gz", "gy", None),
        P(("gz", "gy"), None),
        P(("gz", "gy"), None),
        P(),
        P(),
    )
    out_specs = (P("gz", "gy", None), P(("gz", "gy"), None))
    return jax.shard_map(shards, mesh=mesh, in_specs=in_specs, out_specs=out_specs, check_vma=False)
```

time: 126 us -> 96.1 us (0.76)
  starting transfers between devices: 72.3 us -> 39.4 us
  local copies, waits for them, and re-layouts: 14.6 us -> 1.42 us
  waiting for transfers between devices: 12 us -> 23.1 us
  Pallas kernels: 24 us -> 29.4 us
    ppermute x12 -> x4, starting transfers between devices: 53.4 us -> 17.2 us  [the longest x1 5.86 us: shards(): lax.ppermute(off_chip, 'gz', across + [(j, i) for i, j in across])]
    unnamed x26 -> x16, local copies, waits for them, and re-layouts: 9.86 us -> 0.66 us
    ppermute x12 -> x4, waiting for transfers between devices: 6.28 us -> 12 us  [the longest x1 7.82 us: shards(): lax.ppermute(off_chip, 'gz', across + [(j, i) for i, j in across])]
    pallas_call x9 -> x8, Pallas kernels: 24 us -> 29.4 us  [the longest x1 12.1 us: air_steps(): pl.pallas_call(placed(air_kernel), grid_spec=pltpu.PrefetchScalarGridSpec...]
    all_to_all x1, waiting for transfers between devices: 0.01 us -> 4.01 us  [shards(): came = lax.all_to_all(sent, 'gy', 0, 0).reshape(256, width + 256)]
    all_to_all x1, waiting for transfers between devices: 0.01 us -> 3.33 us  [shards(): came = lax.all_to_all(sent, 'gy', 0, 0)]
    squeeze x2 -> x0, local copies, waits for them, and re-layouts: 2.39 us -> none  [the longest x1 2.29 us: shards(): zhi = lax.ppermute(air_now[0], 'gz', down_z)]
    all_to_all x1, waiting for transfers between devices: 5.75 us -> 3.77 us  [shards(): came = lax.all_to_all(to_plate(scal, came, motion), 'gz', 0, 0)]
  transfers between devices with their start and end apart: 15 -> 7, of which waited for: 2 -> 6; matrix products, arithmetic and copies ran while one was open for 3% -> 1% of each run, Pallas kernels for 14% -> 22%
where the time goes in v2:
time: 96.1 us; the launch traced here: 95.3 us
  starting transfers between devices  39.4 us (41%)
  Pallas kernels  29.4 us (31%)
  waiting for transfers between devices  23.1 us (24%)
  between operations  2 us (2%)
  local copies, waits for them, and re-layouts  1.42 us (1%)
    pallas_call x1, Pallas kernels, air_steps(): pl.pallas_call(placed(air_kernel), grid_spec=pltpu.PrefetchScalarGridSpec...  12.1 us
    all_to_all x1, starting transfers between devices, shards(): came = lax.all_to_all(sent, 'gy', 0, 0).reshape(256, width + 256)  7.96 us
    ppermute x1, waiting for transfers between devices, shards(): lax.ppermute(off_chip, 'gz', across + [(j, i) for i, j in across])  7.82 us
    all_to_all x1, starting transfers between devices, shards(): came = lax.all_to_all(sent, 'gy', 0, 0)  7.21 us
    all_to_all x1, starting transfers between devices, shards(): came = lax.all_to_all(to_plate(scal, came, motion), 'gz', 0, 0)  6.97 us
    ppermute x1, starting transfers between devices, shards(): lax.ppermute(off_chip, 'gz', across + [(j, i) for i, j in across])  5.86 us
    ppermute x1, starting transfers between devices, shards(): hi = lax.ppermute(first, ('gz', 'gy'), down_d)  5.63 us
    all_to_all x1, waiting for transfers between devices, shards(): came = lax.all_to_all(sent, 'gy', 0, 0).reshape(256, width + 256)  4.01 us
  transfers between devices with their start and end apart: 7, of which 6 were waited for; matrix products, arithmetic and copies ran while one was open for 1% of the time, Pallas kernels for 22%

profile of v2, /device:TPU:6, one launch (start us, length us, event | category | flops | bytes accessed | tf_op | source)
XLA Modules:
  0.0 95.3 jit_solution(13904512562158940348)
XLA Ops:
  1.9 3.9 %shard_map.77 = (f32[8,6144]{1,0:T(8,128)}, f32[8,6144]{1,0:T(8,128)}, f32[8,32,1280]{2,1,0:T(8,128)}) custom-call(s32[1]{0:T(128)S(6)} %copy.10.level, s32[1]{0:T(128)S(6)} %copy.11.shift, f32[8,128,1024]{2,1,0:T(8,128)} %refs_0_.8, f32[8,128,1024]{2,1,0:T(8,128)} %refs_0_.8, f32[8,128,1024]{2,1,0:T(8,128)} %refs_1_.7, f32[8,128,1024]{2,1,0:T(8,128)} %refs_1_.7, ...), custom_call_target="tpu_custom_call" | custom-call | flops 6291456 | bytes 6291456 | tf_op jit(solution)/shard_map/pallas_call | solution.py:338
  5.9 3.8 %collective-permute-start = (f32[8,6144]{1,0:T(8,128)}, f32[8,6144]{1,0:T(8,128)S(1)}, u32[]{:S(2)}, u32[]{:S(2)}) collective-permute-start(f32[8,6144]{1,0:T(8,128)} %get-tuple-element.17), channel_id=1, source_target_pairs={{0,1},{1,2},{2,3},{3,4},{4,5},{5,6},{6,7},{7,8},{8,9},{9,10},{10,1... | collective-permute-start | bytes 589832 | tf_op jit(solution)/shard_map/ppermute | solution.py:632
  9.7 5.6 %collective-permute-start.1 = (f32[8,6144]{1,0:T(8,128)}, f32[8,6144]{1,0:T(8,128)S(1)}, u32[]{:S(2)}, u32[]{:S(2)}) collective-permute-start(f32[8,6144]{1,0:T(8,128)} %get-tuple-element.18), channel_id=1, source_target_pairs={{1,0},{2,1},{3,2},{4,3},{5,4},{6,5},{7,6},{8,7},{9,8},{10,9},{11,1... | collective-permute-start | bytes 589832 | tf_op jit(solution)/shard_map/ppermute | solution.py:633
  15.3 2.9 %collective-permute-done.refs_2_.refs_3_.refs_4_ = f32[8,6144]{1,0:T(8,128)S(1)} collective-permute-done((f32[8,6144]{1,0:T(8,128)}, f32[8,6144]{1,0:T(8,128)S(1)}, u32[]{:S(2)}, u32[]{:S(2)}) %collective-permute-start) | collective-permute-done | bytes 196640 | tf_op jit(solution)/shard_map/ppermute | solution.py:632
  18.2 0.0 copy-start.1
  18.2 1.3 %collective-permute-done.1.refs_3_.refs_4_.refs_5_ = f32[8,6144]{1,0:T(8,128)S(1)} collective-permute-done((f32[8,6144]{1,0:T(8,128)}, f32[8,6144]{1,0:T(8,128)S(1)}, u32[]{:S(2)}, u32[]{:S(2)}) %collective-permute-start.1) | collective-permute-done | bytes 196640 | tf_op jit(solution)/shard_map/ppermute | solution.py:633
  19.5 0.0 copy-start.2
  19.5 0.0 copy-start
  19.5 0.0 copy-start.3
  19.5 8.0 %all-to-all-start = ((f32[8,32,1280]{2,1,0:T(8,128)}), f32[8,32,1280]{2,1,0:T(8,128)S(1)}, u32[]{:S(2)}, u32[]{:S(2)}) async-start(f32[8,32,1280]{2,1,0:T(8,128)} %get-tuple-element.25), calls=%async_computation | async-start | bytes 2621440 | tf_op jit(solution)/shard_map/all_to_all | solution.py:635
  27.5 0.0 copy-done.1
  27.5 0.0 copy-done.2
  27.5 0.0 copy-done
  27.5 0.0 copy-done.3
  27.5 1.9 %shard_map.78 = (f32[24,4096]{1,0:T(8,128)S(1)}, f32[8,1024]{1,0:T(8,128)S(1)}) custom-call(s32[1]{0:T(128)S(6)} %copy.10.level, s32[1]{0:T(128)S(6)} %copy.11.shift, f32[16,4096]{1,0:T(8,128)S(1)} %copy-done, f32[16,4096]{1,0:T(8,128)S(1)} %copy-done.3, f32[8,6144]{1,0:T(8,128)S(1)} %collective-permute-done.refs_2_.refs_3_.refs_4_, ...), custom_call_target="tpu_custom_call" | custom-call | flops 4194304 | bytes 4194304 | tf_op jit(solution)/shard_map/pallas_call | solution.py:393
  29.4 0.0 copy-start.4
  29.4 0.6 copy-done.4
  30.1 0.0 copy-start.5
  30.1 3.6 %shard_map.79 = (f32[272,1024]{1,0:T(8,128)}, f32[272,1024]{1,0:T(8,128)}) custom-call(s32[1]{0:T(128)S(6)} %copy.10.level, s32[1]{0:T(128)S(6)} %copy.11.shift, f32[8,128,1024]{2,1,0:T(8,128)} %refs_0_.8, f32[8,128,1024]{2,1,0:T(8,128)} %refs_0_.8, f32[8,128,1024]{2,1,0:T(8,128)} %refs_1_.7, f32[8,6144]{1,0:T(8,128)} %copy-done.1, f32[8,6144]{1,0:T(8,128)} %copy-done.2, ...), custom_call_target="tpu_custom_call" | custom-call | flops 5242880 | bytes 5242880 | tf_op jit(solution)/shard_map/pallas_call | solution.py:146
  33.7 1.9 %collective-permute-start.2 = (f32[272,1024]{1,0:T(8,128)}, f32[272,1024]{1,0:T(8,128)S(1)}, u32[]{:S(2)}, u32[]{:S(2)}) collective-permute-start(f32[272,1024]{1,0:T(8,128)} %get-tuple-element.22), channel_id=1, source_target_pairs={{0,8},{8,0},{16,24},{24,16},{32,40},{40,32},{48,56},{56,48},{64,72... | collective-permute-start | bytes 3342344 | tf_op jit(solution)/shard_map/ppermute | solution.py:639
  35.6 5.9 %collective-permute-start.3 = (f32[272,1024]{1,0:T(8,128)}, f32[272,1024]{1,0:T(8,128)}, u32[]{:S(2)}, u32[]{:S(2)}) collective-permute-start(f32[272,1024]{1,0:T(8,128)} %get-tuple-element.23), channel_id=1, source_target_pairs={{8,16},{24,32},{40,48},{56,64},{72,80},{88,96},{104,112},{16,8},{3... | collective-permute-start | bytes 3342344 | tf_op jit(solution)/shard_map/ppermute | solution.py:641
  41.5 4.0 %all-to-all-done = f32[8,32,1280]{2,1,0:T(8,128)S(1)} async-done(((f32[8,32,1280]{2,1,0:T(8,128)}), f32[8,32,1280]{2,1,0:T(8,128)S(1)}, u32[]{:S(2)}, u32[]{:S(2)}) %all-to-all-start) | async-done | bytes 1310752 | tf_op jit(solution)/shard_map/all_to_all | solution.py:635
  45.5 0.0 copy-done.5
  45.5 1.0 %shard_map.81 = f32[16,8,1280]{2,1,0:T(8,128)} custom-call(s32[1]{0:T(128)S(6)} %copy.10.level, s32[1]{0:T(128)S(6)} %copy.11.shift, f32[256,1280]{1,0:T(8,128)S(1)} %bitcast.1, f32[8,1024]{1,0:T(8,128)S(1)} %copy-done.5), custom_call_target="tpu_custom_call" | custom-call | flops 2097152 | bytes 2097152 | tf_op jit(solution)/shard_map/pallas_call | solution.py:440
  46.6 7.0 %all-to-all-start.1 = ((f32[16,8,1280]{2,1,0:T(8,128)}), f32[16,8,1280]{2,1,0:T(8,128)S(1)}, u32[]{:S(2)}, u32[]{:S(2)}) async-start(f32[16,8,1280]{2,1,0:T(8,128)} %shard_map.81), calls=%async_computation.1 | async-start | bytes 1310720 | tf_op jit(solution)/shard_map/all_to_all | solution.py:643
  53.5 0.0 collective-permute-done.2.refs_2_
  53.5 0.0 copy-start.7
  53.5 7.8 %collective-permute-done.3.refs_3_ = f32[272,1024]{1,0:T(8,128)} collective-permute-done((f32[272,1024]{1,0:T(8,128)}, f32[272,1024]{1,0:T(8,128)}, u32[]{:S(2)}, u32[]{:S(2)}) %collective-permute-start.3) | collective-permute-done | bytes 1114144 | tf_op jit(solution)/shard_map/ppermute | solution.py:641
  61.4 0.8 slice.9.refs_3_
  62.1 3.8 %all-to-all-done.1.refs_0_ = f32[16,8,1280]{2,1,0:T(8,128)S(1)} async-done(((f32[16,8,1280]{2,1,0:T(8,128)}), f32[16,8,1280]{2,1,0:T(8,128)S(1)}, u32[]{:S(2)}, u32[]{:S(2)}) %all-to-all-start.1) | async-done | bytes 655392 | tf_op jit(solution)/shard_map/all_to_all | solution.py:643
  65.9 1.2 %shard_map.82 = (f32[8,1280]{1,0:T(8,128)S(1)}, f32[8,40,1024]{2,1,0:T(8,128)}) custom-call(s32[1]{0:T(128)S(6)} %copy.10.level, s32[1]{0:T(128)S(6)} %copy.11.shift, f32[16,8,1280]{2,1,0:T(8,128)S(1)} %all-to-all-done.1.refs_0_, f32[8,1024]{1,0:T(8,128)S(1)} %copy-done.5, f32[8,1024]{1,0:T(8,128)S(1)} %slice.8.refs_2_, f32[8,1024]{1,0:T(8,128)S(1)} %slice.9.refs_3_), custom_call_target="tpu_custom_call" | custom-call | flops 2097152 | bytes 2097152 | tf_op jit(solution)/shard_map/pallas_call | solution.py:497
  67.1 0.0 copy-done.7
  67.1 7.2 %all-to-all-start.2 = ((f32[8,40,1024]{2,1,0:T(8,128)}), f32[8,40,1024]{2,1,0:T(8,128)S(1)}, u32[]{:S(2)}, u32[]{:S(2)}) async-start(f32[8,40,1024]{2,1,0:T(8,128)} %get-tuple-element.26), calls=%async_computation.2 | async-start | bytes 2621440 | tf_op jit(solution)/shard_map/all_to_all | solution.py:647
  74.4 12.1 %shard_map.80 = (f32[8,128,1024]{2,1,0:T(8,128)}, f32[128,1024]{1,0:T(8,128)}) custom-call(s32[1]{0:T(128)S(6)} %copy.10.level, s32[1]{0:T(128)S(6)} %copy.11.shift, f32[8,128,1024]{2,1,0:T(8,128)} %refs_0_.8, f32[8,128,1024]{2,1,0:T(8,128)} %refs_1_.7, f32[272,1024]{1,0:T(8,128)} %copy-done.7, f32[272,1024]{1,0:T(8,128)} %collective-permute-done.3.refs_3_, ...), custom_call_target="tpu_custom_call" | custom-call | flops 25165824 | bytes 25165824 | tf_op jit(solution)/shard_map/pallas_call | solution.py:257
  86.5 0.0 copy-start.6
  86.5 2.5 %shard_map.84 = f32[16,4096]{1,0:T(8,128)} custom-call(s32[1]{0:T(128)S(6)} %copy.10.level, s32[1]{0:T(128)S(6)} %copy.11.shift, f32[16,4096]{1,0:T(8,128)S(1)} %copy-done, f32[24,4096]{1,0:T(8,128)S(1)} %get-tuple-element.28.refs_1_, f32[8,1280]{1,0:T(8,128)S(1)} %get-tuple-element.29.refs_2_, f32[8,1024]{1,0:T(8,128)S(1)} %copy-done.5), custom_call_target="tpu_custom_call" | custom-call | flops 4194304 | bytes 4194304 | tf_op jit(solution)/shard_map/pallas_call | solution.py:608
  89.0 3.3 %all-to-all-done.2.refs_1_ = f32[8,40,1024]{2,1,0:T(8,128)S(1)} async-done(((f32[8,40,1024]{2,1,0:T(8,128)}), f32[8,40,1024]{2,1,0:T(8,128)S(1)}, u32[]{:S(2)}, u32[]{:S(2)}) %all-to-all-start.2) | async-done | bytes 1310752 | tf_op jit(solution)/shard_map/all_to_all | solution.py:647
  92.4 0.0 copy-done.6
  92.4 2.9 %shard_map.83 = f32[8,128,1024]{2,1,0:T(8,128)} custom-call(s32[1]{0:T(128)S(6)} %copy.10.level, s32[1]{0:T(128)S(6)} %copy.11.shift, f32[8,128,1024]{2,1,0:T(8,128)} %get-tuple-element.24.refs_0_, f32[8,40,1024]{2,1,0:T(8,128)S(1)} %all-to-all-done.2.refs_1_, f32[128,1024]{1,0:T(8,128)S(1)} %copy-done.6), custom_call_target="tpu_custom_call", output_to_operand_aliasing={{}: (2, {})} | custom-call | flops 4194304 | bytes 4194304 | tf_op jit(solution)/shard_map/pallas_call | solution.py:552
  (1 shorter events, 0.0 us)
Async XLA Ops:
  5.9 12.3 %collective-permute-start = (f32[8,6144]{1,0:T(8,128)}, f32[8,6144]{1,0:T(8,128)S(1)}, u32[]{:S(2)}, u32[]{:S(2)}) collective-permute-start(f32[8,6144]{1,0:T(8,128)} %get-tuple-element.17), channel_id=1, source_target_pairs={{0,1},{1,2},{2,3},{3,4},{4,5},{5,6},{6,7},{7,8},{8,9},{9,10},{10,1... | collective-permute-start | bytes 589832 | tf_op jit(solution)/shard_map/ppermute | solution.py:632
  9.7 9.8 %collective-permute-start.1 = (f32[8,6144]{1,0:T(8,128)}, f32[8,6144]{1,0:T(8,128)S(1)}, u32[]{:S(2)}, u32[]{:S(2)}) collective-permute-start(f32[8,6144]{1,0:T(8,128)} %get-tuple-element.18), channel_id=1, source_target_pairs={{1,0},{2,1},{3,2},{4,3},{5,4},{6,5},{7,6},{8,7},{9,8},{10,9},{11,1... | collective-permute-start | bytes 589832 | tf_op jit(solution)/shard_map/ppermute | solution.py:633
  18.2 9.3 %copy-start.1 = (f32[8,6144]{1,0:T(8,128)}, f32[8,6144]{1,0:T(8,128)S(1)}, u32[]{:S(2)}) copy-start(f32[8,6144]{1,0:T(8,128)S(1)} %collective-permute-done.refs_2_.refs_3_.refs_4_) | copy-start | bytes 589828
  19.5 8.0 %copy-start.2 = (f32[8,6144]{1,0:T(8,128)}, f32[8,6144]{1,0:T(8,128)S(1)}, u32[]{:S(2)}) copy-start(f32[8,6144]{1,0:T(8,128)S(1)} %collective-permute-done.1.refs_3_.refs_4_.refs_5_) | copy-start | bytes 589828
  19.5 8.0 %copy-start = (f32[16,4096]{1,0:T(8,128)S(1)}, f32[16,4096]{1,0:T(8,128)}, u32[]{:S(2)}) copy-start(f32[16,4096]{1,0:T(8,128)} %refs_0_.9) | copy-start | bytes 786436
  19.5 8.0 %copy-start.3 = (f32[16,4096]{1,0:T(8,128)S(1)}, f32[16,4096]{1,0:T(8,128)}, u32[]{:S(2)}) copy-start(f32[16,4096]{1,0:T(8,128)} %refs_1_.5) | copy-start | bytes 786436
  19.5 26.0 %all-to-all-start = ((f32[8,32,1280]{2,1,0:T(8,128)}), f32[8,32,1280]{2,1,0:T(8,128)S(1)}, u32[]{:S(2)}, u32[]{:S(2)}) async-start(f32[8,32,1280]{2,1,0:T(8,128)} %get-tuple-element.25), calls=%async_computation | async-start | bytes 2621440 | tf_op jit(solution)/shard_map/all_to_all | solution.py:635
  29.4 0.6 copy-start.4
  30.1 15.5 %copy-start.5 = (f32[8,1024]{1,0:T(8,128)S(1)}, f32[8,1024]{1,0:T(8,128)}, u32[]{:S(2)}) copy-start(f32[8,1024]{1,0:T(8,128)} %copy-done.4) | copy-start | bytes 98308
  33.7 19.8 %collective-permute-start.2 = (f32[272,1024]{1,0:T(8,128)}, f32[272,1024]{1,0:T(8,128)S(1)}, u32[]{:S(2)}, u32[]{:S(2)}) collective-permute-start(f32[272,1024]{1,0:T(8,128)} %get-tuple-element.22), channel_id=1, source_target_pairs={{0,8},{8,0},{16,24},{24,16},{32,40},{40,32},{48,56},{56,48},{64,72... | collective-permute-start | bytes 3342344 | tf_op jit(solution)/shard_map/ppermute | solution.py:639
  35.6 25.7 %collective-permute-start.3 = (f32[272,1024]{1,0:T(8,128)}, f32[272,1024]{1,0:T(8,128)}, u32[]{:S(2)}, u32[]{:S(2)}) collective-permute-start(f32[272,1024]{1,0:T(8,128)} %get-tuple-element.23), channel_id=1, source_target_pairs={{8,16},{24,32},{40,48},{56,64},{72,80},{88,96},{104,112},{16,8},{3... | collective-permute-start | bytes 3342344 | tf_op jit(solution)/shard_map/ppermute | solution.py:641
  46.6 19.3 %all-to-all-start.1 = ((f32[16,8,1280]{2,1,0:T(8,128)}), f32[16,8,1280]{2,1,0:T(8,128)S(1)}, u32[]{:S(2)}, u32[]{:S(2)}) async-start(f32[16,8,1280]{2,1,0:T(8,128)} %shard_map.81), calls=%async_computation.1 | async-start | bytes 1310720 | tf_op jit(solution)/shard_map/all_to_all | solution.py:643
  53.5 13.6 %copy-start.7 = (f32[272,1024]{1,0:T(8,128)}, f32[272,1024]{1,0:T(8,128)S(1)}, u32[]{:S(2)}) copy-start(f32[272,1024]{1,0:T(8,128)S(1)} %collective-permute-done.2.refs_2_) | copy-start | bytes 3342340
  67.1 25.2 %all-to-all-start.2 = ((f32[8,40,1024]{2,1,0:T(8,128)}), f32[8,40,1024]{2,1,0:T(8,128)S(1)}, u32[]{:S(2)}, u32[]{:S(2)}) async-start(f32[8,40,1024]{2,1,0:T(8,128)} %get-tuple-element.26), calls=%async_computation.2 | async-start | bytes 2621440 | tf_op jit(solution)/shard_map/all_to_all | solution.py:647
  86.5 5.9 %copy-start.6 = (f32[128,1024]{1,0:T(8,128)S(1)}, f32[128,1024]{1,0:T(8,128)}, u32[]{:S(2)}) copy-start(f32[128,1024]{1,0:T(8,128)} %get-tuple-element.27.refs_2_) | copy-start | bytes 1572868

commit v3 on v2

--- a/solution.py
+++ b/solution.py
@@ -101,37 +101,28 @@
         out[:, cols + width : cols + 2 * width] = 0.2 * here - old[:, edge, :] + 0.3 * around
 
 
-def face_kernel(scal, here, inner, old, lo, hi, motion, on_chip, off_chip):
-    height, width = here.shape[1], here.shape[2]
-    strip = scal[4]
-    lower_core = (scal[5] & 1) == 0
-
-    def one(level, out):
-        above = jnp.where(strip > 0, lo[pl.ds(level, 1), :], 0.0)
-        below = jnp.where(strip < 7, hi[pl.ds(level, 1), :], 0.0)
-
+def face_kernel(scal, here, inner, old, on_chip, off_chip):
+    height = here.shape[1]
+
+    def one(out):
         def emit(i, x, around):
             at = slice(8 * i, 8 * i + 8)
             out[at, :] = x
             part = 0.2 * x - old[0, at, :] + 0.3 * (around + inner[0, at, :])
             out[height + 8 * i : height + 8 * i + 8, :] = part
 
-        sweep(lambda i: here[0, 8 * i : 8 * i + 8, :], height // 8, above, below, emit)
-        row = iota((8, width), 0)
-        ends = jnp.where(row == 0, above, jnp.where(row == 1, below, 0.0))
-        out[2 * height : 2 * height + 8, :] = ends
-        out[2 * height + 8 : 2 * height + 16, :] = motion[...]
+        sweep(lambda i: here[0, 8 * i : 8 * i + 8, :], height // 8, 0.0, 0.0, emit)
 
     @pl.when(pl.program_id(0) == 0)
     def _():
-        one(jnp.where(lower_core, 7, 0), on_chip)
+        one(on_chip)
 
     @pl.when(pl.program_id(0) == 1)
     def _():
-        one(jnp.where(lower_core, 0, 7), off_chip)
-
-
-def faces(scal, air_now, air_prev, lo, hi, motion, cols):
+        one(off_chip)
+
+
+def faces(scal, air_now, air_prev):
     depth, height, width = air_now.shape
 
     def plane(inner):
@@ -141,8 +132,7 @@
 
         return pl.BlockSpec((1, height, width), where)
 
-    edge = pl.BlockSpec((8, width), lambda i, *scal: (0, cols // width))
-    out = pl.BlockSpec((2 * height + 16, width), lambda i, *scal: (0, 0))
+    out = pl.BlockSpec((2 * height, width), lambda i, *scal: (0, 0))
     return pl.pallas_call(
         placed(face_kernel),
         grid_spec=pltpu.PrefetchScalarGridSpec(
@@ -152,23 +142,51 @@
                 plane(0),
                 plane(1),
                 plane(0),
-                edge,
-                edge,
-                pl.BlockSpec((8, width), lambda i, *scal: (0, 0)),
             ],
             out_specs=[out, out],
         ),
-        out_shape=[jax.ShapeDtypeStruct((2 * height + 16, width), F32)] * 2,
+        out_shape=[jax.ShapeDtypeStruct((2 * height, width), F32)] * 2,
         compiler_params=params(59),
         cost_estimate=cost(5 << 20),
-    )(*scal, air_now, air_now, air_prev, lo, hi, motion)
-
-
-def air_kernel(scal, now, prev, on_chip, off_chip, ylo, yhi, out, press, keep, mid):
+    )(*scal, air_now, air_now, air_prev)
+
+
+def corner_kernel(scal, lo, hi, on_chip, off_chip):
+    strip = scal[4]
+    lower_core = (scal[5] & 1) == 0
+    row = iota(on_chip.shape, 0)
+
+    def ends(level):
+        above = jnp.where(strip > 0, lo[level : level + 1, :], 0.0)
+        below = jnp.where(strip < 7, hi[level : level + 1, :], 0.0)
+        return jnp.where(row == 0, above, jnp.where(row == 1, below, 0.0))
+
+    bottom, top = ends(0), ends(7)
+    on_chip[...] = jnp.where(lower_core, top, bottom)
+    off_chip[...] = jnp.where(lower_core, bottom, top)
+
+
+def corners(scal, lo, hi, cols, width):
+    edge = pl.BlockSpec((8, width), lambda i, *scal: (0, cols // width))
+    out = pl.BlockSpec((8, width), lambda i, *scal: (0, 0))
+    return pl.pallas_call(
+        placed(corner_kernel),
+        grid_spec=pltpu.PrefetchScalarGridSpec(
+            num_scalar_prefetch=2, grid=(1,), in_specs=[edge, edge], out_specs=[out, out]
+        ),
+        out_shape=[jax.ShapeDtypeStruct((8, width), F32)] * 2,
+        compiler_params=params(16),
+        cost_estimate=cost(1 << 20),
+    )(*scal, lo, hi)
+
+
+def air_kernel(
+    scal, now, prev, on_chip, off_chip, ylo, yhi,
+    out, press, keep, mid, older, sems,
+):
     level, shift, first, strip, slab = scal[0], scal[1], scal[2], scal[4], scal[5]
     t = pl.program_id(0)
-    _, height, width = now.shape
-    depth = 8
+    depth, height, width = now.shape
     strips = [slice(8 * i, 8 * i + 8) for i in range(height // 8)]
     y_lo = jnp.where(strip > 0, 1.0, 0.0).astype(F32)
     y_hi = jnp.where(strip < 7, 1.0, 0.0).astype(F32)
@@ -182,24 +200,41 @@
         at = slice(first, first + count)
         return jnp.where(lower_core, on_chip[at, :], off_chip[at, :])
 
+    def fetch_now(z):
+        return pltpu.make_async_copy(now.at[z], keep.at[z + 1], sems.at[0, z])
+
+    def fetch_prev(z):
+        return pltpu.make_async_copy(prev.at[z], older.at[z], sems.at[1, z])
+
     @pl.when(t == 0)
     def _():
-        inside = jnp.where(slab > 0, 1.0, 0.0).astype(F32)
+        for z in range(depth):
+            fetch_now(z).start()
+            fetch_prev(z).start()
+
+    @pl.when(t < depth)
+    def _():
+        fetch_now(t).wait()
+
+    @pl.when((t >= 1) & (t <= depth))
+    def _():
+        fetch_prev(t - 1).wait()
+
+    def outer(target, source, level, inside):
+        inside = jnp.where(inside, 1.0, 0.0).astype(F32)
+        for i, at in enumerate(strips):
+            mid[target, at, :] = inside * (source(height + 8 * i, 8) + 0.3 * keep[level, at, :])
+
+    @pl.when(t == 0)
+    def _():
         for i, at in enumerate(strips):
             keep[0, at, :] = zlo(8 * i, 8)
             keep[depth + 1, at, :] = zhi(8 * i, 8)
-            mid[0, at, :] = inside * (zlo(height + 8 * i, 8) + 0.3 * now[0, at, :])
+        outer(0, zlo, 1, slab > 0)
 
     @pl.when(t == depth - 1)
     def _():
-        inside = jnp.where(slab < 15, 1.0, 0.0).astype(F32)
-        for i, at in enumerate(strips):
-            mid[depth + 1, at, :] = inside * (zhi(height + 8 * i, 8) + 0.3 * now[0, at, :])
-
-    @pl.when(t < depth)
-    def _():
-        for at in strips:
-            keep[t + 1, at, :] = now[0, at, :]
+        outer(depth + 1, zhi, depth, slab < 15)
 
     @pl.when((t >= 1) & (t <= depth))
     def _():
@@ -210,22 +245,19 @@
         def emit(i, x, around):
             at = strips[i]
             total = around + keep[z, at, :] + keep[z + 2, at, :]
-            mid[z + 1, at, :] = 0.2 * x - prev[0, at, :] + 0.3 * total
+            mid[z + 1, at, :] = 0.2 * x - older[z, at, :] + 0.3 * total
 
         sweep(lambda i: keep[z + 1, strips[i], :], len(strips), above, below, emit)
 
     @pl.when(t >= 2)
     def _():
         z = t - 2
-        at_bottom = jnp.where(z == 0, 0.3, 0.0).astype(F32)
-        at_top = jnp.where(z == depth - 1, 0.3, 0.0).astype(F32)
-
-        def rim(rows, line, r):
-            row = rows[pl.ds(z, 1), width : 2 * width] + 0.3 * line
-            return row + at_bottom * zlo(r, 1) + at_top * zhi(r, 1)
-
-        above = y_lo * rim(ylo, keep[z + 1, 0:1, :], 2 * height)
-        below = y_hi * rim(yhi, keep[z + 1, height - 1 : height, :], 2 * height + 1)
+
+        def rim(rows, line):
+            return rows[pl.ds(z, 1), width : 2 * width] + 0.3 * line
+
+        above = y_lo * rim(ylo, keep[z + 1, 0:1, :])
+        below = y_hi * rim(yhi, keep[z + 1, height - 1 : height, :])
 
         def emit(i, x, around):
             at = strips[i]
@@ -252,19 +284,22 @@
             (1, height, width), lambda t, *scal: (jnp.clip(t - lag, 0, depth - 1), 0, 0)
         )
 
-    z_face = pl.BlockSpec((2 * height + 16, width), lambda t, *scal: (0, 0))
+    whole = pl.BlockSpec(memory_space=pl.ANY)
+
+    z_face = pl.BlockSpec((2 * height, width), lambda t, *scal: (0, 0))
     rows = pl.BlockSpec((8, 2 * width), lambda t, *scal: (0, cols // (2 * width)))
     return pl.pallas_call(
         placed(air_kernel),
         grid_spec=pltpu.PrefetchScalarGridSpec(
             num_scalar_prefetch=2,
             grid=(depth + 2,),
-            in_specs=[plane(0), plane(1), z_face, z_face, rows, rows],
+            in_specs=[whole, whole, z_face, z_face, rows, rows],
             out_specs=[
                 plane(2),
                 pl.BlockSpec((height, width), lambda t, *scal: (0, 0)),
             ],
-            scratch_shapes=[pltpu.VMEM((depth + 2, height, width), F32)] * 2,
+            scratch_shapes=[pltpu.VMEM((depth + 2, height, width), F32)] * 2
+            + [pltpu.VMEM(now.shape, F32), pltpu.SemaphoreType.DMA((2, depth))],
         ),
         out_shape=[
             jax.ShapeDtypeStruct(now.shape, F32),
@@ -277,6 +312,10 @@
 
 def fold_row(row):
     return jnp.concatenate([row[:, 128 * q : 128 * q + 128] for q in range(8)], axis=0)
+
+
+def unfold(tile):
+    return jnp.concatenate([tile[q : q + 1] for q in range(8)], axis=1)
 
 
 def press_kernel(scal, up2, up1, at0, dn1, pup1, pat0, out):
@@ -342,7 +381,8 @@
             grid=(1,),
             in_specs=[low, high, low, high, plate, plate]
             + [plane(2), plane(1), plane(0), plane(-1), plane(1), plane(0)],
-            out_specs=[pack, pack, pl.BlockSpec((8, 32, width + 256), lambda k, *scal: (0, 0, 0))],
+            out_specs=[pack, pack]
+            + [pl.BlockSpec((8, 32, width + 256), lambda k, *scal: (0, 0, 0))],
         ),
         out_shape=[jax.ShapeDtypeStruct((8, cols + 2 * width), F32)] * 2
         + [jax.ShapeDtypeStruct((8, 32, width + 256), F32)],
@@ -365,43 +405,49 @@
     return (row >= 0) & (row < last_row)
 
 
-def plate_kernel(n_rows, scal, now, prev, lo, hi, next_ext, motion):
+def plate_step(ext, old, ok):
+    inner = jnp.where(ok, flat_laplace(ext), 0.0)
+    bend = flat_laplace(inner)
+    return (2.0 * ext - 0.99 * old - 0.04 * bend) * (1.0 / 1.01)
+
+
+def plate_kernel(n_rows, scal, now, prev, motion):
     rows, cols = now.shape
     first = scal[3] * rows - 4
     here = now[...]
-    ext = jnp.concatenate([lo[0:4, 0:cols], here, hi[0:4, 0:cols]], axis=0)
-    old = jnp.concatenate([lo[4:8, 0:cols], prev[...], hi[4:8, 0:cols]], axis=0)
+    far = jnp.zeros((4, cols), F32)
+    ext = jnp.concatenate([far, here, far], axis=0)
+    old = jnp.concatenate([far, prev[...], far], axis=0)
     ok = inside_rows(ext.shape, first, n_rows)
-    inner = jnp.where(ok, flat_laplace(ext), 0.0)
-    bend = flat_laplace(inner)
-    nxt = (2.0 * ext - 0.99 * old - 0.04 * bend) * (1.0 / 1.01)
-    nxt = jnp.where(ok, nxt, 0.0)
-    next_ext[...] = nxt
-    both = jnp.concatenate([here - prev[...], nxt[4 : 4 + rows] - here], axis=0)
+    nxt = jnp.where(ok, plate_step(ext, old, ok), 0.0) - ext
+    both = jnp.concatenate([here - prev[...], nxt], axis=0)
     fold = jnp.where((iota((512, 128), 0) >> 2) == iota((512, 128), 1), 1.0, 0.0)
     parts = [
         jnp.dot(both[:, 512 * q : 512 * q + 512], fold, precision=HIGH, preferred_element_type=F32)
         for q in range(cols // 512)
     ]
     narrow = jnp.concatenate(parts, axis=1)
-    pick = jnp.where(iota((8, 32), 0) == (iota((8, 32), 1) >> 2), 1.0 / 16.0, 0.0)
-    motion[...] = jnp.dot(pick, narrow, precision=HIGH, preferred_element_type=F32)
-
-
-def plate_first(scal, now, prev, lo, hi, n_rows):
+    width = narrow.shape[1]
+    row = iota((16, 40), 0)
+    source = jnp.where(row < 4, row, jnp.where(row < 8, row + 1, jnp.where(row == 8, 4, 9)))
+    pick = jnp.where((source == (iota((16, 40), 1) >> 2)) & (row < 10), 1.0 / 16.0, 0.0)
+    lines = jnp.dot(pick, narrow, precision=HIGH, preferred_element_type=F32)
+    motion[:, 0:width] = lines[0:8]
+    motion[:, width : width + 128] = fold_row(lines[8:9])
+    motion[:, width + 128 : width + 256] = fold_row(lines[9:10])
+
+
+def plate_first(scal, now, prev, n_rows):
     rows, cols = now.shape
     return pl.pallas_call(
         placed(functools.partial(plate_kernel, n_rows)),
         in_specs=[pl.BlockSpec(memory_space=pltpu.SMEM)] * 2
-        + [pl.BlockSpec(memory_space=pltpu.VMEM)] * 4,
-        out_specs=[pl.BlockSpec(memory_space=pltpu.VMEM)] * 2,
-        out_shape=[
-            jax.ShapeDtypeStruct((rows + 8, cols), F32),
-            jax.ShapeDtypeStruct((8, cols // 4), F32),
-        ],
+        + [pl.BlockSpec(memory_space=pltpu.VMEM)] * 2,
+        out_specs=pl.BlockSpec(memory_space=pltpu.VMEM),
+        out_shape=jax.ShapeDtypeStruct((8, cols // 4 + 256), F32),
         compiler_params=params(16),
         cost_estimate=cost(4 << 20),
-    )(*scal, now, prev, lo, hi)
+    )(*scal, now, prev)
 
 
 def carries(shape, strip, b):
@@ -412,8 +458,8 @@
     shift, strip = scal[1], scal[4]
     a, b = shift >> 5, shift & 31
     move = motion[...]
-    width = move.shape[1]
-    carry = carries(move.shape, strip, b)
+    width = move.shape[1] - 256
+    carry = carries((8, width), strip, b)
     before = (4 * strip - 1 + b) >> 5
     behind = (4 * strip + 4 + b) >> 5
 
@@ -430,13 +476,15 @@
         after = pl.multiple_of(8 * jnp.minimum(dest + a + 1, 31), 8)
         tile = jnp.where(carry, came[pl.ds(after, 8), 0:width], came[pl.ds(at, 8), 0:width])
         wants = aside & ((pair == dest) | (pair + 1 == dest))
-        out[dest, :, 0:width] = jnp.where(wants, move, tile)
-        out[dest, :, width : width + 128] = folded(dest + a + before, width)
-        out[dest, :, width + 128 : width + 256] = folded(dest + a + behind, width + 128)
+        out[dest, :, 0:width] = jnp.where(wants, move[:, 0:width], tile)
+        for n, block in ((0, dest + a + before), (1, dest + a + behind)):
+            lane = width + 128 * n
+            part = folded(block, lane)
+            out[dest, :, lane : lane + 128] = jnp.where(wants, move[:, lane : lane + 128], part)
 
 
 def to_plate(scal, came, motion):
-    width = motion.shape[1]
+    width = motion.shape[1] - 256
     return pl.pallas_call(
         placed(to_plate_kernel),
         in_specs=[pl.BlockSpec(memory_space=pltpu.SMEM)] * 2
@@ -451,13 +499,12 @@
 def to_air_kernel(scal, came, motion, on_chip, off_chip, pressure, out, moves):
     shift, strip, slab = scal[1], scal[4], scal[5]
     a, b = shift >> 5, shift & 31
-    width = out.shape[2]
+    width = pressure.shape[1] - 256
     pair = jnp.clip((scal[0] - 1) >> 3, 0, 14)
     pressure[...] = came[pair] + came[pair + 1]
     for src in range(16):
-        moves[src] = came[src, :, 0:width]
+        moves[src] = came[src]
     moves[slab] = motion[...]
-
     moves[slab ^ 1] = on_chip[...]
 
     @pl.when((slab > 0) & (slab < 15))
@@ -469,31 +516,40 @@
     row = iota(shape, 0)
     place = (4 * strip + (row & 3) + b) & 31
     first_field = row < 4
+    before = (4 * strip - 1 + b) >> 5
+    behind = (4 * strip + 4 + b) >> 5
+
+    def part(src, lanes):
+        ok = jnp.where((src >= 0) & (src < 16), 1.0, 0.0).astype(F32)
+        return moves[jnp.clip(src, 0, 15), :, lanes] * ok
 
     def tile(block):
-        def one(src):
-            ok = jnp.where((src >= 0) & (src < 16), 1.0, 0.0).astype(F32)
-            return moves[jnp.clip(src, 0, 15)] * ok
-
-        return jnp.where(carry, one(block - a - 1), one(block - a))
-
+        lanes = slice(0, width)
+        return jnp.where(carry, part(block - a - 1, lanes), part(block - a, lanes))
+
+    def rim(block, spot):
+        rows = jnp.where(first_field & (place == spot), tile(block), 0.0)
+        return fold_row(jnp.sum(rows, axis=0, keepdims=True))
+
+    none = jnp.zeros((8, 128), F32)
     for s in range(8):
-        tiles = [tile(4 * s + k) for k in range(4)]
         for k in range(4):
-            out[s, 8 * k : 8 * k + 8, :] = tiles[k]
-        if s > 0:
-            before = jnp.where(first_field & (place == 31), tile(4 * s - 1), 0.0)
-        else:
-            before = jnp.zeros(shape, F32)
-        if s < 7:
-            behind = jnp.where(first_field & (place == 0), tile(4 * s + 4), 0.0)
-        else:
-            behind = jnp.zeros(shape, F32)
-        out[s, 32:40, :] = before + pltpu.roll(behind, 4, 0)
+            at = slice(8 * k, 8 * k + 8)
+            block = 4 * s + k
+            out[s, at, 0:width] = tile(block)
+            lanes = slice(width, width + 128)
+            out[s, at, lanes] = part(block - a - before, lanes)
+            lanes = slice(width + 128, width + 256)
+            out[s, at, lanes] = part(block - a - behind, lanes)
+        lanes = slice(width + 256, width + 384)
+        out[s, 0:8, lanes] = rim(4 * s - 1, 31) if s > 0 else none
+        out[s, 8:16, lanes] = rim(4 * s + 4, 0) if s < 7 else none
+        out[s, 16:24, lanes] = none
+        out[s, 24:32, lanes] = none
 
 
 def to_air(scal, came, motion, on_chip, off_chip):
-    width = motion.shape[1]
+    width = motion.shape[1] - 256
     return pl.pallas_call(
         placed(to_air_kernel),
         in_specs=[pl.BlockSpec(memory_space=pltpu.SMEM)] * 2
@@ -501,12 +557,44 @@
         out_specs=[pl.BlockSpec(memory_space=pltpu.VMEM)] * 2,
         out_shape=[
             jax.ShapeDtypeStruct((8, width + 256), F32),
-            jax.ShapeDtypeStruct((8, 40, width), F32),
+            jax.ShapeDtypeStruct((8, 32, width + 384), F32),
         ],
-        scratch_shapes=[pltpu.VMEM((16, 8, width), F32)],
+        scratch_shapes=[pltpu.VMEM((16, 8, width + 256), F32)],
         compiler_params=params(16),
         cost_estimate=cost(2 << 20),
     )(*scal, came, motion, on_chip, off_chip)
+
+
+def add_corner_kernel(scal, field, on_chip, off_chip, out):
+    t = pl.program_id(0)
+    lower_core = (scal[5] & 1) == 0
+    low = t < 2
+    first_end = (t & 1) == 0
+    near = jnp.where(jnp.logical_not(jnp.logical_xor(low, lower_core)), off_chip[...], on_chip[...])
+    line = jnp.where(first_end, near[0:1], near[1:2])
+    row = iota(out.shape[1:], 0)
+    spot = jnp.where(first_end, 0, 7)
+    out[0] = field[0] + jnp.where(row == spot, 0.18 * line, 0.0)
+
+
+def add_corners(scal, field, on_chip, off_chip):
+    depth, height, width = field.shape
+
+    def where(t, *scal):
+        return ((t >> 1) * (depth - 1), (t & 1) * (height // 8 - 1), 0)
+
+    tile = pl.BlockSpec((1, 8, width), where)
+    pack = pl.BlockSpec((8, width), lambda t, *scal: (0, 0))
+    return pl.pallas_call(
+        placed(add_corner_kernel),
+        grid_spec=pltpu.PrefetchScalarGridSpec(
+            num_scalar_prefetch=2, grid=(4,), in_specs=[tile, pack, pack], out_specs=tile
+        ),
+        out_shape=jax.ShapeDtypeStruct(field.shape, F32),
+        input_output_aliases={2: 0},
+        compiler_params=params(59),
+        cost_estimate=cost(1 << 20),
+    )(*scal, field, on_chip, off_chip)
 
 
 def force_kernel(scal, field, came, press, out, q, r):
@@ -519,14 +607,23 @@
     @pl.when(t == 0)
     def _():
         for k in range(height // 32):
-            for f, ref in ((0, r), (1, q)):
-                rows = [came[y, 8 * k + 4 * f : 8 * k + 4 * f + 4, :] for y in range(8)]
-                ref[32 * k : 32 * k + 32, :] = pltpu.roll(jnp.concatenate(rows, axis=0), b, 0)
-        rim = came[0, 32:40, :]
+            at = slice(32 * k, 32 * k + 32)
+            tiles = [came[y, 8 * k : 8 * k + 8, :] for y in range(8)]
+            now = jnp.concatenate([x[0:4, 0:width] for x in tiles], axis=0)
+            later = []
+            for y in range(8):
+                own = tiles[y][4:8, 0:width]
+                row = iota(own.shape, 0)
+                top = unfold(tiles[(y - 1) % 8][:, width + 128 : width + 256])
+                bottom = unfold(tiles[(y + 1) % 8][:, width : width + 128])
+                own = own + jnp.where(row == 0, top, 0.0) + jnp.where(row == 3, bottom, 0.0)
+                later.append(own)
+            r[at, :] = pltpu.roll(now, b, 0)
+            q[at, :] = pltpu.roll(jnp.concatenate(later, axis=0), b, 0)
+        rim = came[0, 0:16, width + 256 : width + 384]
         for y in range(1, 8):
-            rim = rim + came[y, 32:40, :]
-        above = jnp.sum(rim[0:4], axis=0, keepdims=True)
-        below = jnp.sum(rim[4:8], axis=0, keepdims=True)
+            rim = rim + came[y, 0:16, width + 256 : width + 384]
+        above, below = unfold(rim[0:8]), unfold(rim[8:16])
         motion = r[...]
         around = left_right(motion) + up_down(motion, above, below)
         q[...] = (0.55 - 0.6) * motion + 0.15 * around + 0.5 * q[...] + press[...]
@@ -556,7 +653,7 @@
             grid=(4,),
             in_specs=[
                 plane,
-                pl.BlockSpec((8, 40, width), lambda t, *scal: (0, 0, 0)),
+                pl.BlockSpec((8, 32, width + 384), lambda t, *scal: (0, 0, 0)),
                 pl.BlockSpec((height, width), lambda t, *scal: (0, 0)),
             ],
             out_specs=plane,
@@ -569,19 +666,15 @@
     )(*scal, field, came, press)
 
 
-def unfold(tile):
-    return jnp.concatenate([tile[q : q + 1] for q in range(8)], axis=1)
-
-
-def plate_last_kernel(n_rows, scal, now, next_ext, pressure, motion, out):
+def plate_last_kernel(n_rows, scal, now, prev, below, above, pressure, motion, out):
     rows, cols = now.shape
     first = scal[3] * rows - 4
-    width = motion.shape[1]
+    width = motion.shape[1] - 256
     press = pressure[0:4, 0:width]
     lo = unfold(pressure[:, width : width + 128])
     hi = unfold(pressure[:, width + 128 : width + 256])
     around = left_right(press) + up_down(press, lo, hi) - 4.0 * press
-    later = 2.0 * press + 0.3 * around + pressure[4:8, 0:width] - motion[0:4]
+    later = 2.0 * press + 0.3 * around + pressure[4:8, 0:width] - motion[0:4, 0:width]
     lines = jnp.concatenate([press, later, lo, hi, jnp.zeros((6, width), F32)], axis=0)
     spread = jnp.where((iota((128, 512), 1) >> 2) == iota((128, 512), 0), 1.0, 0.0)
     parts = [
@@ -596,24 +689,27 @@
     push = jnp.dot(pick, wide, precision=HIGH, preferred_element_type=F32)
     pick = jnp.where(iota((16, 16), 1) == 4 + (iota((16, 16), 0) >> 2), C_PRESS, 0.0)
     push_last = jnp.dot(pick, wide, precision=HIGH, preferred_element_type=F32)
-    ok = inside_rows(next_ext.shape, first, n_rows)
-    mid = jnp.where(ok, next_ext[...] + push, 0.0)
+    here = now[...]
+    ext = jnp.concatenate([below[0:4, 0:cols], here, above[0:4, 0:cols]], axis=0)
+    old = jnp.concatenate([below[4:8, 0:cols], prev[...], above[4:8, 0:cols]], axis=0)
+    ok = inside_rows(ext.shape, first, n_rows)
+    mid = jnp.where(ok, plate_step(ext, old, ok) + push, 0.0)
     inner = jnp.where(ok, flat_laplace(mid), 0.0)
     bend = flat_laplace(inner)[4 : 4 + rows]
-    final = (2.0 * mid[4 : 4 + rows] - 0.99 * now[...] - 0.04 * bend) * (1.0 / 1.01)
+    final = (2.0 * mid[4 : 4 + rows] - 0.99 * here - 0.04 * bend) * (1.0 / 1.01)
     out[...] = final + push_last
 
 
-def plate_last(scal, now, next_ext, pressure, motion, n_rows):
+def plate_last(scal, now, prev, lo, hi, pressure, motion, n_rows):
     return pl.pallas_call(
         placed(functools.partial(plate_last_kernel, n_rows)),
         in_specs=[pl.BlockSpec(memory_space=pltpu.SMEM)] * 2
-        + [pl.BlockSpec(memory_space=pltpu.VMEM)] * 4,
+        + [pl.BlockSpec(memory_space=pltpu.VMEM)] * 6,
         out_specs=pl.BlockSpec(memory_space=pltpu.VMEM),
         out_shape=jax.ShapeDtypeStruct(now.shape, F32),
         compiler_params=params(16),
         cost_estimate=cost(4 << 20),
-    )(*scal, now, next_ext, pressure, motion)
+    )(*scal, now, prev, lo, hi, pressure, motion)
 
 
 def neighbours(n):
@@ -629,24 +725,35 @@
     up_d, down_d = neighbours(n_gz * n_gy)
 
     first, last, sent = front(scal, air_now, air_prev, plate_now, plate_prev)
+    came = lax.all_to_all(sent, "gy", 0, 0).reshape(256, width + 256)
     lo = lax.ppermute(last, ("gz", "gy"), up_d)
     hi = lax.ppermute(first, ("gz", "gy"), down_d)
-    sent, lo, hi = lax.optimization_barrier((sent, lo, hi))
-    came = lax.all_to_all(sent, "gy", 0, 0).reshape(256, width + 256)
-
-    plate_ext, motion = plate_first(scal, plate_now, plate_prev, lo, hi, n_rows)
-    on_chip, off_chip = faces(scal, air_now, air_prev, lo, hi, motion, cols)
-    on_chip = lax.ppermute(on_chip, "gz", [(i, i ^ 1) for i in range(n_gz)])
+
     across = [(i, i + 1) for i in range(1, n_gz - 1, 2)]
-    off_chip = lax.ppermute(off_chip, "gz", across + [(j, i) for i, j in across])
+    pairs_on = [(i, i ^ 1) for i in range(n_gz)]
+    pairs_off = across + [(j, i) for i, j in across]
+    motion = plate_first(scal, plate_now, plate_prev, n_rows)
+    motion_on = lax.ppermute(motion, "gz", pairs_on)
+    motion_off = lax.ppermute(motion, "gz", pairs_off)
+    level, motion_on, motion_off = lax.optimization_barrier((plate_level, motion_on, motion_off))
+    on_chip, off_chip = faces((level, plate_shift), air_now, air_prev)
+    motion, on_chip, off_chip = lax.optimization_barrier((motion, on_chip, off_chip))
+    on_chip = lax.ppermute(on_chip, "gz", pairs_on)
+    off_chip = lax.ppermute(off_chip, "gz", pairs_off)
 
     came = lax.all_to_all(to_plate(scal, came, motion), "gz", 0, 0)
-    air_2, press_now = air_steps(scal, air_now, air_prev, on_chip, off_chip, lo, hi, cols)
-    end = 2 * height + 8
-    pressure, sent = to_air(scal, came, motion, on_chip[end : end + 8], off_chip[end : end + 8])
+    came, lo, hi, on_chip, off_chip = lax.optimization_barrier((came, lo, hi, on_chip, off_chip))
+    corner_on, corner_off = corners(scal, lo, hi, cols, width)
+    corner_on = lax.ppermute(corner_on, "gz", pairs_on)
+    corner_off = lax.ppermute(corner_off, "gz", pairs_off)
+    pressure, sent = to_air(scal, came, motion, motion_on, motion_off)
+    air_2, press_now = air_steps(
+        scal, air_now, air_prev, on_chip, off_chip, lo, hi, cols
+    )
     came = lax.all_to_all(sent, "gy", 0, 0)
 
-    plate_2 = plate_last(scal, plate_now, plate_ext, pressure, motion, n_rows)
+    plate_2 = plate_last(scal, plate_now, plate_prev, lo, hi, pressure, motion, n_rows)
+    air_2 = add_corners(scal, air_2, corner_on, corner_off)
     air_2 = add_force(scal, air_2, came, press_now)
     return (air_2, plate_2)
 

time: 96.1 us -> 90 us (0.937)
  waiting for transfers between devices: 23.1 us -> 12.3 us
  starting transfers between devices: 39.4 us -> 41.7 us
  Pallas kernels: 29.4 us -> 30.7 us
    ppermute x2 -> x6, starting transfers between devices: 7.78 us -> 12.2 us  [the longest x1 5.29 us: shards(): off_chip = lax.ppermute(off_chip, 'gz', pairs_off)]
    all_to_all x1, waiting for transfers between devices: 3.77 us -> 0.01 us  [shards(): came = lax.all_to_all(to_plate(scal, came, motion), 'gz', 0, 0)]
    all_to_all x1, waiting for transfers between devices: 3.33 us -> 0.01 us  [shards(): came = lax.all_to_all(sent, 'gy', 0, 0)]
    pallas_call x0 -> x2, Pallas kernels: none -> 2.89 us  [the longest x1 2.87 us: add_corners(): pl.pallas_call(placed(add_corner_kernel), grid_spec=pltpu.PrefetchScalarG...]
    ppermute x1, waiting for transfers between devices: 2.89 us -> 0.01 us  [shards(): lo = lax.ppermute(last, ('gz', 'gy'), up_d)]
    all_to_all x1, waiting for transfers between devices: 4.01 us -> 6.22 us  [shards(): came = lax.all_to_all(sent, 'gy', 0, 0).reshape(256, width + 256)]
    ppermute x2 -> x6, waiting for transfers between devices: 7.82 us -> 6.11 us  [the longest x1 3.96 us: shards(): motion_off = lax.ppermute(motion, 'gz', pairs_off)]
    all_to_all x1, starting transfers between devices: 7.21 us -> 5.88 us  [shards(): came = lax.all_to_all(sent, 'gy', 0, 0)]
  transfers between devices with their start and end apart: 7 -> 11, of which waited for: 6 -> 4; matrix products, arithmetic and copies ran while one was open for 1% -> 0% of each run, Pallas kernels for 22% -> 26%
where the time goes in v3:
time: 90 us; the launch traced here: 88.6 us
  starting transfers between devices  41.7 us (46%)
  Pallas kernels  30.7 us (34%)
  waiting for transfers between devices  12.3 us (14%)
  between operations  2.1 us (2%)
  local copies, waits for them, and re-layouts  1.74 us (2%)
    pallas_call x1, Pallas kernels, air_steps(): pl.pallas_call(placed(air_kernel), grid_spec=pltpu.PrefetchScalarGridSpec...  10.9 us
    all_to_all x1, starting transfers between devices, shards(): came = lax.all_to_all(sent, 'gy', 0, 0).reshape(256, width + 256)  8.28 us
    ppermute x1, starting transfers between devices, shards(): hi = lax.ppermute(first, ('gz', 'gy'), down_d)  6.69 us
    all_to_all x1, waiting for transfers between devices, shards(): came = lax.all_to_all(sent, 'gy', 0, 0).reshape(256, width + 256)  6.22 us
    all_to_all x1, starting transfers between devices, shards(): came = lax.all_to_all(to_plate(scal, came, motion), 'gz', 0, 0)  5.96 us
    all_to_all x1, starting transfers between devices, shards(): came = lax.all_to_all(sent, 'gy', 0, 0)  5.88 us
    ppermute x1, starting transfers between devices, shards(): off_chip = lax.ppermute(off_chip, 'gz', pairs_off)  5.29 us
    ppermute x1, waiting for transfers between devices, shards(): motion_off = lax.ppermute(motion, 'gz', pairs_off)  3.96 us
  transfers between devices with their start and end apart: 11, of which 4 were waited for; matrix products, arithmetic and copies ran while one was open for 0% of the time, Pallas kernels for 26%

profile of v3, /device:TPU:6, one launch (start us, length us, event | category | flops | bytes accessed | tf_op | source)
XLA Modules:
  0.0 88.6 jit_solution(11005257488500482807)
XLA Ops:
  1.9 0.0 copy-start
  1.9 0.0 copy-start.1
  1.9 4.0 %shard_map.77 = (f32[8,6144]{1,0:T(8,128)}, f32[8,6144]{1,0:T(8,128)}, f32[8,32,1280]{2,1,0:T(8,128)}) custom-call(s32[1]{0:T(128)S(6)} %copy.12.level, s32[1]{0:T(128)S(6)} %copy.13.shift, f32[8,128,1024]{2,1,0:T(8,128)} %refs_0_.8, f32[8,128,1024]{2,1,0:T(8,128)} %refs_0_.8, f32[8,128,1024]{2,1,0:T(8,128)} %refs_1_.8, f32[8,128,1024]{2,1,0:T(8,128)} %refs_1_.8, ...), custom_call_target="tpu_custom_call" | custom-call | flops 6291456 | bytes 6291456 | tf_op jit(solution)/shard_map/pallas_call | solution.py:377
  5.9 8.3 %all-to-all-start = ((f32[8,32,1280]{2,1,0:T(8,128)}), f32[8,32,1280]{2,1,0:T(8,128)S(1)}, u32[]{:S(2)}, u32[]{:S(2)}) async-start(f32[8,32,1280]{2,1,0:T(8,128)} %get-tuple-element.24), calls=%async_computation | async-start | bytes 2621440 | tf_op jit(solution)/shard_map/all_to_all | solution.py:728
  14.2 0.0 copy-done
  14.2 0.0 copy-done.1
  14.2 1.9 %shard_map.78.refs_1_.refs_5_ = f32[8,1280]{1,0:T(8,128)S(1)} custom-call(s32[1]{0:T(128)S(6)} %copy.12.level, s32[1]{0:T(128)S(6)} %copy.13.shift, f32[16,4096]{1,0:T(8,128)S(1)} %copy-done, f32[16,4096]{1,0:T(8,128)S(1)} %copy-done.1), custom_call_target="tpu_custom_call" | custom-call | flops 4194304 | bytes 4194304 | tf_op jit(solution)/shard_map/pallas_call | solution.py:442
  16.1 0.0 copy-start.10
  16.1 0.0 copy-start.9
  16.1 3.6 %shard_map.79 = (f32[256,1024]{1,0:T(8,128)}, f32[256,1024]{1,0:T(8,128)}) custom-call(s32[1]{0:T(128)S(6)} %copy.12.level, s32[1]{0:T(128)S(6)} %copy.13.shift, f32[8,128,1024]{2,1,0:T(8,128)} %refs_0_.8, f32[8,128,1024]{2,1,0:T(8,128)} %refs_0_.8, f32[8,128,1024]{2,1,0:T(8,128)} %refs_1_.8), custom_call_target="tpu_custom_call" | custom-call | flops 5242880 | bytes 5242880 | tf_op jit(solution)/shard_map/pallas_call | solution.py:136
  19.7 0.0 collective-permute-start.4
  19.7 5.3 %collective-permute-start.5 = (f32[256,1024]{1,0:T(8,128)}, f32[256,1024]{1,0:T(8,128)}, u32[]{:S(2)}, u32[]{:S(2)}) collective-permute-start(f32[256,1024]{1,0:T(8,128)} %get-tuple-element.32), channel_id=1, source_target_pairs={{8,16},{24,32},{40,48},{56,64},{72,80},{88,96},{104,112},{16,8},{3... | collective-permute-start | bytes 3145736 | tf_op jit(solution)/shard_map/ppermute | solution.py:742
  25.0 6.2 %all-to-all-done = f32[8,32,1280]{2,1,0:T(8,128)S(1)} async-done(((f32[8,32,1280]{2,1,0:T(8,128)}), f32[8,32,1280]{2,1,0:T(8,128)S(1)}, u32[]{:S(2)}, u32[]{:S(2)}) %all-to-all-start) | async-done | bytes 1310752 | tf_op jit(solution)/shard_map/all_to_all | solution.py:728
  31.2 1.0 %shard_map.80 = f32[16,8,1280]{2,1,0:T(8,128)} custom-call(s32[1]{0:T(128)S(6)} %copy.12.level, s32[1]{0:T(128)S(6)} %copy.13.shift, f32[256,1280]{1,0:T(8,128)S(1)} %bitcast.1, f32[8,1280]{1,0:T(8,128)S(1)} %shard_map.78.refs_1_.refs_5_), custom_call_target="tpu_custom_call" | custom-call | flops 2097152 | bytes 2097152 | tf_op jit(solution)/shard_map/pallas_call | solution.py:488
  32.3 6.0 %all-to-all-start.1 = ((f32[16,8,1280]{2,1,0:T(8,128)}), f32[16,8,1280]{2,1,0:T(8,128)S(1)}, u32[]{:S(2)}, u32[]{:S(2)}) async-start(f32[16,8,1280]{2,1,0:T(8,128)} %shard_map.80), calls=%async_computation.1 | async-start | bytes 1310720 | tf_op jit(solution)/shard_map/all_to_all | solution.py:744
  38.2 0.0 copy-done.10
  38.2 2.8 %collective-permute-start.2 = (f32[8,6144]{1,0:T(8,128)S(1)}, f32[8,6144]{1,0:T(8,128)S(1)}, u32[]{:S(2)}, u32[]{:S(2)}) collective-permute-start(f32[8,6144]{1,0:T(8,128)S(1)} %copy-done.10), channel_id=1, source_target_pairs={{0,1},{1,2},{2,3},{3,4},{4,5},{5,6},{6,7},{7,8},{8,9},{9,10},{10,1... | collective-permute-start | bytes 589832 | tf_op jit(solution)/shard_map/ppermute | solution.py:729
  41.0 0.0 copy-done.9
  41.0 6.7 %collective-permute-start.3 = (f32[8,6144]{1,0:T(8,128)S(1)}, f32[8,6144]{1,0:T(8,128)S(1)}, u32[]{:S(2)}, u32[]{:S(2)}) collective-permute-start(f32[8,6144]{1,0:T(8,128)S(1)} %copy-done.9), channel_id=1, source_target_pairs={{1,0},{2,1},{3,2},{4,3},{5,4},{6,5},{7,6},{8,7},{9,8},{10,9},{11,1... | collective-permute-start | bytes 589832 | tf_op jit(solution)/shard_map/ppermute | solution.py:730
  47.7 3.8 %collective-permute-start.1 = (f32[8,1280]{1,0:T(8,128)S(1)}, f32[8,1280]{1,0:T(8,128)S(1)}, u32[]{:S(2)}, u32[]{:S(2)}) collective-permute-start(f32[8,1280]{1,0:T(8,128)S(1)} %shard_map.78.refs_1_.refs_5_), channel_id=1, source_target_pairs={{8,16},{24,32},{40,48},{56,64},{72,80},{88,96},{104,112},{16,8},{3... | collective-permute-start | bytes 122888 | tf_op jit(solution)/shard_map/ppermute | solution.py:737
  51.5 4.0 %collective-permute-done.1.refs_3_ = f32[8,1280]{1,0:T(8,128)S(1)} collective-permute-done((f32[8,1280]{1,0:T(8,128)S(1)}, f32[8,1280]{1,0:T(8,128)S(1)}, u32[]{:S(2)}, u32[]{:S(2)}) %collective-permute-start.1) | collective-permute-done | bytes 40992 | tf_op jit(solution)/shard_map/ppermute | solution.py:737
  55.4 0.0 collective-permute-start
  55.4 1.2 %collective-permute-done.refs_2_ = f32[8,1280]{1,0:T(8,128)S(1)} collective-permute-done((f32[8,1280]{1,0:T(8,128)S(1)}, f32[8,1280]{1,0:T(8,128)S(1)}, u32[]{:S(2)}, u32[]{:S(2)}) %collective-permute-start) | collective-permute-done | bytes 40992 | tf_op jit(solution)/shard_map/ppermute | solution.py:736
  56.7 0.0 collective-permute-done.2.refs_4_.refs_0_.refs_2_
  56.7 0.0 copy-start.2
  56.7 0.0 collective-permute-done.3.refs_5_.refs_1_.refs_3_
  56.7 0.0 copy-start.3
  56.7 0.0 collective-permute-done.4.refs_2_
  56.7 0.0 copy-start.6
  56.7 0.0 collective-permute-done.5.refs_3_
  56.7 0.0 all-to-all-done.1.refs_0_
  56.7 0.4 shard_map.84
  57.1 0.0 copy-start.4
  57.1 1.1 %copy-done.4 = f32[8,32,1408]{2,1,0:T(8,128)} copy-done((f32[8,32,1408]{2,1,0:T(8,128)}, f32[8,32,1408]{2,1,0:T(8,128)S(1)}, u32[]{:S(2)}) %copy-start.4) | copy-done | bytes 1441816
  58.3 5.9 %all-to-all-start.2 = ((f32[8,32,1408]{2,1,0:T(8,128)}), f32[8,32,1408]{2,1,0:T(8,128)S(1)}, u32[]{:S(2)}, u32[]{:S(2)}) async-start(f32[8,32,1408]{2,1,0:T(8,128)} %copy-done.4), calls=%async_computation.2 | async-start | bytes 2883584 | tf_op jit(solution)/shard_map/all_to_all | solution.py:753
  64.2 0.1 collective-permute-start.6
  64.2 3.0 %collective-permute-start.7 = (f32[8,1024]{1,0:T(8,128)S(1)}, f32[8,1024]{1,0:T(8,128)S(1)}, u32[]{:S(2)}, u32[]{:S(2)}) collective-permute-start(f32[8,1024]{1,0:T(8,128)S(1)} %get-tuple-element.39), channel_id=1, source_target_pairs={{8,16},{24,32},{40,48},{56,64},{72,80},{88,96},{104,112},{16,8},{3... | collective-permute-start | bytes 98312 | tf_op jit(solution)/shard_map/ppermute | solution.py:748
  67.3 2.8 %shard_map.86 = f32[16,4096]{1,0:T(8,128)} custom-call(s32[1]{0:T(128)S(6)} %copy.12.level, s32[1]{0:T(128)S(6)} %copy.13.shift, f32[16,4096]{1,0:T(8,128)S(1)} %copy-done, f32[16,4096]{1,0:T(8,128)S(1)} %copy-done.1, f32[8,6144]{1,0:T(8,128)S(1)} %collective-permute-done.2.refs_4_.refs_0_.refs_2_, ...), custom_call_target="tpu_custom_call" | custom-call | flops 4194304 | bytes 4194304 | tf_op jit(solution)/shard_map/pallas_call | solution.py:704
  70.0 0.0 copy-done.2
  70.0 0.0 copy-done.3
  70.0 0.0 copy-done.6
  70.0 10.9 %shard_map.81 = (f32[8,128,1024]{2,1,0:T(8,128)}, f32[128,1024]{1,0:T(8,128)}) custom-call(s32[1]{0:T(128)S(6)} %copy.12.level, s32[1]{0:T(128)S(6)} %copy.13.shift, f32[8,128,1024]{2,1,0:T(8,128)} %refs_0_.8, f32[8,128,1024]{2,1,0:T(8,128)} %refs_1_.8, f32[256,1024]{1,0:T(8,128)} %copy-done.6, f32[256,1024]{1,0:T(8,128)} %collective-permute-done.5.refs_3_, ...), custom_call_target="tpu_custom_call" | custom-call | flops 25165824 | bytes 25165824 | tf_op jit(solution)/shard_map/pallas_call | solution.py:291
  80.9 0.0 collective-permute-done.6.refs_1_
  80.9 0.0 copy-start.7
  80.9 0.9 %collective-permute-done.7.refs_2_ = f32[8,1024]{1,0:T(8,128)S(1)} collective-permute-done((f32[8,1024]{1,0:T(8,128)S(1)}, f32[8,1024]{1,0:T(8,128)S(1)}, u32[]{:S(2)}, u32[]{:S(2)}) %collective-permute-start.7) | collective-permute-done | bytes 32800 | tf_op jit(solution)/shard_map/ppermute | solution.py:748
  81.9 0.0 copy-start.8
  81.9 0.0 copy-done.7
  81.9 0.6 copy-done.8
  82.5 0.0 copy-start.5
  82.5 2.9 %shard_map.83.refs_0_ = f32[8,128,1024]{2,1,0:T(8,128)} custom-call(s32[1]{0:T(128)S(6)} %copy.12.level, s32[1]{0:T(128)S(6)} %copy.13.shift, f32[8,128,1024]{2,1,0:T(8,128)} %get-tuple-element.37.refs_0_, f32[8,1024]{1,0:T(8,128)} %copy-done.7, f32[8,1024]{1,0:T(8,128)} %copy-done.8), custom_call_target="tpu_custom_call", output_to_operand_aliasing={{}: (2, {})} | custom-call | flops 1048576 | bytes 1048576 | tf_op jit(solution)/shard_map/pallas_call | solution.py:588
  85.3 0.0 all-to-all-done.2.refs_1_
  85.3 0.0 copy-done.5
  85.4 3.3 %shard_map.85 = f32[8,128,1024]{2,1,0:T(8,128)} custom-call(s32[1]{0:T(128)S(6)} %copy.12.level, s32[1]{0:T(128)S(6)} %copy.13.shift, f32[8,128,1024]{2,1,0:T(8,128)} %shard_map.83.refs_0_, f32[8,32,1408]{2,1,0:T(8,128)S(1)} %all-to-all-done.2.refs_1_, f32[128,1024]{1,0:T(8,128)S(1)} %copy-done.5), custom_call_target="tpu_custom_call", output_to_operand_aliasing={{}: (2, {})} | custom-call | flops 4194304 | bytes 4194304 | tf_op jit(solution)/shard_map/pallas_call | solution.py:649
  (1 shorter events, 0.0 us)
Async XLA Ops:
  1.9 12.2 %copy-start = (f32[16,4096]{1,0:T(8,128)S(1)}, f32[16,4096]{1,0:T(8,128)}, u32[]{:S(2)}) copy-start(f32[16,4096]{1,0:T(8,128)} %refs_0_.9) | copy-start | bytes 786436
  1.9 12.2 %copy-start.1 = (f32[16,4096]{1,0:T(8,128)S(1)}, f32[16,4096]{1,0:T(8,128)}, u32[]{:S(2)}) copy-start(f32[16,4096]{1,0:T(8,128)} %refs_1_.9) | copy-start | bytes 786436
  5.9 25.3 %all-to-all-start = ((f32[8,32,1280]{2,1,0:T(8,128)}), f32[8,32,1280]{2,1,0:T(8,128)S(1)}, u32[]{:S(2)}, u32[]{:S(2)}) async-start(f32[8,32,1280]{2,1,0:T(8,128)} %get-tuple-element.24), calls=%async_computation | async-start | bytes 2621440 | tf_op jit(solution)/shard_map/all_to_all | solution.py:728
  16.1 22.1 %copy-start.10 = (f32[8,6144]{1,0:T(8,128)S(1)}, f32[8,6144]{1,0:T(8,128)}, u32[]{:S(2)}) copy-start(f32[8,6144]{1,0:T(8,128)} %get-tuple-element.29) | copy-start | bytes 589828
  16.1 24.9 %copy-start.9 = (f32[8,6144]{1,0:T(8,128)S(1)}, f32[8,6144]{1,0:T(8,128)}, u32[]{:S(2)}) copy-start(f32[8,6144]{1,0:T(8,128)} %get-tuple-element.30) | copy-start | bytes 589828
  19.7 37.0 %collective-permute-start.4 = (f32[256,1024]{1,0:T(8,128)}, f32[256,1024]{1,0:T(8,128)S(1)}, u32[]{:S(2)}, u32[]{:S(2)}) collective-permute-start(f32[256,1024]{1,0:T(8,128)} %get-tuple-element.31), channel_id=1, source_target_pairs={{0,8},{8,0},{16,24},{24,16},{32,40},{40,32},{48,56},{56,48},{64,72... | collective-permute-start | bytes 3145736 | tf_op jit(solution)/shard_map/ppermute | solution.py:741
  19.7 37.0 %collective-permute-start.5 = (f32[256,1024]{1,0:T(8,128)}, f32[256,1024]{1,0:T(8,128)}, u32[]{:S(2)}, u32[]{:S(2)}) collective-permute-start(f32[256,1024]{1,0:T(8,128)} %get-tuple-element.32), channel_id=1, source_target_pairs={{8,16},{24,32},{40,48},{56,64},{72,80},{88,96},{104,112},{16,8},{3... | collective-permute-start | bytes 3145736 | tf_op jit(solution)/shard_map/ppermute | solution.py:742
  32.3 24.5 %all-to-all-start.1 = ((f32[16,8,1280]{2,1,0:T(8,128)}), f32[16,8,1280]{2,1,0:T(8,128)S(1)}, u32[]{:S(2)}, u32[]{:S(2)}) async-start(f32[16,8,1280]{2,1,0:T(8,128)} %shard_map.80), calls=%async_computation.1 | async-start | bytes 1310720 | tf_op jit(solution)/shard_map/all_to_all | solution.py:744
  38.2 18.4 %collective-permute-start.2 = (f32[8,6144]{1,0:T(8,128)S(1)}, f32[8,6144]{1,0:T(8,128)S(1)}, u32[]{:S(2)}, u32[]{:S(2)}) collective-permute-start(f32[8,6144]{1,0:T(8,128)S(1)} %copy-done.10), channel_id=1, source_target_pairs={{0,1},{1,2},{2,3},{3,4},{4,5},{5,6},{6,7},{7,8},{8,9},{9,10},{10,1... | collective-permute-start | bytes 589832 | tf_op jit(solution)/shard_map/ppermute | solution.py:729
  41.0 15.7 %collective-permute-start.3 = (f32[8,6144]{1,0:T(8,128)S(1)}, f32[8,6144]{1,0:T(8,128)S(1)}, u32[]{:S(2)}, u32[]{:S(2)}) collective-permute-start(f32[8,6144]{1,0:T(8,128)S(1)} %copy-done.9), channel_id=1, source_target_pairs={{1,0},{2,1},{3,2},{4,3},{5,4},{6,5},{7,6},{8,7},{9,8},{10,9},{11,1... | collective-permute-start | bytes 589832 | tf_op jit(solution)/shard_map/ppermute | solution.py:730
  47.7 7.7 %collective-permute-start.1 = (f32[8,1280]{1,0:T(8,128)S(1)}, f32[8,1280]{1,0:T(8,128)S(1)}, u32[]{:S(2)}, u32[]{:S(2)}) collective-permute-start(f32[8,1280]{1,0:T(8,128)S(1)} %shard_map.78.refs_1_.refs_5_), channel_id=1, source_target_pairs={{8,16},{24,32},{40,48},{56,64},{72,80},{88,96},{104,112},{16,8},{3... | collective-permute-start | bytes 122888 | tf_op jit(solution)/shard_map/ppermute | solution.py:737
  55.4 1.2 %collective-permute-start = (f32[8,1280]{1,0:T(8,128)S(1)}, f32[8,1280]{1,0:T(8,128)S(1)}, u32[]{:S(2)}, u32[]{:S(2)}) collective-permute-start(f32[8,1280]{1,0:T(8,128)S(1)} %shard_map.78.refs_1_.refs_5_), channel_id=1, source_target_pairs={{0,8},{8,0},{16,24},{24,16},{32,40},{40,32},{48,56},{56,48},{64,72... | collective-permute-start | bytes 122888 | tf_op jit(solution)/shard_map/ppermute | solution.py:736
  56.7 13.4 %copy-start.2 = (f32[8,6144]{1,0:T(8,128)}, f32[8,6144]{1,0:T(8,128)S(1)}, u32[]{:S(2)}) copy-start(f32[8,6144]{1,0:T(8,128)S(1)} %collective-permute-done.2.refs_4_.refs_0_.refs_2_) | copy-start | bytes 589828
  56.7 13.4 %copy-start.3 = (f32[8,6144]{1,0:T(8,128)}, f32[8,6144]{1,0:T(8,128)S(1)}, u32[]{:S(2)}) copy-start(f32[8,6144]{1,0:T(8,128)S(1)} %collective-permute-done.3.refs_5_.refs_1_.refs_3_) | copy-start | bytes 589828
  56.7 13.3 %copy-start.6 = (f32[256,1024]{1,0:T(8,128)}, f32[256,1024]{1,0:T(8,128)S(1)}, u32[]{:S(2)}) copy-start(f32[256,1024]{1,0:T(8,128)S(1)} %collective-permute-done.4.refs_2_) | copy-start | bytes 3145732
  57.1 1.1 %copy-start.4 = (f32[8,32,1408]{2,1,0:T(8,128)}, f32[8,32,1408]{2,1,0:T(8,128)S(1)}, u32[]{:S(2)}) copy-start(f32[8,32,1408]{2,1,0:T(8,128)S(1)} %get-tuple-element.43) | copy-start | bytes 4325380
  58.3 27.1 %all-to-all-start.2 = ((f32[8,32,1408]{2,1,0:T(8,128)}), f32[8,32,1408]{2,1,0:T(8,128)S(1)}, u32[]{:S(2)}, u32[]{:S(2)}) async-start(f32[8,32,1408]{2,1,0:T(8,128)} %copy-done.4), calls=%async_computation.2 | async-start | bytes 2883584 | tf_op jit(solution)/shard_map/all_to_all | solution.py:753
  64.2 16.8 %collective-permute-start.6 = (f32[8,1024]{1,0:T(8,128)S(1)}, f32[8,1024]{1,0:T(8,128)S(1)}, u32[]{:S(2)}, u32[]{:S(2)}) collective-permute-start(f32[8,1024]{1,0:T(8,128)S(1)} %get-tuple-element.38), channel_id=1, source_target_pairs={{0,8},{8,0},{16,24},{24,16},{32,40},{40,32},{48,56},{56,48},{64,72... | collective-permute-start | bytes 98312 | tf_op jit(solution)/shard_map/ppermute | solution.py:747
  64.2 17.6 %collective-permute-start.7 = (f32[8,1024]{1,0:T(8,128)S(1)}, f32[8,1024]{1,0:T(8,128)S(1)}, u32[]{:S(2)}, u32[]{:S(2)}) collective-permute-start(f32[8,1024]{1,0:T(8,128)S(1)} %get-tuple-element.39), channel_id=1, source_target_pairs={{8,16},{24,32},{40,48},{56,64},{72,80},{88,96},{104,112},{16,8},{3... | collective-permute-start | bytes 98312 | tf_op jit(solution)/shard_map/ppermute | solution.py:748
  80.9 0.9 %copy-start.7 = (f32[8,1024]{1,0:T(8,128)}, f32[8,1024]{1,0:T(8,128)S(1)}, u32[]{:S(2)}) copy-start(f32[8,1024]{1,0:T(8,128)S(1)} %collective-permute-done.6.refs_1_) | copy-start | bytes 98308
  81.9 0.6 copy-start.8
  82.5 2.9 %copy-start.5 = (f32[128,1024]{1,0:T(8,128)S(1)}, f32[128,1024]{1,0:T(8,128)}, u32[]{:S(2)}) copy-start(f32[128,1024]{1,0:T(8,128)} %get-tuple-element.44.refs_2_) | copy-start | bytes 1572868

commit v4 on v3

--- a/solution.py
+++ b/solution.py
@@ -566,29 +566,32 @@
 
 
 def add_corner_kernel(scal, field, on_chip, off_chip, out):
-    t = pl.program_id(0)
     lower_core = (scal[5] & 1) == 0
-    low = t < 2
-    first_end = (t & 1) == 0
-    near = jnp.where(jnp.logical_not(jnp.logical_xor(low, lower_core)), off_chip[...], on_chip[...])
-    line = jnp.where(first_end, near[0:1], near[1:2])
-    row = iota(out.shape[1:], 0)
+    first_end = pl.program_id(0) == 0
+    depth = field.shape[0]
+    row = iota(field.shape[1:], 0)
     spot = jnp.where(first_end, 0, 7)
-    out[0] = field[0] + jnp.where(row == spot, 0.18 * line, 0.0)
+
+    def line(near):
+        return jnp.where(row == spot, 0.18 * jnp.where(first_end, near[0:1], near[1:2]), 0.0)
+
+    below = line(jnp.where(lower_core, off_chip[...], on_chip[...]))
+    above = line(jnp.where(lower_core, on_chip[...], off_chip[...]))
+    out[0] = field[0] + below
+    for z in range(1, depth - 1):
+        out[z] = field[z]
+    out[depth - 1] = field[depth - 1] + above
 
 
 def add_corners(scal, field, on_chip, off_chip):
     depth, height, width = field.shape
 
-    def where(t, *scal):
-        return ((t >> 1) * (depth - 1), (t & 1) * (height // 8 - 1), 0)
-
-    tile = pl.BlockSpec((1, 8, width), where)
+    tile = pl.BlockSpec((depth, 8, width), lambda t, *scal: (0, t * (height // 8 - 1), 0))
     pack = pl.BlockSpec((8, width), lambda t, *scal: (0, 0))
     return pl.pallas_call(
         placed(add_corner_kernel),
         grid_spec=pltpu.PrefetchScalarGridSpec(
-            num_scalar_prefetch=2, grid=(4,), in_specs=[tile, pack, pack], out_specs=tile
+            num_scalar_prefetch=2, grid=(2,), in_specs=[tile, pack, pack], out_specs=tile
         ),
         out_shape=jax.ShapeDtypeStruct(field.shape, F32),
         input_output_aliases={2: 0},

time: 90 us -> 88.2 us (0.980)
  Pallas kernels: 30.7 us -> 29.7 us
    pallas_call x1, Pallas kernels: 2.87 us -> 1.86 us  [add_corners(): pl.pallas_call(placed(add_corner_kernel), grid_spec=pltpu.PrefetchScalarG...]
  transfers between devices with their start and end apart: 11 -> 11, of which waited for: 4 -> 4; matrix products, arithmetic and copies ran while one was open for 0% -> 0% of each run, Pallas kernels for 26% -> 25%
where the time goes in v4:
time: 88.2 us; the launch traced here: 87.6 us
  starting transfers between devices  41.7 us (47%)
  Pallas kernels  29.7 us (34%)
  waiting for transfers between devices  12.3 us (14%)
  between operations  2.1 us (2%)
  local copies, waits for them, and re-layouts  1.74 us (2%)
    pallas_call x1, Pallas kernels, air_steps(): pl.pallas_call(placed(air_kernel), grid_spec=pltpu.PrefetchScalarGridSpec...  10.9 us
    all_to_all x1, starting transfers between devices, shards(): came = lax.all_to_all(sent, 'gy', 0, 0).reshape(256, width + 256)  8.28 us
    ppermute x1, starting transfers between devices, shards(): hi = lax.ppermute(first, ('gz', 'gy'), down_d)  6.69 us
    all_to_all x1, waiting for transfers between devices, shards(): came = lax.all_to_all(sent, 'gy', 0, 0).reshape(256, width + 256)  6.22 us
    all_to_all x1, starting transfers between devices, shards(): came = lax.all_to_all(to_plate(scal, came, motion), 'gz', 0, 0)  5.95 us
    all_to_all x1, starting transfers between devices, shards(): came = lax.all_to_all(sent, 'gy', 0, 0)  5.89 us
    ppermute x1, starting transfers between devices, shards(): off_chip = lax.ppermute(off_chip, 'gz', pairs_off)  5.29 us
    pallas_call x1, Pallas kernels, front(): pl.pallas_call(placed(front_kernel), grid_spec=pltpu.PrefetchScalarGridSp...  3.96 us
  transfers between devices with their start and end apart: 11, of which 4 were waited for; matrix products, arithmetic and copies ran while one was open for 0% of the time, Pallas kernels for 25%

profile of v4, /device:TPU:6, one launch (start us, length us, event | category | flops | bytes accessed | tf_op | source)
XLA Modules:
  0.0 87.6 jit_solution(13844911368908737821)
XLA Ops:
  1.9 0.0 copy-start
  1.9 0.0 copy-start.1
  1.9 4.0 %shard_map.77 = (f32[8,6144]{1,0:T(8,128)}, f32[8,6144]{1,0:T(8,128)}, f32[8,32,1280]{2,1,0:T(8,128)}) custom-call(s32[1]{0:T(128)S(6)} %copy.12.level, s32[1]{0:T(128)S(6)} %copy.13.shift, f32[8,128,1024]{2,1,0:T(8,128)} %refs_0_.8, f32[8,128,1024]{2,1,0:T(8,128)} %refs_0_.8, f32[8,128,1024]{2,1,0:T(8,128)} %refs_1_.8, f32[8,128,1024]{2,1,0:T(8,128)} %refs_1_.8, ...), custom_call_target="tpu_custom_call" | custom-call | flops 6291456 | bytes 6291456 | tf_op jit(solution)/shard_map/pallas_call | solution.py:377
  5.9 8.3 %all-to-all-start = ((f32[8,32,1280]{2,1,0:T(8,128)}), f32[8,32,1280]{2,1,0:T(8,128)S(1)}, u32[]{:S(2)}, u32[]{:S(2)}) async-start(f32[8,32,1280]{2,1,0:T(8,128)} %get-tuple-element.24), calls=%async_computation | async-start | bytes 2621440 | tf_op jit(solution)/shard_map/all_to_all | solution.py:731
  14.2 0.0 copy-done
  14.2 0.0 copy-done.1
  14.2 1.9 %shard_map.78.refs_1_.refs_5_ = f32[8,1280]{1,0:T(8,128)S(1)} custom-call(s32[1]{0:T(128)S(6)} %copy.12.level, s32[1]{0:T(128)S(6)} %copy.13.shift, f32[16,4096]{1,0:T(8,128)S(1)} %copy-done, f32[16,4096]{1,0:T(8,128)S(1)} %copy-done.1), custom_call_target="tpu_custom_call" | custom-call | flops 4194304 | bytes 4194304 | tf_op jit(solution)/shard_map/pallas_call | solution.py:442
  16.1 0.0 copy-start.10
  16.1 0.0 copy-start.9
  16.1 3.6 %shard_map.79 = (f32[256,1024]{1,0:T(8,128)}, f32[256,1024]{1,0:T(8,128)}) custom-call(s32[1]{0:T(128)S(6)} %copy.12.level, s32[1]{0:T(128)S(6)} %copy.13.shift, f32[8,128,1024]{2,1,0:T(8,128)} %refs_0_.8, f32[8,128,1024]{2,1,0:T(8,128)} %refs_0_.8, f32[8,128,1024]{2,1,0:T(8,128)} %refs_1_.8), custom_call_target="tpu_custom_call" | custom-call | flops 5242880 | bytes 5242880 | tf_op jit(solution)/shard_map/pallas_call | solution.py:136
  19.7 0.0 collective-permute-start.4
  19.7 5.3 %collective-permute-start.5 = (f32[256,1024]{1,0:T(8,128)}, f32[256,1024]{1,0:T(8,128)}, u32[]{:S(2)}, u32[]{:S(2)}) collective-permute-start(f32[256,1024]{1,0:T(8,128)} %get-tuple-element.32), channel_id=1, source_target_pairs={{8,16},{24,32},{40,48},{56,64},{72,80},{88,96},{104,112},{16,8},{3... | collective-permute-start | bytes 3145736 | tf_op jit(solution)/shard_map/ppermute | solution.py:745
  25.0 6.2 %all-to-all-done = f32[8,32,1280]{2,1,0:T(8,128)S(1)} async-done(((f32[8,32,1280]{2,1,0:T(8,128)}), f32[8,32,1280]{2,1,0:T(8,128)S(1)}, u32[]{:S(2)}, u32[]{:S(2)}) %all-to-all-start) | async-done | bytes 1310752 | tf_op jit(solution)/shard_map/all_to_all | solution.py:731
  31.2 1.0 %shard_map.80 = f32[16,8,1280]{2,1,0:T(8,128)} custom-call(s32[1]{0:T(128)S(6)} %copy.12.level, s32[1]{0:T(128)S(6)} %copy.13.shift, f32[256,1280]{1,0:T(8,128)S(1)} %bitcast.1, f32[8,1280]{1,0:T(8,128)S(1)} %shard_map.78.refs_1_.refs_5_), custom_call_target="tpu_custom_call" | custom-call | flops 2097152 | bytes 2097152 | tf_op jit(solution)/shard_map/pallas_call | solution.py:488
  32.3 5.9 %all-to-all-start.1 = ((f32[16,8,1280]{2,1,0:T(8,128)}), f32[16,8,1280]{2,1,0:T(8,128)S(1)}, u32[]{:S(2)}, u32[]{:S(2)}) async-start(f32[16,8,1280]{2,1,0:T(8,128)} %shard_map.80), calls=%async_computation.1 | async-start | bytes 1310720 | tf_op jit(solution)/shard_map/all_to_all | solution.py:747
  38.2 0.0 copy-done.10
  38.2 2.8 %collective-permute-start.2 = (f32[8,6144]{1,0:T(8,128)S(1)}, f32[8,6144]{1,0:T(8,128)S(1)}, u32[]{:S(2)}, u32[]{:S(2)}) collective-permute-start(f32[8,6144]{1,0:T(8,128)S(1)} %copy-done.10), channel_id=1, source_target_pairs={{0,1},{1,2},{2,3},{3,4},{4,5},{5,6},{6,7},{7,8},{8,9},{9,10},{10,1... | collective-permute-start | bytes 589832 | tf_op jit(solution)/shard_map/ppermute | solution.py:732
  41.0 0.0 copy-done.9
  41.0 6.7 %collective-permute-start.3 = (f32[8,6144]{1,0:T(8,128)S(1)}, f32[8,6144]{1,0:T(8,128)S(1)}, u32[]{:S(2)}, u32[]{:S(2)}) collective-permute-start(f32[8,6144]{1,0:T(8,128)S(1)} %copy-done.9), channel_id=1, source_target_pairs={{1,0},{2,1},{3,2},{4,3},{5,4},{6,5},{7,6},{8,7},{9,8},{10,9},{11,1... | collective-permute-start | bytes 589832 | tf_op jit(solution)/shard_map/ppermute | solution.py:733
  47.7 3.8 %collective-permute-start.1 = (f32[8,1280]{1,0:T(8,128)S(1)}, f32[8,1280]{1,0:T(8,128)S(1)}, u32[]{:S(2)}, u32[]{:S(2)}) collective-permute-start(f32[8,1280]{1,0:T(8,128)S(1)} %shard_map.78.refs_1_.refs_5_), channel_id=1, source_target_pairs={{8,16},{24,32},{40,48},{56,64},{72,80},{88,96},{104,112},{16,8},{3... | collective-permute-start | bytes 122888 | tf_op jit(solution)/shard_map/ppermute | solution.py:740
  51.5 4.0 %collective-permute-done.1.refs_3_ = f32[8,1280]{1,0:T(8,128)S(1)} collective-permute-done((f32[8,1280]{1,0:T(8,128)S(1)}, f32[8,1280]{1,0:T(8,128)S(1)}, u32[]{:S(2)}, u32[]{:S(2)}) %collective-permute-start.1) | collective-permute-done | bytes 40992 | tf_op jit(solution)/shard_map/ppermute | solution.py:740
  55.4 0.0 collective-permute-start
  55.4 1.2 %collective-permute-done.refs_2_ = f32[8,1280]{1,0:T(8,128)S(1)} collective-permute-done((f32[8,1280]{1,0:T(8,128)S(1)}, f32[8,1280]{1,0:T(8,128)S(1)}, u32[]{:S(2)}, u32[]{:S(2)}) %collective-permute-start) | collective-permute-done | bytes 40992 | tf_op jit(solution)/shard_map/ppermute | solution.py:739
  56.7 0.0 collective-permute-done.2.refs_4_.refs_0_.refs_2_
  56.7 0.0 copy-start.2
  56.7 0.0 collective-permute-done.3.refs_5_.refs_1_.refs_3_
  56.7 0.0 copy-start.3
  56.7 0.0 collective-permute-done.4.refs_2_
  56.7 0.0 copy-start.6
  56.7 0.0 collective-permute-done.5.refs_3_
  56.7 0.0 all-to-all-done.1.refs_0_
  56.7 0.4 shard_map.84
  57.1 0.0 copy-start.4
  57.1 1.1 %copy-done.4 = f32[8,32,1408]{2,1,0:T(8,128)} copy-done((f32[8,32,1408]{2,1,0:T(8,128)}, f32[8,32,1408]{2,1,0:T(8,128)S(1)}, u32[]{:S(2)}) %copy-start.4) | copy-done | bytes 1441816
  58.3 5.9 %all-to-all-start.2 = ((f32[8,32,1408]{2,1,0:T(8,128)}), f32[8,32,1408]{2,1,0:T(8,128)S(1)}, u32[]{:S(2)}, u32[]{:S(2)}) async-start(f32[8,32,1408]{2,1,0:T(8,128)} %copy-done.4), calls=%async_computation.2 | async-start | bytes 2883584 | tf_op jit(solution)/shard_map/all_to_all | solution.py:756
  64.2 0.1 collective-permute-start.6
  64.3 3.0 %collective-permute-start.7 = (f32[8,1024]{1,0:T(8,128)S(1)}, f32[8,1024]{1,0:T(8,128)S(1)}, u32[]{:S(2)}, u32[]{:S(2)}) collective-permute-start(f32[8,1024]{1,0:T(8,128)S(1)} %get-tuple-element.39), channel_id=1, source_target_pairs={{8,16},{24,32},{40,48},{56,64},{72,80},{88,96},{104,112},{16,8},{3... | collective-permute-start | bytes 98312 | tf_op jit(solution)/shard_map/ppermute | solution.py:751
  67.3 2.8 %shard_map.86 = f32[16,4096]{1,0:T(8,128)} custom-call(s32[1]{0:T(128)S(6)} %copy.12.level, s32[1]{0:T(128)S(6)} %copy.13.shift, f32[16,4096]{1,0:T(8,128)S(1)} %copy-done, f32[16,4096]{1,0:T(8,128)S(1)} %copy-done.1, f32[8,6144]{1,0:T(8,128)S(1)} %collective-permute-done.2.refs_4_.refs_0_.refs_2_, ...), custom_call_target="tpu_custom_call" | custom-call | flops 4194304 | bytes 4194304 | tf_op jit(solution)/shard_map/pallas_call | solution.py:707
  70.0 0.0 copy-done.2
  70.0 0.0 copy-done.3
  70.0 0.0 copy-done.6
  70.0 10.9 %shard_map.81 = (f32[8,128,1024]{2,1,0:T(8,128)}, f32[128,1024]{1,0:T(8,128)}) custom-call(s32[1]{0:T(128)S(6)} %copy.12.level, s32[1]{0:T(128)S(6)} %copy.13.shift, f32[8,128,1024]{2,1,0:T(8,128)} %refs_0_.8, f32[8,128,1024]{2,1,0:T(8,128)} %refs_1_.8, f32[256,1024]{1,0:T(8,128)} %copy-done.6, f32[256,1024]{1,0:T(8,128)} %collective-permute-done.5.refs_3_, ...), custom_call_target="tpu_custom_call" | custom-call | flops 25165824 | bytes 25165824 | tf_op jit(solution)/shard_map/pallas_call | solution.py:291
  80.9 0.0 collective-permute-done.6.refs_1_
  80.9 0.0 copy-start.7
  80.9 0.9 %collective-permute-done.7.refs_2_ = f32[8,1024]{1,0:T(8,128)S(1)} collective-permute-done((f32[8,1024]{1,0:T(8,128)S(1)}, f32[8,1024]{1,0:T(8,128)S(1)}, u32[]{:S(2)}, u32[]{:S(2)}) %collective-permute-start.7) | collective-permute-done | bytes 32800 | tf_op jit(solution)/shard_map/ppermute | solution.py:751
  81.9 0.0 copy-start.8
  81.9 0.0 copy-done.7
  81.9 0.6 copy-done.8
  82.5 0.0 copy-start.5
  82.5 1.9 %shard_map.83.refs_0_ = f32[8,128,1024]{2,1,0:T(8,128)} custom-call(s32[1]{0:T(128)S(6)} %copy.12.level, s32[1]{0:T(128)S(6)} %copy.13.shift, f32[8,128,1024]{2,1,0:T(8,128)} %get-tuple-element.37.refs_0_, f32[8,1024]{1,0:T(8,128)} %copy-done.7, f32[8,1024]{1,0:T(8,128)} %copy-done.8), custom_call_target="tpu_custom_call", output_to_operand_aliasing={{}: (2, {})} | custom-call | flops 1048576 | bytes 1048576 | tf_op jit(solution)/shard_map/pallas_call | solution.py:591
  84.3 0.0 all-to-all-done.2.refs_1_
  84.3 0.0 copy-done.5
  84.3 3.3 %shard_map.85 = f32[8,128,1024]{2,1,0:T(8,128)} custom-call(s32[1]{0:T(128)S(6)} %copy.12.level, s32[1]{0:T(128)S(6)} %copy.13.shift, f32[8,128,1024]{2,1,0:T(8,128)} %shard_map.83.refs_0_, f32[8,32,1408]{2,1,0:T(8,128)S(1)} %all-to-all-done.2.refs_1_, f32[128,1024]{1,0:T(8,128)S(1)} %copy-done.5), custom_call_target="tpu_custom_call", output_to_operand_aliasing={{}: (2, {})} | custom-call | flops 4194304 | bytes 4194304 | tf_op jit(solution)/shard_map/pallas_call | solution.py:652
  (1 shorter events, 0.0 us)
Async XLA Ops:
  1.9 12.3 %copy-start = (f32[16,4096]{1,0:T(8,128)S(1)}, f32[16,4096]{1,0:T(8,128)}, u32[]{:S(2)}) copy-start(f32[16,4096]{1,0:T(8,128)} %refs_0_.9) | copy-start | bytes 786436
  1.9 12.2 %copy-start.1 = (f32[16,4096]{1,0:T(8,128)S(1)}, f32[16,4096]{1,0:T(8,128)}, u32[]{:S(2)}) copy-start(f32[16,4096]{1,0:T(8,128)} %refs_1_.9) | copy-start | bytes 786436
  5.9 25.3 %all-to-all-start = ((f32[8,32,1280]{2,1,0:T(8,128)}), f32[8,32,1280]{2,1,0:T(8,128)S(1)}, u32[]{:S(2)}, u32[]{:S(2)}) async-start(f32[8,32,1280]{2,1,0:T(8,128)} %get-tuple-element.24), calls=%async_computation | async-start | bytes 2621440 | tf_op jit(solution)/shard_map/all_to_all | solution.py:731
  16.1 22.1 %copy-start.10 = (f32[8,6144]{1,0:T(8,128)S(1)}, f32[8,6144]{1,0:T(8,128)}, u32[]{:S(2)}) copy-start(f32[8,6144]{1,0:T(8,128)} %get-tuple-element.29) | copy-start | bytes 589828
  16.1 24.9 %copy-start.9 = (f32[8,6144]{1,0:T(8,128)S(1)}, f32[8,6144]{1,0:T(8,128)}, u32[]{:S(2)}) copy-start(f32[8,6144]{1,0:T(8,128)} %get-tuple-element.30) | copy-start | bytes 589828
  19.7 37.0 %collective-permute-start.4 = (f32[256,1024]{1,0:T(8,128)}, f32[256,1024]{1,0:T(8,128)S(1)}, u32[]{:S(2)}, u32[]{:S(2)}) collective-permute-start(f32[256,1024]{1,0:T(8,128)} %get-tuple-element.31), channel_id=1, source_target_pairs={{0,8},{8,0},{16,24},{24,16},{32,40},{40,32},{48,56},{56,48},{64,72... | collective-permute-start | bytes 3145736 | tf_op jit(solution)/shard_map/ppermute | solution.py:744
  19.7 37.0 %collective-permute-start.5 = (f32[256,1024]{1,0:T(8,128)}, f32[256,1024]{1,0:T(8,128)}, u32[]{:S(2)}, u32[]{:S(2)}) collective-permute-start(f32[256,1024]{1,0:T(8,128)} %get-tuple-element.32), channel_id=1, source_target_pairs={{8,16},{24,32},{40,48},{56,64},{72,80},{88,96},{104,112},{16,8},{3... | collective-permute-start | bytes 3145736 | tf_op jit(solution)/shard_map/ppermute | solution.py:745
  32.3 24.4 %all-to-all-start.1 = ((f32[16,8,1280]{2,1,0:T(8,128)}), f32[16,8,1280]{2,1,0:T(8,128)S(1)}, u32[]{:S(2)}, u32[]{:S(2)}) async-start(f32[16,8,1280]{2,1,0:T(8,128)} %shard_map.80), calls=%async_computation.1 | async-start | bytes 1310720 | tf_op jit(solution)/shard_map/all_to_all | solution.py:747
  38.2 18.4 %collective-permute-start.2 = (f32[8,6144]{1,0:T(8,128)S(1)}, f32[8,6144]{1,0:T(8,128)S(1)}, u32[]{:S(2)}, u32[]{:S(2)}) collective-permute-start(f32[8,6144]{1,0:T(8,128)S(1)} %copy-done.10), channel_id=1, source_target_pairs={{0,1},{1,2},{2,3},{3,4},{4,5},{5,6},{6,7},{7,8},{8,9},{9,10},{10,1... | collective-permute-start | bytes 589832 | tf_op jit(solution)/shard_map/ppermute | solution.py:732
  41.0 15.7 %collective-permute-start.3 = (f32[8,6144]{1,0:T(8,128)S(1)}, f32[8,6144]{1,0:T(8,128)S(1)}, u32[]{:S(2)}, u32[]{:S(2)}) collective-permute-start(f32[8,6144]{1,0:T(8,128)S(1)} %copy-done.9), channel_id=1, source_target_pairs={{1,0},{2,1},{3,2},{4,3},{5,4},{6,5},{7,6},{8,7},{9,8},{10,9},{11,1... | collective-permute-start | bytes 589832 | tf_op jit(solution)/shard_map/ppermute | solution.py:733
  47.7 7.7 %collective-permute-start.1 = (f32[8,1280]{1,0:T(8,128)S(1)}, f32[8,1280]{1,0:T(8,128)S(1)}, u32[]{:S(2)}, u32[]{:S(2)}) collective-permute-start(f32[8,1280]{1,0:T(8,128)S(1)} %shard_map.78.refs_1_.refs_5_), channel_id=1, source_target_pairs={{8,16},{24,32},{40,48},{56,64},{72,80},{88,96},{104,112},{16,8},{3... | collective-permute-start | bytes 122888 | tf_op jit(solution)/shard_map/ppermute | solution.py:740
  55.4 1.2 %collective-permute-start = (f32[8,1280]{1,0:T(8,128)S(1)}, f32[8,1280]{1,0:T(8,128)S(1)}, u32[]{:S(2)}, u32[]{:S(2)}) collective-permute-start(f32[8,1280]{1,0:T(8,128)S(1)} %shard_map.78.refs_1_.refs_5_), channel_id=1, source_target_pairs={{0,8},{8,0},{16,24},{24,16},{32,40},{40,32},{48,56},{56,48},{64,72... | collective-permute-start | bytes 122888 | tf_op jit(solution)/shard_map/ppermute | solution.py:739
  56.7 13.4 %copy-start.2 = (f32[8,6144]{1,0:T(8,128)}, f32[8,6144]{1,0:T(8,128)S(1)}, u32[]{:S(2)}) copy-start(f32[8,6144]{1,0:T(8,128)S(1)} %collective-permute-done.2.refs_4_.refs_0_.refs_2_) | copy-start | bytes 589828
  56.7 13.4 %copy-start.3 = (f32[8,6144]{1,0:T(8,128)}, f32[8,6144]{1,0:T(8,128)S(1)}, u32[]{:S(2)}) copy-start(f32[8,6144]{1,0:T(8,128)S(1)} %collective-permute-done.3.refs_5_.refs_1_.refs_3_) | copy-start | bytes 589828
  56.7 13.3 %copy-start.6 = (f32[256,1024]{1,0:T(8,128)}, f32[256,1024]{1,0:T(8,128)S(1)}, u32[]{:S(2)}) copy-start(f32[256,1024]{1,0:T(8,128)S(1)} %collective-permute-done.4.refs_2_) | copy-start | bytes 3145732
  57.1 1.1 %copy-start.4 = (f32[8,32,1408]{2,1,0:T(8,128)}, f32[8,32,1408]{2,1,0:T(8,128)S(1)}, u32[]{:S(2)}) copy-start(f32[8,32,1408]{2,1,0:T(8,128)S(1)} %get-tuple-element.43) | copy-start | bytes 4325380
  58.3 26.1 %all-to-all-start.2 = ((f32[8,32,1408]{2,1,0:T(8,128)}), f32[8,32,1408]{2,1,0:T(8,128)S(1)}, u32[]{:S(2)}, u32[]{:S(2)}) async-start(f32[8,32,1408]{2,1,0:T(8,128)} %copy-done.4), calls=%async_computation.2 | async-start | bytes 2883584 | tf_op jit(solution)/shard_map/all_to_all | solution.py:756
  64.2 16.8 %collective-permute-start.6 = (f32[8,1024]{1,0:T(8,128)S(1)}, f32[8,1024]{1,0:T(8,128)S(1)}, u32[]{:S(2)}, u32[]{:S(2)}) collective-permute-start(f32[8,1024]{1,0:T(8,128)S(1)} %get-tuple-element.38), channel_id=1, source_target_pairs={{0,8},{8,0},{16,24},{24,16},{32,40},{40,32},{48,56},{56,48},{64,72... | collective-permute-start | bytes 98312 | tf_op jit(solution)/shard_map/ppermute | solution.py:750
  64.3 17.6 %collective-permute-start.7 = (f32[8,1024]{1,0:T(8,128)S(1)}, f32[8,1024]{1,0:T(8,128)S(1)}, u32[]{:S(2)}, u32[]{:S(2)}) collective-permute-start(f32[8,1024]{1,0:T(8,128)S(1)} %get-tuple-element.39), channel_id=1, source_target_pairs={{8,16},{24,32},{40,48},{56,64},{72,80},{88,96},{104,112},{16,8},{3... | collective-permute-start | bytes 98312 | tf_op jit(solution)/shard_map/ppermute | solution.py:751
  80.9 0.9 %copy-start.7 = (f32[8,1024]{1,0:T(8,128)}, f32[8,1024]{1,0:T(8,128)S(1)}, u32[]{:S(2)}) copy-start(f32[8,1024]{1,0:T(8,128)S(1)} %collective-permute-done.6.refs_1_) | copy-start | bytes 98308
  81.9 0.6 copy-start.8
  82.5 1.9 %copy-start.5 = (f32[128,1024]{1,0:T(8,128)S(1)}, f32[128,1024]{1,0:T(8,128)}, u32[]{:S(2)}) copy-start(f32[128,1024]{1,0:T(8,128)} %get-tuple-element.44.refs_2_) | copy-start | bytes 1572868

commit v5 on v3

--- a/solution.py
+++ b/solution.py
@@ -212,13 +212,21 @@
             fetch_now(z).start()
             fetch_prev(z).start()
 
-    @pl.when(t < depth)
-    def _():
-        fetch_now(t).wait()
-
-    @pl.when((t >= 1) & (t <= depth))
-    def _():
-        fetch_prev(t - 1).wait()
+    pairs = depth // 2
+
+    @pl.when(t == 0)
+    def _():
+        fetch_now(0).wait()
+
+    @pl.when(t < pairs)
+    def _():
+        fetch_now(2 * t + 1).wait()
+        fetch_prev(2 * t).wait()
+        fetch_prev(2 * t + 1).wait()
+
+    @pl.when(t < pairs - 1)
+    def _():
+        fetch_now(2 * t + 2).wait()
 
     def outer(target, source, level, inside):
         inside = jnp.where(inside, 1.0, 0.0).astype(F32)
@@ -232,13 +240,11 @@
             keep[depth + 1, at, :] = zhi(8 * i, 8)
         outer(0, zlo, 1, slab > 0)
 
-    @pl.when(t == depth - 1)
+    @pl.when(t == pairs - 1)
     def _():
         outer(depth + 1, zhi, depth, slab < 15)
 
-    @pl.when((t >= 1) & (t <= depth))
-    def _():
-        z = t - 1
+    def first_step(z):
         above = y_lo * ylo[pl.ds(z, 1), 0:width]
         below = y_hi * yhi[pl.ds(z, 1), 0:width]
 
@@ -249,10 +255,7 @@
 
         sweep(lambda i: keep[z + 1, strips[i], :], len(strips), above, below, emit)
 
-    @pl.when(t >= 2)
-    def _():
-        z = t - 2
-
+    def second_step(z, slot):
         def rim(rows, line):
             return rows[pl.ds(z, 1), width : 2 * width] + 0.3 * line
 
@@ -262,11 +265,21 @@
         def emit(i, x, around):
             at = strips[i]
             total = around + mid[z, at, :] + mid[z + 2, at, :]
-            out[0, at, :] = 0.2 * x - keep[z + 1, at, :] + 0.3 * total
+            out[slot, at, :] = 0.2 * x - keep[z + 1, at, :] + 0.3 * total
 
         sweep(lambda i: mid[z + 1, strips[i], :], len(strips), above, below, emit)
 
-    @pl.when(t == depth)
+    @pl.when(t < pairs)
+    def _():
+        first_step(2 * t)
+        first_step(2 * t + 1)
+
+    @pl.when(t >= 1)
+    def _():
+        second_step(2 * t - 2, 0)
+        second_step(2 * t - 1, 1)
+
+    @pl.when(t == pairs)
     def _():
         upper = jnp.clip(level + 1 - first, -1, depth) + 1
         lower = jnp.clip(level - first, -1, depth) + 1
@@ -279,11 +292,9 @@
 def air_steps(scal, now, prev, on_chip, off_chip, ylo, yhi, cols):
     depth, height, width = now.shape
 
-    def plane(lag):
-        return pl.BlockSpec(
-            (1, height, width), lambda t, *scal: (jnp.clip(t - lag, 0, depth - 1), 0, 0)
-        )
-
+    pair = pl.BlockSpec(
+        (2, height, width), lambda t, *scal: (jnp.clip(t - 1, 0, depth // 2 - 1), 0, 0)
+    )
     whole = pl.BlockSpec(memory_space=pl.ANY)
 
     z_face = pl.BlockSpec((2 * height, width), lambda t, *scal: (0, 0))
@@ -292,10 +303,10 @@
         placed(air_kernel),
         grid_spec=pltpu.PrefetchScalarGridSpec(
             num_scalar_prefetch=2,
-            grid=(depth + 2,),
+            grid=(depth // 2 + 1,),
             in_specs=[whole, whole, z_face, z_face, rows, rows],
             out_specs=[
-                plane(2),
+                pair,
                 pl.BlockSpec((height, width), lambda t, *scal: (0, 0)),
             ],
             scratch_shapes=[pltpu.VMEM((depth + 2, height, width), F32)] * 2

time: 90 us -> 89.5 us (level); the launches traced: 88.6 us -> 89.1 us
  no operation moved by 1% of the time
where the time goes in v5:
time: 89.5 us; the launch traced here: 89.1 us
  starting transfers between devices  42.6 us (48%)
  Pallas kernels  30.4 us (34%)
  waiting for transfers between devices  12.2 us (14%)
  between operations  2.1 us (2%)
  local copies, waits for them, and re-layouts  1.74 us (2%)
    pallas_call x1, Pallas kernels, air_steps(): pl.pallas_call(placed(air_kernel), grid_spec=pltpu.PrefetchScalarGridSpec...  10.6 us
    all_to_all x1, starting transfers between devices, shards(): came = lax.all_to_all(sent, 'gy', 0, 0).reshape(256, width + 256)  8.28 us
    ppermute x1, starting transfers between devices, shards(): hi = lax.ppermute(first, ('gz', 'gy'), down_d)  6.69 us
    all_to_all x1, starting transfers between devices, shards(): came = lax.all_to_all(sent, 'gy', 0, 0)  6.35 us
    all_to_all x1, starting transfers between devices, shards(): came = lax.all_to_all(to_plate(scal, came, motion), 'gz', 0, 0)  5.95 us
    all_to_all x1, waiting for transfers between devices, shards(): came = lax.all_to_all(sent, 'gy', 0, 0).reshape(256, width + 256)  5.77 us
    ppermute x1, starting transfers between devices, shards(): off_chip = lax.ppermute(off_chip, 'gz', pairs_off)  5.74 us
    pallas_call x1, Pallas kernels, front(): pl.pallas_call(placed(front_kernel), grid_spec=pltpu.PrefetchScalarGridSp...  3.96 us
  transfers between devices with their start and end apart: 11, of which 4 were waited for; matrix products, arithmetic and copies ran while one was open for 0% of the time, Pallas kernels for 26%

profile of v5, /device:TPU:6, one launch (start us, length us, event | category | flops | bytes accessed | tf_op | source)
XLA Modules:
  0.0 89.1 jit_solution(100208164309003542)
XLA Ops:
  1.9 0.0 copy-start
  1.9 0.0 copy-start.1
  1.9 4.0 %shard_map.77 = (f32[8,6144]{1,0:T(8,128)}, f32[8,6144]{1,0:T(8,128)}, f32[8,32,1280]{2,1,0:T(8,128)}) custom-call(s32[1]{0:T(128)S(6)} %copy.12.level, s32[1]{0:T(128)S(6)} %copy.13.shift, f32[8,128,1024]{2,1,0:T(8,128)} %refs_0_.8, f32[8,128,1024]{2,1,0:T(8,128)} %refs_0_.8, f32[8,128,1024]{2,1,0:T(8,128)} %refs_1_.8, f32[8,128,1024]{2,1,0:T(8,128)} %refs_1_.8, ...), custom_call_target="tpu_custom_call" | custom-call | flops 6291456 | bytes 6291456 | tf_op jit(solution)/shard_map/pallas_call | solution.py:388
  5.9 8.3 %all-to-all-start = ((f32[8,32,1280]{2,1,0:T(8,128)}), f32[8,32,1280]{2,1,0:T(8,128)S(1)}, u32[]{:S(2)}, u32[]{:S(2)}) async-start(f32[8,32,1280]{2,1,0:T(8,128)} %get-tuple-element.24), calls=%async_computation | async-start | bytes 2621440 | tf_op jit(solution)/shard_map/all_to_all | solution.py:739
  14.2 0.0 copy-done
  14.2 0.0 copy-done.1
  14.2 1.9 %shard_map.78.refs_1_.refs_5_ = f32[8,1280]{1,0:T(8,128)S(1)} custom-call(s32[1]{0:T(128)S(6)} %copy.12.level, s32[1]{0:T(128)S(6)} %copy.13.shift, f32[16,4096]{1,0:T(8,128)S(1)} %copy-done, f32[16,4096]{1,0:T(8,128)S(1)} %copy-done.1), custom_call_target="tpu_custom_call" | custom-call | flops 4194304 | bytes 4194304 | tf_op jit(solution)/shard_map/pallas_call | solution.py:453
  16.1 0.0 copy-start.10
  16.1 0.0 copy-start.9
  16.1 3.6 %shard_map.79 = (f32[256,1024]{1,0:T(8,128)}, f32[256,1024]{1,0:T(8,128)}) custom-call(s32[1]{0:T(128)S(6)} %copy.12.level, s32[1]{0:T(128)S(6)} %copy.13.shift, f32[8,128,1024]{2,1,0:T(8,128)} %refs_0_.8, f32[8,128,1024]{2,1,0:T(8,128)} %refs_0_.8, f32[8,128,1024]{2,1,0:T(8,128)} %refs_1_.8), custom_call_target="tpu_custom_call" | custom-call | flops 5242880 | bytes 5242880 | tf_op jit(solution)/shard_map/pallas_call | solution.py:136
  19.7 0.0 collective-permute-start.4
  19.7 5.7 %collective-permute-start.5 = (f32[256,1024]{1,0:T(8,128)}, f32[256,1024]{1,0:T(8,128)}, u32[]{:S(2)}, u32[]{:S(2)}) collective-permute-start(f32[256,1024]{1,0:T(8,128)} %get-tuple-element.32), channel_id=1, source_target_pairs={{8,16},{24,32},{40,48},{56,64},{72,80},{88,96},{104,112},{16,8},{3... | collective-permute-start | bytes 3145736 | tf_op jit(solution)/shard_map/ppermute | solution.py:753
  25.5 5.8 %all-to-all-done = f32[8,32,1280]{2,1,0:T(8,128)S(1)} async-done(((f32[8,32,1280]{2,1,0:T(8,128)}), f32[8,32,1280]{2,1,0:T(8,128)S(1)}, u32[]{:S(2)}, u32[]{:S(2)}) %all-to-all-start) | async-done | bytes 1310752 | tf_op jit(solution)/shard_map/all_to_all | solution.py:739
  31.2 1.0 %shard_map.80 = f32[16,8,1280]{2,1,0:T(8,128)} custom-call(s32[1]{0:T(128)S(6)} %copy.12.level, s32[1]{0:T(128)S(6)} %copy.13.shift, f32[256,1280]{1,0:T(8,128)S(1)} %bitcast.1, f32[8,1280]{1,0:T(8,128)S(1)} %shard_map.78.refs_1_.refs_5_), custom_call_target="tpu_custom_call" | custom-call | flops 2097152 | bytes 2097152 | tf_op jit(solution)/shard_map/pallas_call | solution.py:499
  32.3 5.9 %all-to-all-start.1 = ((f32[16,8,1280]{2,1,0:T(8,128)}), f32[16,8,1280]{2,1,0:T(8,128)S(1)}, u32[]{:S(2)}, u32[]{:S(2)}) async-start(f32[16,8,1280]{2,1,0:T(8,128)} %shard_map.80), calls=%async_computation.1 | async-start | bytes 1310720 | tf_op jit(solution)/shard_map/all_to_all | solution.py:755
  38.2 0.0 copy-done.10
  38.2 2.8 %collective-permute-start.2 = (f32[8,6144]{1,0:T(8,128)S(1)}, f32[8,6144]{1,0:T(8,128)S(1)}, u32[]{:S(2)}, u32[]{:S(2)}) collective-permute-start(f32[8,6144]{1,0:T(8,128)S(1)} %copy-done.10), channel_id=1, source_target_pairs={{0,1},{1,2},{2,3},{3,4},{4,5},{5,6},{6,7},{7,8},{8,9},{9,10},{10,1... | collective-permute-start | bytes 589832 | tf_op jit(solution)/shard_map/ppermute | solution.py:740
  41.0 0.0 copy-done.9
  41.0 6.7 %collective-permute-start.3 = (f32[8,6144]{1,0:T(8,128)S(1)}, f32[8,6144]{1,0:T(8,128)S(1)}, u32[]{:S(2)}, u32[]{:S(2)}) collective-permute-start(f32[8,6144]{1,0:T(8,128)S(1)} %copy-done.9), channel_id=1, source_target_pairs={{1,0},{2,1},{3,2},{4,3},{5,4},{6,5},{7,6},{8,7},{9,8},{10,9},{11,1... | collective-permute-start | bytes 589832 | tf_op jit(solution)/shard_map/ppermute | solution.py:741
  47.7 3.8 %collective-permute-start.1 = (f32[8,1280]{1,0:T(8,128)S(1)}, f32[8,1280]{1,0:T(8,128)S(1)}, u32[]{:S(2)}, u32[]{:S(2)}) collective-permute-start(f32[8,1280]{1,0:T(8,128)S(1)} %shard_map.78.refs_1_.refs_5_), channel_id=1, source_target_pairs={{8,16},{24,32},{40,48},{56,64},{72,80},{88,96},{104,112},{16,8},{3... | collective-permute-start | bytes 122888 | tf_op jit(solution)/shard_map/ppermute | solution.py:748
  51.5 4.0 %collective-permute-done.1.refs_3_ = f32[8,1280]{1,0:T(8,128)S(1)} collective-permute-done((f32[8,1280]{1,0:T(8,128)S(1)}, f32[8,1280]{1,0:T(8,128)S(1)}, u32[]{:S(2)}, u32[]{:S(2)}) %collective-permute-start.1) | collective-permute-done | bytes 40992 | tf_op jit(solution)/shard_map/ppermute | solution.py:748
  55.4 0.0 collective-permute-start
  55.4 1.2 %collective-permute-done.refs_2_ = f32[8,1280]{1,0:T(8,128)S(1)} collective-permute-done((f32[8,1280]{1,0:T(8,128)S(1)}, f32[8,1280]{1,0:T(8,128)S(1)}, u32[]{:S(2)}, u32[]{:S(2)}) %collective-permute-start) | collective-permute-done | bytes 40992 | tf_op jit(solution)/shard_map/ppermute | solution.py:747
  56.7 0.0 collective-permute-done.2.refs_4_.refs_0_.refs_2_
  56.7 0.0 copy-start.2
  56.7 0.0 collective-permute-done.3.refs_5_.refs_1_.refs_3_
  56.7 0.0 copy-start.3
  56.7 0.0 collective-permute-done.4.refs_2_
  56.7 0.0 copy-start.6
  56.7 0.0 collective-permute-done.5.refs_3_
  56.7 0.0 all-to-all-done.1.refs_0_
  56.7 0.4 shard_map.84
  57.1 0.0 copy-start.4
  57.1 1.1 %copy-done.4 = f32[8,32,1408]{2,1,0:T(8,128)} copy-done((f32[8,32,1408]{2,1,0:T(8,128)}, f32[8,32,1408]{2,1,0:T(8,128)S(1)}, u32[]{:S(2)}) %copy-start.4) | copy-done | bytes 1441816
  58.3 6.4 %all-to-all-start.2 = ((f32[8,32,1408]{2,1,0:T(8,128)}), f32[8,32,1408]{2,1,0:T(8,128)S(1)}, u32[]{:S(2)}, u32[]{:S(2)}) async-start(f32[8,32,1408]{2,1,0:T(8,128)} %copy-done.4), calls=%async_computation.2 | async-start | bytes 2883584 | tf_op jit(solution)/shard_map/all_to_all | solution.py:764
  64.6 0.1 collective-permute-start.6
  64.7 3.0 %collective-permute-start.7 = (f32[8,1024]{1,0:T(8,128)S(1)}, f32[8,1024]{1,0:T(8,128)S(1)}, u32[]{:S(2)}, u32[]{:S(2)}) collective-permute-start(f32[8,1024]{1,0:T(8,128)S(1)} %get-tuple-element.39), channel_id=1, source_target_pairs={{8,16},{24,32},{40,48},{56,64},{72,80},{88,96},{104,112},{16,8},{3... | collective-permute-start | bytes 98312 | tf_op jit(solution)/shard_map/ppermute | solution.py:759
  67.7 2.8 %shard_map.86 = f32[16,4096]{1,0:T(8,128)} custom-call(s32[1]{0:T(128)S(6)} %copy.12.level, s32[1]{0:T(128)S(6)} %copy.13.shift, f32[16,4096]{1,0:T(8,128)S(1)} %copy-done, f32[16,4096]{1,0:T(8,128)S(1)} %copy-done.1, f32[8,6144]{1,0:T(8,128)S(1)} %collective-permute-done.2.refs_4_.refs_0_.refs_2_, ...), custom_call_target="tpu_custom_call" | custom-call | flops 4194304 | bytes 4194304 | tf_op jit(solution)/shard_map/pallas_call | solution.py:715
  70.5 0.0 copy-done.2
  70.5 0.0 copy-done.3
  70.5 0.0 copy-done.6
  70.5 10.6 %shard_map.81 = (f32[8,128,1024]{2,1,0:T(8,128)}, f32[128,1024]{1,0:T(8,128)}) custom-call(s32[1]{0:T(128)S(6)} %copy.12.level, s32[1]{0:T(128)S(6)} %copy.13.shift, f32[8,128,1024]{2,1,0:T(8,128)} %refs_0_.8, f32[8,128,1024]{2,1,0:T(8,128)} %refs_1_.8, f32[256,1024]{1,0:T(8,128)} %copy-done.6, f32[256,1024]{1,0:T(8,128)} %collective-permute-done.5.refs_3_, ...), custom_call_target="tpu_custom_call" | custom-call | flops 25165824 | bytes 25165824 | tf_op jit(solution)/shard_map/pallas_call | solution.py:302
  81.1 0.0 collective-permute-done.6.refs_1_
  81.1 0.0 copy-start.7
  81.1 1.2 %collective-permute-done.7.refs_2_ = f32[8,1024]{1,0:T(8,128)S(1)} collective-permute-done((f32[8,1024]{1,0:T(8,128)S(1)}, f32[8,1024]{1,0:T(8,128)S(1)}, u32[]{:S(2)}, u32[]{:S(2)}) %collective-permute-start.7) | collective-permute-done | bytes 32800 | tf_op jit(solution)/shard_map/ppermute | solution.py:759
  82.3 0.0 copy-start.8
  82.3 0.0 copy-done.7
  82.3 0.6 copy-done.8
  82.9 0.0 copy-start.5
  82.9 2.9 %shard_map.83.refs_0_ = f32[8,128,1024]{2,1,0:T(8,128)} custom-call(s32[1]{0:T(128)S(6)} %copy.12.level, s32[1]{0:T(128)S(6)} %copy.13.shift, f32[8,128,1024]{2,1,0:T(8,128)} %get-tuple-element.37.refs_0_, f32[8,1024]{1,0:T(8,128)} %copy-done.7, f32[8,1024]{1,0:T(8,128)} %copy-done.8), custom_call_target="tpu_custom_call", output_to_operand_aliasing={{}: (2, {})} | custom-call | flops 1048576 | bytes 1048576 | tf_op jit(solution)/shard_map/pallas_call | solution.py:599
  85.8 0.0 all-to-all-done.2.refs_1_
  85.8 0.0 copy-done.5
  85.8 3.3 %shard_map.85 = f32[8,128,1024]{2,1,0:T(8,128)} custom-call(s32[1]{0:T(128)S(6)} %copy.12.level, s32[1]{0:T(128)S(6)} %copy.13.shift, f32[8,128,1024]{2,1,0:T(8,128)} %shard_map.83.refs_0_, f32[8,32,1408]{2,1,0:T(8,128)S(1)} %all-to-all-done.2.refs_1_, f32[128,1024]{1,0:T(8,128)S(1)} %copy-done.5), custom_call_target="tpu_custom_call", output_to_operand_aliasing={{}: (2, {})} | custom-call | flops 4194304 | bytes 4194304 | tf_op jit(solution)/shard_map/pallas_call | solution.py:660
  (1 shorter events, 0.0 us)
Async XLA Ops:
  1.9 12.3 %copy-start = (f32[16,4096]{1,0:T(8,128)S(1)}, f32[16,4096]{1,0:T(8,128)}, u32[]{:S(2)}) copy-start(f32[16,4096]{1,0:T(8,128)} %refs_0_.9) | copy-start | bytes 786436
  1.9 12.2 %copy-start.1 = (f32[16,4096]{1,0:T(8,128)S(1)}, f32[16,4096]{1,0:T(8,128)}, u32[]{:S(2)}) copy-start(f32[16,4096]{1,0:T(8,128)} %refs_1_.9) | copy-start | bytes 786436
  5.9 25.3 %all-to-all-start = ((f32[8,32,1280]{2,1,0:T(8,128)}), f32[8,32,1280]{2,1,0:T(8,128)S(1)}, u32[]{:S(2)}, u32[]{:S(2)}) async-start(f32[8,32,1280]{2,1,0:T(8,128)} %get-tuple-element.24), calls=%async_computation | async-start | bytes 2621440 | tf_op jit(solution)/shard_map/all_to_all | solution.py:739
  16.1 22.1 %copy-start.10 = (f32[8,6144]{1,0:T(8,128)S(1)}, f32[8,6144]{1,0:T(8,128)}, u32[]{:S(2)}) copy-start(f32[8,6144]{1,0:T(8,128)} %get-tuple-element.29) | copy-start | bytes 589828
  16.1 24.9 %copy-start.9 = (f32[8,6144]{1,0:T(8,128)S(1)}, f32[8,6144]{1,0:T(8,128)}, u32[]{:S(2)}) copy-start(f32[8,6144]{1,0:T(8,128)} %get-tuple-element.30) | copy-start | bytes 589828
  19.7 37.0 %collective-permute-start.4 = (f32[256,1024]{1,0:T(8,128)}, f32[256,1024]{1,0:T(8,128)S(1)}, u32[]{:S(2)}, u32[]{:S(2)}) collective-permute-start(f32[256,1024]{1,0:T(8,128)} %get-tuple-element.31), channel_id=1, source_target_pairs={{0,8},{8,0},{16,24},{24,16},{32,40},{40,32},{48,56},{56,48},{64,72... | collective-permute-start | bytes 3145736 | tf_op jit(solution)/shard_map/ppermute | solution.py:752
  19.7 37.0 %collective-permute-start.5 = (f32[256,1024]{1,0:T(8,128)}, f32[256,1024]{1,0:T(8,128)}, u32[]{:S(2)}, u32[]{:S(2)}) collective-permute-start(f32[256,1024]{1,0:T(8,128)} %get-tuple-element.32), channel_id=1, source_target_pairs={{8,16},{24,32},{40,48},{56,64},{72,80},{88,96},{104,112},{16,8},{3... | collective-permute-start | bytes 3145736 | tf_op jit(solution)/shard_map/ppermute | solution.py:753
  32.3 24.4 %all-to-all-start.1 = ((f32[16,8,1280]{2,1,0:T(8,128)}), f32[16,8,1280]{2,1,0:T(8,128)S(1)}, u32[]{:S(2)}, u32[]{:S(2)}) async-start(f32[16,8,1280]{2,1,0:T(8,128)} %shard_map.80), calls=%async_computation.1 | async-start | bytes 1310720 | tf_op jit(solution)/shard_map/all_to_all | solution.py:755
  38.2 18.4 %collective-permute-start.2 = (f32[8,6144]{1,0:T(8,128)S(1)}, f32[8,6144]{1,0:T(8,128)S(1)}, u32[]{:S(2)}, u32[]{:S(2)}) collective-permute-start(f32[8,6144]{1,0:T(8,128)S(1)} %copy-done.10), channel_id=1, source_target_pairs={{0,1},{1,2},{2,3},{3,4},{4,5},{5,6},{6,7},{7,8},{8,9},{9,10},{10,1... | collective-permute-start | bytes 589832 | tf_op jit(solution)/shard_map/ppermute | solution.py:740
  41.0 15.7 %collective-permute-start.3 = (f32[8,6144]{1,0:T(8,128)S(1)}, f32[8,6144]{1,0:T(8,128)S(1)}, u32[]{:S(2)}, u32[]{:S(2)}) collective-permute-start(f32[8,6144]{1,0:T(8,128)S(1)} %copy-done.9), channel_id=1, source_target_pairs={{1,0},{2,1},{3,2},{4,3},{5,4},{6,5},{7,6},{8,7},{9,8},{10,9},{11,1... | collective-permute-start | bytes 589832 | tf_op jit(solution)/shard_map/ppermute | solution.py:741
  47.7 7.7 %collective-permute-start.1 = (f32[8,1280]{1,0:T(8,128)S(1)}, f32[8,1280]{1,0:T(8,128)S(1)}, u32[]{:S(2)}, u32[]{:S(2)}) collective-permute-start(f32[8,1280]{1,0:T(8,128)S(1)} %shard_map.78.refs_1_.refs_5_), channel_id=1, source_target_pairs={{8,16},{24,32},{40,48},{56,64},{72,80},{88,96},{104,112},{16,8},{3... | collective-permute-start | bytes 122888 | tf_op jit(solution)/shard_map/ppermute | solution.py:748
  55.4 1.2 %collective-permute-start = (f32[8,1280]{1,0:T(8,128)S(1)}, f32[8,1280]{1,0:T(8,128)S(1)}, u32[]{:S(2)}, u32[]{:S(2)}) collective-permute-start(f32[8,1280]{1,0:T(8,128)S(1)} %shard_map.78.refs_1_.refs_5_), channel_id=1, source_target_pairs={{0,8},{8,0},{16,24},{24,16},{32,40},{40,32},{48,56},{56,48},{64,72... | collective-permute-start | bytes 122888 | tf_op jit(solution)/shard_map/ppermute | solution.py:747
  56.7 13.8 %copy-start.2 = (f32[8,6144]{1,0:T(8,128)}, f32[8,6144]{1,0:T(8,128)S(1)}, u32[]{:S(2)}) copy-start(f32[8,6144]{1,0:T(8,128)S(1)} %collective-permute-done.2.refs_4_.refs_0_.refs_2_) | copy-start | bytes 589828
  56.7 13.8 %copy-start.3 = (f32[8,6144]{1,0:T(8,128)}, f32[8,6144]{1,0:T(8,128)S(1)}, u32[]{:S(2)}) copy-start(f32[8,6144]{1,0:T(8,128)S(1)} %collective-permute-done.3.refs_5_.refs_1_.refs_3_) | copy-start | bytes 589828
  56.7 13.8 %copy-start.6 = (f32[256,1024]{1,0:T(8,128)}, f32[256,1024]{1,0:T(8,128)S(1)}, u32[]{:S(2)}) copy-start(f32[256,1024]{1,0:T(8,128)S(1)} %collective-permute-done.4.refs_2_) | copy-start | bytes 3145732
  57.1 1.1 %copy-start.4 = (f32[8,32,1408]{2,1,0:T(8,128)}, f32[8,32,1408]{2,1,0:T(8,128)S(1)}, u32[]{:S(2)}) copy-start(f32[8,32,1408]{2,1,0:T(8,128)S(1)} %get-tuple-element.43) | copy-start | bytes 4325380
  58.3 27.6 %all-to-all-start.2 = ((f32[8,32,1408]{2,1,0:T(8,128)}), f32[8,32,1408]{2,1,0:T(8,128)S(1)}, u32[]{:S(2)}, u32[]{:S(2)}) async-start(f32[8,32,1408]{2,1,0:T(8,128)} %copy-done.4), calls=%async_computation.2 | async-start | bytes 2883584 | tf_op jit(solution)/shard_map/all_to_all | solution.py:764
  64.6 16.4 %collective-permute-start.6 = (f32[8,1024]{1,0:T(8,128)S(1)}, f32[8,1024]{1,0:T(8,128)S(1)}, u32[]{:S(2)}, u32[]{:S(2)}) collective-permute-start(f32[8,1024]{1,0:T(8,128)S(1)} %get-tuple-element.38), channel_id=1, source_target_pairs={{0,8},{8,0},{16,24},{24,16},{32,40},{40,32},{48,56},{56,48},{64,72... | collective-permute-start | bytes 98312 | tf_op jit(solution)/shard_map/ppermute | solution.py:758
  64.7 17.6 %collective-permute-start.7 = (f32[8,1024]{1,0:T(8,128)S(1)}, f32[8,1024]{1,0:T(8,128)S(1)}, u32[]{:S(2)}, u32[]{:S(2)}) collective-permute-start(f32[8,1024]{1,0:T(8,128)S(1)} %get-tuple-element.39), channel_id=1, source_target_pairs={{8,16},{24,32},{40,48},{56,64},{72,80},{88,96},{104,112},{16,8},{3... | collective-permute-start | bytes 98312 | tf_op jit(solution)/shard_map/ppermute | solution.py:759
  81.1 1.3 %copy-start.7 = (f32[8,1024]{1,0:T(8,128)}, f32[8,1024]{1,0:T(8,128)S(1)}, u32[]{:S(2)}) copy-start(f32[8,1024]{1,0:T(8,128)S(1)} %collective-permute-done.6.refs_1_) | copy-start | bytes 98308
  82.3 0.6 copy-start.8
  82.9 2.9 %copy-start.5 = (f32[128,1024]{1,0:T(8,128)S(1)}, f32[128,1024]{1,0:T(8,128)}, u32[]{:S(2)}) copy-start(f32[128,1024]{1,0:T(8,128)} %get-tuple-element.44.refs_2_) | copy-start | bytes 1572868

commit v6 on v5

--- a/solution.py
+++ b/solution.py
@@ -577,33 +577,36 @@
 
 
 def add_corner_kernel(scal, field, on_chip, off_chip, out):
-    t = pl.program_id(0)
     lower_core = (scal[5] & 1) == 0
-    low = t < 2
-    first_end = (t & 1) == 0
-    near = jnp.where(jnp.logical_not(jnp.logical_xor(low, lower_core)), off_chip[...], on_chip[...])
-    line = jnp.where(first_end, near[0:1], near[1:2])
-    row = iota(out.shape[1:], 0)
+    first_end = pl.program_id(0) == 0
+    depth = field.shape[0]
+    row = iota(field.shape[1:], 0)
     spot = jnp.where(first_end, 0, 7)
-    out[0] = field[0] + jnp.where(row == spot, 0.18 * line, 0.0)
+
+    def line(near):
+        return jnp.where(row == spot, 0.18 * jnp.where(first_end, near[0:1], near[1:2]), 0.0)
+
+    below = line(jnp.where(lower_core, off_chip[...], on_chip[...]))
+    above = line(jnp.where(lower_core, on_chip[...], off_chip[...]))
+    out[0] = field[0] + below
+    for z in range(1, depth - 1):
+        out[z] = field[z]
+    out[depth - 1] = field[depth - 1] + above
 
 
 def add_corners(scal, field, on_chip, off_chip):
     depth, height, width = field.shape
 
-    def where(t, *scal):
-        return ((t >> 1) * (depth - 1), (t & 1) * (height // 8 - 1), 0)
-
-    tile = pl.BlockSpec((1, 8, width), where)
+    tile = pl.BlockSpec((depth, 8, width), lambda t, *scal: (0, t * (height // 8 - 1), 0))
     pack = pl.BlockSpec((8, width), lambda t, *scal: (0, 0))
     return pl.pallas_call(
         placed(add_corner_kernel),
         grid_spec=pltpu.PrefetchScalarGridSpec(
-            num_scalar_prefetch=2, grid=(4,), in_specs=[tile, pack, pack], out_specs=tile
+            num_scalar_prefetch=2, grid=(2,), in_specs=[tile, pack, pack], out_specs=tile
         ),
         out_shape=jax.ShapeDtypeStruct(field.shape, F32),
         input_output_aliases={2: 0},
-        compiler_params=params(59),
+        compiler_params=params(8),
         cost_estimate=cost(1 << 20),
     )(*scal, field, on_chip, off_chip)
 

time: 89.5 us -> 88.1 us (0.984)
  Pallas kernels: 30.4 us -> 29.4 us
  starting transfers between devices: 42.6 us -> 41.7 us
    pallas_call x1, Pallas kernels: 2.87 us -> 1.83 us  [add_corners(): pl.pallas_call(placed(add_corner_kernel), grid_spec=pltpu.PrefetchScalarG...]
  transfers between devices with their start and end apart: 11 -> 11, of which waited for: 4 -> 4; matrix products, arithmetic and copies ran while one was open for 0% -> 0% of each run, Pallas kernels for 26% -> 25%
where the time goes in v6:
time: 88.1 us; the launch traced here: 87 us
  starting transfers between devices  41.7 us (47%)
  Pallas kernels  29.4 us (33%)
  waiting for transfers between devices  12.6 us (14%)
  between operations  2.09 us (2%)
  local copies, waits for them, and re-layouts  1.17 us (1%)
    pallas_call x1, Pallas kernels, air_steps(): pl.pallas_call(placed(air_kernel), grid_spec=pltpu.PrefetchScalarGridSpec...  10.6 us
    all_to_all x1, starting transfers between devices, shards(): came = lax.all_to_all(sent, 'gy', 0, 0).reshape(256, width + 256)  8.28 us
    ppermute x1, starting transfers between devices, shards(): hi = lax.ppermute(first, ('gz', 'gy'), down_d)  6.69 us
    all_to_all x1, waiting for transfers between devices, shards(): came = lax.all_to_all(sent, 'gy', 0, 0).reshape(256, width + 256)  6.19 us
    all_to_all x1, starting transfers between devices, shards(): came = lax.all_to_all(to_plate(scal, came, motion), 'gz', 0, 0)  5.95 us
    all_to_all x1, starting transfers between devices, shards(): came = lax.all_to_all(sent, 'gy', 0, 0)  5.89 us
    ppermute x1, starting transfers between devices, shards(): off_chip = lax.ppermute(off_chip, 'gz', pairs_off)  5.29 us
    pallas_call x1, Pallas kernels, front(): pl.pallas_call(placed(front_kernel), grid_spec=pltpu.PrefetchScalarGridSp...  3.96 us
  transfers between devices with their start and end apart: 11, of which 4 were waited for; matrix products, arithmetic and copies ran while one was open for 0% of the time, Pallas kernels for 25%

profile of v6, /device:TPU:6, one launch (start us, length us, event | category | flops | bytes accessed | tf_op | source)
XLA Modules:
  0.0 87.0 jit_solution(10597585121945067644)
XLA Ops:
  1.9 0.0 copy-start
  1.9 0.0 copy-start.1
  1.9 4.0 %shard_map.77 = (f32[8,6144]{1,0:T(8,128)}, f32[8,6144]{1,0:T(8,128)}, f32[8,32,1280]{2,1,0:T(8,128)}) custom-call(s32[1]{0:T(128)S(6)} %copy.12.level, s32[1]{0:T(128)S(6)} %copy.13.shift, f32[8,128,1024]{2,1,0:T(8,128)} %refs_0_.8, f32[8,128,1024]{2,1,0:T(8,128)} %refs_0_.8, f32[8,128,1024]{2,1,0:T(8,128)} %refs_1_.8, f32[8,128,1024]{2,1,0:T(8,128)} %refs_1_.8, ...), custom_call_target="tpu_custom_call" | custom-call | flops 6291456 | bytes 6291456 | tf_op jit(solution)/shard_map/pallas_call | solution.py:388
  5.9 8.3 %all-to-all-start = ((f32[8,32,1280]{2,1,0:T(8,128)}), f32[8,32,1280]{2,1,0:T(8,128)S(1)}, u32[]{:S(2)}, u32[]{:S(2)}) async-start(f32[8,32,1280]{2,1,0:T(8,128)} %get-tuple-element.24), calls=%async_computation | async-start | bytes 2621440 | tf_op jit(solution)/shard_map/all_to_all | solution.py:742
  14.2 0.0 copy-done
  14.2 0.0 copy-done.1
  14.2 1.9 %shard_map.78.refs_1_.refs_5_ = f32[8,1280]{1,0:T(8,128)S(1)} custom-call(s32[1]{0:T(128)S(6)} %copy.12.level, s32[1]{0:T(128)S(6)} %copy.13.shift, f32[16,4096]{1,0:T(8,128)S(1)} %copy-done, f32[16,4096]{1,0:T(8,128)S(1)} %copy-done.1), custom_call_target="tpu_custom_call" | custom-call | flops 4194304 | bytes 4194304 | tf_op jit(solution)/shard_map/pallas_call | solution.py:453
  16.1 0.0 copy-start.8
  16.1 0.0 copy-start.7
  16.1 3.6 %shard_map.79 = (f32[256,1024]{1,0:T(8,128)}, f32[256,1024]{1,0:T(8,128)}) custom-call(s32[1]{0:T(128)S(6)} %copy.12.level, s32[1]{0:T(128)S(6)} %copy.13.shift, f32[8,128,1024]{2,1,0:T(8,128)} %refs_0_.8, f32[8,128,1024]{2,1,0:T(8,128)} %refs_0_.8, f32[8,128,1024]{2,1,0:T(8,128)} %refs_1_.8), custom_call_target="tpu_custom_call" | custom-call | flops 5242880 | bytes 5242880 | tf_op jit(solution)/shard_map/pallas_call | solution.py:136
  19.7 0.0 collective-permute-start.4
  19.7 5.3 %collective-permute-start.5 = (f32[256,1024]{1,0:T(8,128)}, f32[256,1024]{1,0:T(8,128)}, u32[]{:S(2)}, u32[]{:S(2)}) collective-permute-start(f32[256,1024]{1,0:T(8,128)} %get-tuple-element.32), channel_id=1, source_target_pairs={{8,16},{24,32},{40,48},{56,64},{72,80},{88,96},{104,112},{16,8},{3... | collective-permute-start | bytes 3145736 | tf_op jit(solution)/shard_map/ppermute | solution.py:756
  25.0 6.2 %all-to-all-done = f32[8,32,1280]{2,1,0:T(8,128)S(1)} async-done(((f32[8,32,1280]{2,1,0:T(8,128)}), f32[8,32,1280]{2,1,0:T(8,128)S(1)}, u32[]{:S(2)}, u32[]{:S(2)}) %all-to-all-start) | async-done | bytes 1310752 | tf_op jit(solution)/shard_map/all_to_all | solution.py:742
  31.2 1.0 %shard_map.80 = f32[16,8,1280]{2,1,0:T(8,128)} custom-call(s32[1]{0:T(128)S(6)} %copy.12.level, s32[1]{0:T(128)S(6)} %copy.13.shift, f32[256,1280]{1,0:T(8,128)S(1)} %bitcast.1, f32[8,1280]{1,0:T(8,128)S(1)} %shard_map.78.refs_1_.refs_5_), custom_call_target="tpu_custom_call" | custom-call | flops 2097152 | bytes 2097152 | tf_op jit(solution)/shard_map/pallas_call | solution.py:499
  32.3 5.9 %all-to-all-start.1 = ((f32[16,8,1280]{2,1,0:T(8,128)}), f32[16,8,1280]{2,1,0:T(8,128)S(1)}, u32[]{:S(2)}, u32[]{:S(2)}) async-start(f32[16,8,1280]{2,1,0:T(8,128)} %shard_map.80), calls=%async_computation.1 | async-start | bytes 1310720 | tf_op jit(solution)/shard_map/all_to_all | solution.py:758
  38.2 0.0 copy-done.8
  38.2 2.8 %collective-permute-start.2 = (f32[8,6144]{1,0:T(8,128)S(1)}, f32[8,6144]{1,0:T(8,128)S(1)}, u32[]{:S(2)}, u32[]{:S(2)}) collective-permute-start(f32[8,6144]{1,0:T(8,128)S(1)} %copy-done.8), channel_id=1, source_target_pairs={{0,1},{1,2},{2,3},{3,4},{4,5},{5,6},{6,7},{7,8},{8,9},{9,10},{10,1... | collective-permute-start | bytes 589832 | tf_op jit(solution)/shard_map/ppermute | solution.py:743
  41.0 0.0 copy-done.7
  41.0 6.7 %collective-permute-start.3 = (f32[8,6144]{1,0:T(8,128)S(1)}, f32[8,6144]{1,0:T(8,128)S(1)}, u32[]{:S(2)}, u32[]{:S(2)}) collective-permute-start(f32[8,6144]{1,0:T(8,128)S(1)} %copy-done.7), channel_id=1, source_target_pairs={{1,0},{2,1},{3,2},{4,3},{5,4},{6,5},{7,6},{8,7},{9,8},{10,9},{11,1... | collective-permute-start | bytes 589832 | tf_op jit(solution)/shard_map/ppermute | solution.py:744
  47.7 3.8 %collective-permute-start.1 = (f32[8,1280]{1,0:T(8,128)S(1)}, f32[8,1280]{1,0:T(8,128)S(1)}, u32[]{:S(2)}, u32[]{:S(2)}) collective-permute-start(f32[8,1280]{1,0:T(8,128)S(1)} %shard_map.78.refs_1_.refs_5_), channel_id=1, source_target_pairs={{8,16},{24,32},{40,48},{56,64},{72,80},{88,96},{104,112},{16,8},{3... | collective-permute-start | bytes 122888 | tf_op jit(solution)/shard_map/ppermute | solution.py:751
  51.5 4.0 %collective-permute-done.1.refs_3_ = f32[8,1280]{1,0:T(8,128)S(1)} collective-permute-done((f32[8,1280]{1,0:T(8,128)S(1)}, f32[8,1280]{1,0:T(8,128)S(1)}, u32[]{:S(2)}, u32[]{:S(2)}) %collective-permute-start.1) | collective-permute-done | bytes 40992 | tf_op jit(solution)/shard_map/ppermute | solution.py:751
  55.4 0.0 collective-permute-start
  55.4 1.2 %collective-permute-done.refs_2_ = f32[8,1280]{1,0:T(8,128)S(1)} collective-permute-done((f32[8,1280]{1,0:T(8,128)S(1)}, f32[8,1280]{1,0:T(8,128)S(1)}, u32[]{:S(2)}, u32[]{:S(2)}) %collective-permute-start) | collective-permute-done | bytes 40992 | tf_op jit(solution)/shard_map/ppermute | solution.py:750
  56.7 0.0 collective-permute-done.2.refs_4_.refs_0_.refs_2_
  56.7 0.0 copy-start.2
  56.7 0.0 collective-permute-done.3.refs_5_.refs_1_.refs_3_
  56.7 0.0 copy-start.3
  56.7 0.0 collective-permute-done.4.refs_2_
  56.7 0.0 copy-start.6
  56.7 0.0 collective-permute-done.5.refs_3_
  56.7 0.0 all-to-all-done.1.refs_0_
  56.7 0.4 shard_map.84
  57.1 0.0 copy-start.4
  57.1 1.1 %copy-done.4 = f32[8,32,1408]{2,1,0:T(8,128)} copy-done((f32[8,32,1408]{2,1,0:T(8,128)}, f32[8,32,1408]{2,1,0:T(8,128)S(1)}, u32[]{:S(2)}) %copy-start.4) | copy-done | bytes 1441816
  58.3 5.9 %all-to-all-start.2 = ((f32[8,32,1408]{2,1,0:T(8,128)}), f32[8,32,1408]{2,1,0:T(8,128)S(1)}, u32[]{:S(2)}, u32[]{:S(2)}) async-start(f32[8,32,1408]{2,1,0:T(8,128)} %copy-done.4), calls=%async_computation.2 | async-start | bytes 2883584 | tf_op jit(solution)/shard_map/all_to_all | solution.py:767
  64.2 0.1 collective-permute-start.6
  64.3 3.0 %collective-permute-start.7 = (f32[8,1024]{1,0:T(8,128)S(1)}, f32[8,1024]{1,0:T(8,128)S(1)}, u32[]{:S(2)}, u32[]{:S(2)}) collective-permute-start(f32[8,1024]{1,0:T(8,128)S(1)} %get-tuple-element.39), channel_id=1, source_target_pairs={{8,16},{24,32},{40,48},{56,64},{72,80},{88,96},{104,112},{16,8},{3... | collective-permute-start | bytes 98312 | tf_op jit(solution)/shard_map/ppermute | solution.py:762
  67.3 2.8 %shard_map.86 = f32[16,4096]{1,0:T(8,128)} custom-call(s32[1]{0:T(128)S(6)} %copy.12.level, s32[1]{0:T(128)S(6)} %copy.13.shift, f32[16,4096]{1,0:T(8,128)S(1)} %copy-done, f32[16,4096]{1,0:T(8,128)S(1)} %copy-done.1, f32[8,6144]{1,0:T(8,128)S(1)} %collective-permute-done.2.refs_4_.refs_0_.refs_2_, ...), custom_call_target="tpu_custom_call" | custom-call | flops 4194304 | bytes 4194304 | tf_op jit(solution)/shard_map/pallas_call | solution.py:718
  70.1 0.0 copy-done.2
  70.1 0.0 copy-done.3
  70.1 0.0 copy-done.6
  70.1 10.6 %shard_map.81 = (f32[8,128,1024]{2,1,0:T(8,128)}, f32[128,1024]{1,0:T(8,128)}) custom-call(s32[1]{0:T(128)S(6)} %copy.12.level, s32[1]{0:T(128)S(6)} %copy.13.shift, f32[8,128,1024]{2,1,0:T(8,128)} %refs_0_.8, f32[8,128,1024]{2,1,0:T(8,128)} %refs_1_.8, f32[256,1024]{1,0:T(8,128)} %copy-done.6, f32[256,1024]{1,0:T(8,128)} %collective-permute-done.5.refs_3_, ...), custom_call_target="tpu_custom_call" | custom-call | flops 25165824 | bytes 25165824 | tf_op jit(solution)/shard_map/pallas_call | solution.py:302
  80.6 0.0 collective-permute-done.6.refs_1_
  80.7 1.2 %collective-permute-done.7.refs_2_ = f32[8,1024]{1,0:T(8,128)S(1)} collective-permute-done((f32[8,1024]{1,0:T(8,128)S(1)}, f32[8,1024]{1,0:T(8,128)S(1)}, u32[]{:S(2)}, u32[]{:S(2)}) %collective-permute-start.7) | collective-permute-done | bytes 32800 | tf_op jit(solution)/shard_map/ppermute | solution.py:762
  81.9 0.0 copy-start.5
  81.9 1.8 %shard_map.83.refs_0_ = f32[8,128,1024]{2,1,0:T(8,128)} custom-call(s32[1]{0:T(128)S(6)} %copy.12.level, s32[1]{0:T(128)S(6)} %copy.13.shift, f32[8,128,1024]{2,1,0:T(8,128)} %get-tuple-element.37.refs_0_, f32[8,1024]{1,0:T(8,128)S(1)} %collective-permute-done.6.refs_1_, f32[8,1024]{1,0:T(8,128)S(1)} %collective-permute-done.7.refs_2_), custom_call_target="tpu_custom_call", output_to_operand_aliasing={{}: (2, {})} | custom-call | flops 1048576 | bytes 1048576 | tf_op jit(solution)/shard_map/pallas_call | solution.py:602
  83.7 0.0 all-to-all-done.2.refs_1_
  83.7 0.0 copy-done.5
  83.7 3.3 %shard_map.85 = f32[8,128,1024]{2,1,0:T(8,128)} custom-call(s32[1]{0:T(128)S(6)} %copy.12.level, s32[1]{0:T(128)S(6)} %copy.13.shift, f32[8,128,1024]{2,1,0:T(8,128)} %shard_map.83.refs_0_, f32[8,32,1408]{2,1,0:T(8,128)S(1)} %all-to-all-done.2.refs_1_, f32[128,1024]{1,0:T(8,128)S(1)} %copy-done.5), custom_call_target="tpu_custom_call", output_to_operand_aliasing={{}: (2, {})} | custom-call | flops 4194304 | bytes 4194304 | tf_op jit(solution)/shard_map/pallas_call | solution.py:663
  (1 shorter events, 0.0 us)
Async XLA Ops:
  1.9 12.3 %copy-start = (f32[16,4096]{1,0:T(8,128)S(1)}, f32[16,4096]{1,0:T(8,128)}, u32[]{:S(2)}) copy-start(f32[16,4096]{1,0:T(8,128)} %refs_0_.9) | copy-start | bytes 786436
  1.9 12.2 %copy-start.1 = (f32[16,4096]{1,0:T(8,128)S(1)}, f32[16,4096]{1,0:T(8,128)}, u32[]{:S(2)}) copy-start(f32[16,4096]{1,0:T(8,128)} %refs_1_.9) | copy-start | bytes 786436
  5.9 25.3 %all-to-all-start = ((f32[8,32,1280]{2,1,0:T(8,128)}), f32[8,32,1280]{2,1,0:T(8,128)S(1)}, u32[]{:S(2)}, u32[]{:S(2)}) async-start(f32[8,32,1280]{2,1,0:T(8,128)} %get-tuple-element.24), calls=%async_computation | async-start | bytes 2621440 | tf_op jit(solution)/shard_map/all_to_all | solution.py:742
  16.1 22.1 %copy-start.8 = (f32[8,6144]{1,0:T(8,128)S(1)}, f32[8,6144]{1,0:T(8,128)}, u32[]{:S(2)}) copy-start(f32[8,6144]{1,0:T(8,128)} %get-tuple-element.29) | copy-start | bytes 589828
  16.1 24.9 %copy-start.7 = (f32[8,6144]{1,0:T(8,128)S(1)}, f32[8,6144]{1,0:T(8,128)}, u32[]{:S(2)}) copy-start(f32[8,6144]{1,0:T(8,128)} %get-tuple-element.30) | copy-start | bytes 589828
  19.7 37.0 %collective-permute-start.4 = (f32[256,1024]{1,0:T(8,128)}, f32[256,1024]{1,0:T(8,128)S(1)}, u32[]{:S(2)}, u32[]{:S(2)}) collective-permute-start(f32[256,1024]{1,0:T(8,128)} %get-tuple-element.31), channel_id=1, source_target_pairs={{0,8},{8,0},{16,24},{24,16},{32,40},{40,32},{48,56},{56,48},{64,72... | collective-permute-start | bytes 3145736 | tf_op jit(solution)/shard_map/ppermute | solution.py:755
  19.7 37.0 %collective-permute-start.5 = (f32[256,1024]{1,0:T(8,128)}, f32[256,1024]{1,0:T(8,128)}, u32[]{:S(2)}, u32[]{:S(2)}) collective-permute-start(f32[256,1024]{1,0:T(8,128)} %get-tuple-element.32), channel_id=1, source_target_pairs={{8,16},{24,32},{40,48},{56,64},{72,80},{88,96},{104,112},{16,8},{3... | collective-permute-start | bytes 3145736 | tf_op jit(solution)/shard_map/ppermute | solution.py:756
  32.3 24.4 %all-to-all-start.1 = ((f32[16,8,1280]{2,1,0:T(8,128)}), f32[16,8,1280]{2,1,0:T(8,128)S(1)}, u32[]{:S(2)}, u32[]{:S(2)}) async-start(f32[16,8,1280]{2,1,0:T(8,128)} %shard_map.80), calls=%async_computation.1 | async-start | bytes 1310720 | tf_op jit(solution)/shard_map/all_to_all | solution.py:758
  38.2 18.4 %collective-permute-start.2 = (f32[8,6144]{1,0:T(8,128)S(1)}, f32[8,6144]{1,0:T(8,128)S(1)}, u32[]{:S(2)}, u32[]{:S(2)}) collective-permute-start(f32[8,6144]{1,0:T(8,128)S(1)} %copy-done.8), channel_id=1, source_target_pairs={{0,1},{1,2},{2,3},{3,4},{4,5},{5,6},{6,7},{7,8},{8,9},{9,10},{10,1... | collective-permute-start | bytes 589832 | tf_op jit(solution)/shard_map/ppermute | solution.py:743
  41.0 15.7 %collective-permute-start.3 = (f32[8,6144]{1,0:T(8,128)S(1)}, f32[8,6144]{1,0:T(8,128)S(1)}, u32[]{:S(2)}, u32[]{:S(2)}) collective-permute-start(f32[8,6144]{1,0:T(8,128)S(1)} %copy-done.7), channel_id=1, source_target_pairs={{1,0},{2,1},{3,2},{4,3},{5,4},{6,5},{7,6},{8,7},{9,8},{10,9},{11,1... | collective-permute-start | bytes 589832 | tf_op jit(solution)/shard_map/ppermute | solution.py:744
  47.7 7.7 %collective-permute-start.1 = (f32[8,1280]{1,0:T(8,128)S(1)}, f32[8,1280]{1,0:T(8,128)S(1)}, u32[]{:S(2)}, u32[]{:S(2)}) collective-permute-start(f32[8,1280]{1,0:T(8,128)S(1)} %shard_map.78.refs_1_.refs_5_), channel_id=1, source_target_pairs={{8,16},{24,32},{40,48},{56,64},{72,80},{88,96},{104,112},{16,8},{3... | collective-permute-start | bytes 122888 | tf_op jit(solution)/shard_map/ppermute | solution.py:751
  55.4 1.2 %collective-permute-start = (f32[8,1280]{1,0:T(8,128)S(1)}, f32[8,1280]{1,0:T(8,128)S(1)}, u32[]{:S(2)}, u32[]{:S(2)}) collective-permute-start(f32[8,1280]{1,0:T(8,128)S(1)} %shard_map.78.refs_1_.refs_5_), channel_id=1, source_target_pairs={{0,8},{8,0},{16,24},{24,16},{32,40},{40,32},{48,56},{56,48},{64,72... | collective-permute-start | bytes 122888 | tf_op jit(solution)/shard_map/ppermute | solution.py:750
  56.7 13.4 %copy-start.2 = (f32[8,6144]{1,0:T(8,128)}, f32[8,6144]{1,0:T(8,128)S(1)}, u32[]{:S(2)}) copy-start(f32[8,6144]{1,0:T(8,128)S(1)} %collective-permute-done.2.refs_4_.refs_0_.refs_2_) | copy-start | bytes 589828
  56.7 13.4 %copy-start.3 = (f32[8,6144]{1,0:T(8,128)}, f32[8,6144]{1,0:T(8,128)S(1)}, u32[]{:S(2)}) copy-start(f32[8,6144]{1,0:T(8,128)S(1)} %collective-permute-done.3.refs_5_.refs_1_.refs_3_) | copy-start | bytes 589828
  56.7 13.4 %copy-start.6 = (f32[256,1024]{1,0:T(8,128)}, f32[256,1024]{1,0:T(8,128)S(1)}, u32[]{:S(2)}) copy-start(f32[256,1024]{1,0:T(8,128)S(1)} %collective-permute-done.4.refs_2_) | copy-start | bytes 3145732
  57.1 1.1 %copy-start.4 = (f32[8,32,1408]{2,1,0:T(8,128)}, f32[8,32,1408]{2,1,0:T(8,128)S(1)}, u32[]{:S(2)}) copy-start(f32[8,32,1408]{2,1,0:T(8,128)S(1)} %get-tuple-element.43) | copy-start | bytes 4325380
  58.3 25.5 %all-to-all-start.2 = ((f32[8,32,1408]{2,1,0:T(8,128)}), f32[8,32,1408]{2,1,0:T(8,128)S(1)}, u32[]{:S(2)}, u32[]{:S(2)}) async-start(f32[8,32,1408]{2,1,0:T(8,128)} %copy-done.4), calls=%async_computation.2 | async-start | bytes 2883584 | tf_op jit(solution)/shard_map/all_to_all | solution.py:767
  64.2 16.5 %collective-permute-start.6 = (f32[8,1024]{1,0:T(8,128)S(1)}, f32[8,1024]{1,0:T(8,128)S(1)}, u32[]{:S(2)}, u32[]{:S(2)}) collective-permute-start(f32[8,1024]{1,0:T(8,128)S(1)} %get-tuple-element.38), channel_id=1, source_target_pairs={{0,8},{8,0},{16,24},{24,16},{32,40},{40,32},{48,56},{56,48},{64,72... | collective-permute-start | bytes 98312 | tf_op jit(solution)/shard_map/ppermute | solution.py:761
  64.3 17.6 %collective-permute-start.7 = (f32[8,1024]{1,0:T(8,128)S(1)}, f32[8,1024]{1,0:T(8,128)S(1)}, u32[]{:S(2)}, u32[]{:S(2)}) collective-permute-start(f32[8,1024]{1,0:T(8,128)S(1)} %get-tuple-element.39), channel_id=1, source_target_pairs={{8,16},{24,32},{40,48},{56,64},{72,80},{88,96},{104,112},{16,8},{3... | collective-permute-start | bytes 98312 | tf_op jit(solution)/shard_map/ppermute | solution.py:762
  81.9 1.8 %copy-start.5 = (f32[128,1024]{1,0:T(8,128)S(1)}, f32[128,1024]{1,0:T(8,128)}, u32[]{:S(2)}) copy-start(f32[128,1024]{1,0:T(8,128)} %get-tuple-element.44.refs_2_) | copy-start | bytes 1572868
